TPU v7x, 32 devices: a whole 2x2x4 slice. The times are simulated.
32 devices in a mesh: tower: 4 (over y, x), shard: 8 (over z, core).
Axes of the slice: x: 2, y: 2, z: 4, core: 2. Of those that a mesh axis runs over, the one named last changes fastest.
Arguments:
- out_grad: bfloat16 [1024, 1024], P(('tower', 'shard')), may hold values from -6 to 6
- pooled: bfloat16 [4, 1024, 2048], P('tower', 'shard'), may hold values from -6 to 6
- down_proj: bfloat16 [4, 2048, 256], P('tower'), may hold values from -0.125 to 0.125
- up_proj: bfloat16 [4, 256, 2048], P('tower'), may hold values from -0.375 to 0.375
- cross_bias: float32 [4, 2048], P('tower'), may hold values from -3 to 3
- out_proj: bfloat16 [4, 2048, 256], P('tower'), may hold values from -0.125 to 0.125
- assign: int32 [64], replicated, may hold values from 0 to 63, each once
Outputs:
- feature_grad: bfloat16 [1024, 8192], P(('tower', 'shard'))
- weight_grad: float32 [4, 768, 2048], P('tower', 'shard')
- bias_grad: float32 [4, 2048], P('tower')
Inputs may be any that keep to these rules, and one draw needn't show every extreme that they name: `assign`: slot k of the 64 slots belongs to tower k // 16; every feature sits in exactly one slot.
All inputs are finite; a program needn't handle non-finite values.
Results may differ from a plain program's by a relative error of at most 0.01.
Values may be sent and summed in bfloat16 or wider, within the bound.
No kernel may reach another device: no remote copies, remote signals or barrier semaphores. Data moves between devices by JAX's collectives and lax.ppermute only.
A program may use at most 64 MiB of HBM per device.

v0:
```python
import math

import jax
import jax.numpy as jnp
from jax import lax
from jax.sharding import PartitionSpec as P

EMB = 128


def body(out_grad, pooled, down_proj, up_proj, cross_bias, out_proj, assign):
    grad_out = lax.all_to_all(out_grad, "tower", split_axis=1, concat_axis=0, tiled=True)
    feature_in = pooled[0]
    w_down = down_proj[0]
    w_up = up_proj[0]
    w_out = out_proj[0]
    bias_row = cross_bias[0]
    hidden_low = jnp.dot(feature_in, w_down, preferred_element_type=jnp.float32).astype(
        jnp.bfloat16
    )
    gate_full = jnp.dot(hidden_low, w_up, preferred_element_type=jnp.float32) + bias_row[None, :]
    factor = gate_full + 1.0
    crossed = (feature_in * factor).astype(jnp.bfloat16)
    grad_crossed = jnp.einsum(
        "no,wo->nw", grad_out, w_out, preferred_element_type=jnp.float32
    ).astype(jnp.bfloat16)
    grad_gate = grad_crossed.astype(jnp.float32) * feature_in
    grad_gate_low = grad_gate.astype(jnp.bfloat16)
    grad_hidden = jnp.einsum(
        "nw,rw->nr", grad_gate_low, w_up, preferred_element_type=jnp.float32
    ).astype(jnp.bfloat16)
    grad_inputs = (
        grad_crossed.astype(jnp.float32) * factor
        + jnp.einsum("nr,wr->nw", grad_hidden, w_down, preferred_element_type=jnp.float32)
    ).astype(jnp.bfloat16)
    returned = lax.all_to_all(grad_inputs, "tower", split_axis=0, concat_axis=1, tiled=True)
    local_rows = returned.shape[0]
    blocks = returned.reshape(local_rows, -1, EMB)
    inverse = jnp.argsort(assign)
    feature_grad = jnp.take(blocks, inverse, axis=1).reshape(local_rows, -1)
    shards = lax.axis_size("shard")
    weight_scale = 1.0 / math.sqrt(grad_out.shape[0] * shards)
    stacked = jnp.concatenate(
        [
            jnp.einsum("nr,nw->rw", grad_hidden, feature_in, preferred_element_type=jnp.float32),
            jnp.einsum("nr,nw->rw", hidden_low, grad_gate_low, preferred_element_type=jnp.float32),
            jnp.einsum("nr,nw->rw", grad_out, crossed, preferred_element_type=jnp.float32),
        ],
        axis=0,
    )
    summed = lax.psum_scatter(stacked, "shard", scatter_dimension=0, tiled=True)
    weight_grad = (summed * weight_scale)[None]
    bias_grad = lax.psum(jnp.sum(grad_gate, axis=0), "shard")[None]
    return (feature_grad, weight_grad, bias_grad)


def solution(mesh):
    placed = (
        P(("tower", "shard"), None),
        P("tower", "shard", None),
        P("tower", None, None),
        P("tower", None, None),
        P("tower", None),
        P("tower", None, None),
        P(),
    )
    return jax.shard_map(
        body,
        mesh=mesh,
        in_specs=placed,
        out_specs=(P(("tower", "shard"), None), P("tower", "shard", None), P("tower", None)),
        check_vma=False,
    )
```

profile of v0, /device:TPU:0, one launch (start us, length us, event | category | flops | bytes accessed | tf_op | source)
XLA Modules:
  0.0 106.4 jit_solution(7354557486619503054)
XLA Ops:
  7.2 0.0 copy-start
  7.2 0.0 copy-start.1
  7.2 1.6 %copy.24 = bf16[4,4,8,256]{3,2,0,1:T(8,128)(2,1)} copy(bf16[4,4,8,256]{3,2,1,0:T(8,128)(2,1)} %bitcast.60) | data formatting | bytes 131072 | tf_op jit(solution)/shard_map/all_to_all | solution.py:12
  8.8 5.2 %all-to-all-start = ((bf16[32,4,256]{2,0,1:T(8,128)(2,1)}), bf16[32,4,256]{2,0,1:T(8,128)(2,1)S(1)}, u32[]{:S(2)}, u32[]{:S(2)}) async-start(bf16[32,4,256]{2,0,1:T(8,128)(2,1)} %bitcast.56), calls=%async_computation | async-start | bytes 131072 | tf_op jit(solution)/shard_map/all_to_all | solution.py:12
  13.9 0.0 reduce-scatter.2.cloned.1.call-start
  13.9 1.7 %convolution_convert_fusion.2 = bf16[128,256]{1,0:T(8,128)(2,1)S(1)} fusion(bf16[1,2048,256]{2,1,0:T(8,128)(2,1)} %param.9, bf16[1,128,2048]{2,1,0:T(8,128)(2,1)} %param.8), kind=kOutput, calls=%fused_computation.12 | convolution fusion | flops 134250496 | bytes 1638400 | tf_op jit(solution)/shard_map/dot_general | solution.py:18
  15.7 2.0 %fusion = f32[128,2048]{1,0:T(8,128)} fusion(bf16[128,256]{1,0:T(8,128)(2,1)S(1)} %convolution_convert_fusion.2, bf16[1,256,2048]{2,1,0:T(8,128)(2,1)S(1)} %copy-done, f32[2048]{0:T(1024)} %bitcast.62), kind=kOutput, calls=%fused_computation.5 | convolution fusion | flops 134742016 | bytes 2170880 | tf_op jit(solution)/shard_map/dot_general | solution.py:21
  17.7 1.1 %all-to-all-done = bf16[32,4,256]{2,0,1:T(8,128)(2,1)S(1)} async-done(((bf16[32,4,256]{2,0,1:T(8,128)(2,1)}), bf16[32,4,256]{2,0,1:T(8,128)(2,1)S(1)}, u32[]{:S(2)}, u32[]{:S(2)}) %all-to-all-start) | async-done | bytes 65568 | tf_op jit(solution)/shard_map/all_to_all | solution.py:12
  18.8 0.0 copy-done.1
  18.8 1.7 %fusion.9 = (f32[2048]{0:T(1024)S(1)}, f32[128,2048]{1,0:T(8,128)S(1)}) fusion(bf16[1,128,2048]{2,1,0:T(8,128)(2,1)S(1)} %copy-done.1, bf16[128,256]{1,0:T(8,128)(2,1)S(1)} %bitcast.58, bf16[1,2048,256]{2,1,0:T(8,128)(2,1)} %param.12), kind=kOutput, calls=%fused_computation.20 | convolution fusion | flops 135526400 | bytes 2695168 | tf_op jit(solution)/shard_map/no,wo->nw/dot_general | solution.py:24
  20.5 0.5 convolution_convert_fusion.1
  21.0 0.0 copy-start.2
  21.0 0.5 fusion.16
  21.5 0.8 copy-done.2
  22.2 0.5 convolution_bitcast_fusion
  22.7 0.5 fusion.13
  23.2 3.1 %pad_maximum_fusion = f32[768,2048]{1,0:T(8,128)} fusion(f32[256,2048]{1,0:T(8,128)S(1)} %convolution_bitcast_fusion, f32[256,2048]{1,0:T(8,128)S(1)} %fusion.16, f32[256,2048]{1,0:T(8,128)S(1)} %fusion.13), kind=kLoop, calls=%fused_computation.1 | loop fusion | flops 3145728 | bytes 12582912 | tf_op jit(solution)/shard_map/concatenate | solution.py:43
  26.3 0.0 reduce-scatter.2.cloned.1.call-update
  26.3 0.6 copy-done.3
  26.9 2.0 %sort.17 = (s32[64]{0:T(128)}, s32[64]{0:T(128)S(1)}) sort(s32[64]{0:T(128)S(1)} %copy-done.3, s32[64]{0:T(128)S(1)} %iota.4), dimensions={0}, to_apply=%region_0.0 | sort | flops 384 | bytes 1024 | tf_op jit(solution)/shard_map/jit(argsort)/sort | solution.py:39
  29.0 2.8 %fusion.1 = bf16[128,2048]{1,0:T(8,128)(2,1)} fusion(bf16[128,256]{1,0:T(8,128)(2,1)S(1)} %convolution_convert_fusion.1, bf16[1,2048,256]{2,1,0:T(8,128)(2,1)} %param.9, f32[128,2048]{1,0:T(8,128)S(1)} %get-tuple-element.6, f32[128,2048]{1,0:T(8,128)} %fusion), kind=kOutput, calls=%fused_computation.6 | convolution fusion | flops 135004160 | bytes 3735552 | tf_op jit(solution)/shard_map/nr,wr->nw/dot_general | solution.py:34
  31.8 3.5 %all-to-all-start.1 = ((bf16[4,32,2048]{2,1,0:T(8,128)(2,1)}), bf16[4,32,2048]{2,1,0:T(8,128)(2,1)S(1)}, u32[]{:S(2)}, u32[]{:S(2)}) async-start(bf16[4,32,2048]{2,1,0:T(8,128)(2,1)} %bitcast.8), calls=%async_computation.1 | async-start | bytes 1048576 | tf_op jit(solution)/shard_map/all_to_all | solution.py:36
  35.3 0.1 broadcast_bitcast_fusion
  35.4 17.2 %psum.7 = f32[1,2048]{1,0:T(1,128)} all-reduce(f32[1,2048]{1,0:T(1,128)S(1)} %bitcast.61), channel_id=1, replica_groups=mesh['tower'=4,'shard'=8] {'shard'}, use_global_device_ids=true, to_apply=%region_3.4 | all-reduce | flops 2048 | bytes 16384 | tf_op jit(solution)/shard_map/psum | solution.py:53
  52.6 0.0 all-to-all-done.1
  52.6 0.4 copy.17
  53.0 0.3 reshape.24
  53.3 0.3 copy.18
  53.7 0.7 gather_fusion
  54.3 0.9 bitcast_select_fusion
  55.2 42.3 %reduce-scatter.2.cloned.1.call-done = f32[96,2048]{1,0:T(8,128)} async-done(((f32[768,2048]{1,0:T(8,128)}), f32[96,2048]{1,0:T(8,128)}) %reduce-scatter.2.cloned.1.call-update) | async-done | bytes 786448 | tf_op jit(solution)/shard_map/reduce_scatter | solution.py:51
  97.5 2.1 %multiply_bitcast_fusion = f32[1,96,2048]{2,1,0:T(8,128)} fusion(f32[96,2048]{1,0:T(8,128)} %reduce-scatter.2.cloned.1.call-done), kind=kLoop, calls=%fused_computation.19 | loop fusion | flops 196608 | bytes 1572864 | tf_op jit(solution)/shard_map/broadcast_in_dim | solution.py:52
  (6 shorter events, 0.0 us)
Async XLA Ops:
  7.2 8.5 %copy-start = (bf16[1,256,2048]{2,1,0:T(8,128)(2,1)S(1)}, bf16[1,256,2048]{2,1,0:T(8,128)(2,1)}, u32[]{:S(2)}) copy-start(bf16[1,256,2048]{2,1,0:T(8,128)(2,1)} %param.10) | copy-start | bytes 3145732
  7.2 11.6 %copy-start.1 = (bf16[1,128,2048]{2,1,0:T(8,128)(2,1)S(1)}, bf16[1,128,2048]{2,1,0:T(8,128)(2,1)}, u32[]{:S(2)}) copy-start(bf16[1,128,2048]{2,1,0:T(8,128)(2,1)} %param.8) | copy-start | bytes 1572868
  8.8 10.0 %all-to-all-start = ((bf16[32,4,256]{2,0,1:T(8,128)(2,1)}), bf16[32,4,256]{2,0,1:T(8,128)(2,1)S(1)}, u32[]{:S(2)}, u32[]{:S(2)}) async-start(bf16[32,4,256]{2,0,1:T(8,128)(2,1)} %bitcast.56), calls=%async_computation | async-start | bytes 131072 | tf_op jit(solution)/shard_map/all_to_all | solution.py:12
  13.9 83.5 %reduce-scatter.2.cloned.1.call-start = ((), (), s32[]{:S(2)}) async-start(), calls=%async_computation.3 | async-start | bytes 7077888 | tf_op jit(solution)/shard_map/reduce_scatter | solution.py:51
  21.0 1.2 %copy-start.2 = (f32[128,2048]{1,0:T(8,128)S(1)}, f32[128,2048]{1,0:T(8,128)}, u32[]{:S(2)}) copy-start(f32[128,2048]{1,0:T(8,128)} %fusion) | copy-start | bytes 3145732
  26.3 0.7 copy-start.3
  31.8 20.8 %all-to-all-start.1 = ((bf16[4,32,2048]{2,1,0:T(8,128)(2,1)}), bf16[4,32,2048]{2,1,0:T(8,128)(2,1)S(1)}, u32[]{:S(2)}, u32[]{:S(2)}) async-start(bf16[4,32,2048]{2,1,0:T(8,128)(2,1)} %bitcast.8), calls=%async_computation.1 | async-start | bytes 1048576 | tf_op jit(solution)/shard_map/all_to_all | solution.py:36
Sparse Core Ops, SparseCore 0:
  26.4 71.0 reduce-scatter.1
where the time goes:
time: 107 us; the launch traced here: 106 us
  waiting for transfers between devices  43.4 us (41%)
  blocking collectives  17.2 us (16%)
  between operations  14.1 us (13%)
  matrix products  10.1 us (9%)
  starting transfers between devices  8.64 us (8%)
  other arithmetic  8.11 us (8%)
  local copies, waits for them, and re-layouts  4.8 us (4%)
    reduce_scatter x1, waiting for transfers between devices, body(): summed = lax.psum_scatter(stacked, 'shard', scatter_dimension=0, tiled=True)  42.3 us
    psum x1, blocking collectives, body(): bias_grad = lax.psum(jnp.sum(grad_gate, axis=0), 'shard')[None]  17.2 us
    all_to_all x1, starting transfers between devices, body(): lax.all_to_all(out_grad, 'tower', split_axis=1, concat_axis=0, tiled=True)  5.16 us
    all_to_all x1, starting transfers between devices, body(): lax.all_to_all(grad_inputs, 'tower', split_axis=0, concat_axis=1, tiled=T...  3.48 us
    concatenate x1, other arithmetic, body(): jnp.concatenate([jnp.einsum('nr,nw->rw', grad_hidden, feature_in, preferr...  3.09 us
    dot_general x1, matrix products, body(): jnp.einsum('nr,wr->nw', grad_hidden, w_down, preferred_element_type=jnp.f...  2.81 us
  transfers between devices with their start and end apart: 3, of which 2 were waited for; matrix products, arithmetic and copies ran while one was open for 11% of the time, Pallas kernels for 0%

commit v1 on v0

v1 whole, which is shorter than its diff:
```python
import functools
import math

import jax
import jax.numpy as jnp
from jax import lax
from jax.experimental import pallas as pl
from jax.experimental.pallas import tpu as pltpu
from jax.sharding import PartitionSpec as P

EMB = 128
VMEM_LIMIT = 48 * 1024 * 1024
BF16 = jnp.bfloat16
F32 = jnp.float32


def mm(a, b):
    return jnp.dot(a, b, preferred_element_type=F32)


def mm_nt(a, b):
    return lax.dot_general(a, b, (((1,), (1,)), ((), ())), preferred_element_type=F32)


def call(kernel, outs, scratch, n_smem, args, flops, name):
    smem = [pl.BlockSpec(memory_space=pltpu.SMEM)] * n_smem
    vmem = [pl.BlockSpec(memory_space=pltpu.VMEM)] * (len(args) - n_smem)
    moved = sum(a.size * a.dtype.itemsize for a in args) + sum(
        o.size * o.dtype.itemsize for o in outs
    )
    return pl.pallas_call(
        kernel,
        out_shape=outs,
        in_specs=smem + vmem,
        out_specs=[pl.BlockSpec(memory_space=pltpu.VMEM)] * len(outs),
        scratch_shapes=scratch,
        compiler_params=pltpu.CompilerParams(vmem_limit_bytes=VMEM_LIMIT),
        cost_estimate=pl.CostEstimate(flops=flops, bytes_accessed=moved, transcendentals=0),
        name=name,
    )(*args)


def column_chunks(width):
    step = 512 if width % 512 == 0 else width
    return [slice(c, c + step) for c in range(0, width, step)]


def split_kernel(n_tower, own_ref, other_ref, *out_refs):
    me = lax.axis_index("tower")
    rows = own_ref.shape[0]
    out = out_refs[0].shape[1]
    for k in range(n_tower):
        columns = pl.ds(pl.multiple_of((me ^ k) * out, out), out)
        out_refs[k][:rows] = own_ref[:, columns]
        out_refs[k][rows:] = other_ref[:, columns]


def gather_rows(piece_refs, half, g_ref):
    me = lax.axis_index("tower")
    rows = piece_refs[0].shape[0] // 2
    for k, piece in enumerate(piece_refs):
        g_ref[pl.ds(pl.multiple_of((me ^ k) * rows, rows), rows), :] = piece[
            half * rows : (half + 1) * rows, :
        ]


def tower_rows(x_ref, g_ref, wd_ref, wu_ref, wo_ref, bias_ref, ht_ref, gg_ref, cr_ref, bg_ref, direct_ref):
    rank = wu_ref.shape[0]
    g = g_ref[...]
    hidden_low = mm(x_ref[...], wd_ref[...]).astype(BF16)
    grad_hidden = jnp.zeros((x_ref.shape[0], rank), F32)
    for c in column_chunks(x_ref.shape[1]):
        x = x_ref[:, c].astype(F32)
        factor = (mm(hidden_low, wu_ref[:, c]) + bias_ref[:, c]) + 1.0
        cr_ref[:, c] = (x * factor).astype(BF16)
        grad_crossed = mm_nt(g, wo_ref[c, :]).astype(BF16).astype(F32)
        grad_gate = grad_crossed * x
        bg_ref[:, c] = jnp.sum(grad_gate, axis=0, keepdims=True)
        low = grad_gate.astype(BF16)
        gg_ref[:, c] = low
        grad_hidden += mm_nt(low, wu_ref[:, c])
        if direct_ref is not None:
            direct_ref[:, c] = grad_crossed * factor
    grad_hidden = grad_hidden.astype(BF16)
    ht_ref[0:rank, :] = grad_hidden.T
    ht_ref[rank : 2 * rank, :] = hidden_low.T
    ht_ref[2 * rank :, :] = g.T
    return grad_hidden


def own_kernel(n_tower, *refs):
    wd_ref, wu_ref, wo_ref, bias_ref, x_ref = refs[:5]
    pieces = refs[5 : 5 + n_tower]
    ht_ref, gg_ref, cr_ref, bg_ref, gi_ref, g_ref, direct_ref = refs[5 + n_tower :]
    gather_rows(pieces, 0, g_ref)
    grad_hidden = tower_rows(
        x_ref, g_ref, wd_ref, wu_ref, wo_ref, bias_ref, ht_ref, gg_ref, cr_ref, bg_ref, direct_ref
    )
    for c in column_chunks(x_ref.shape[1]):
        gi_ref[:, c] = (direct_ref[:, c] + mm_nt(grad_hidden, wd_ref[c, :])).astype(BF16)


def products(group, ht_a, ht_b, x_a, x_b, gg_a, gg_b, cr_a, cr_b, lhs_ref, acc_ref, send_ref, keep_ref):
    shard = lax.axis_index("shard")
    block = send_ref.shape[0]
    rank = ht_a.shape[0] // 3
    rows_a = ht_a.shape[1]
    core = lax.rem(shard, 2)
    first = (group * 4 + (lax.rem(shard, 4) - core)) * block
    picked = pl.ds(pl.multiple_of(first, 2 * block), 2 * block)
    lhs_ref[:, :rows_a] = ht_a[picked, :]
    lhs_ref[:, rows_a:] = ht_b[picked, :]
    acc_ref[...] = jnp.zeros_like(acc_ref)
    for part, (a_ref, b_ref) in enumerate(((x_a, x_b), (gg_a, gg_b), (cr_a, cr_b))):

        @pl.when((first < (part + 1) * rank) & (first + 2 * block > part * rank))
        def _():
            at = first + lax.broadcasted_iota(jnp.int32, lhs_ref.shape, 0)
            inside = (at >= part * rank) & (at < (part + 1) * rank)
            lhs = jnp.where(inside, lhs_ref[...].astype(F32), 0.0).astype(BF16)
            for c in column_chunks(acc_ref.shape[1]):
                rhs = jnp.concatenate([a_ref[:, c], b_ref[:, c]], axis=0)
                acc_ref[:, c] += mm(lhs, rhs)

    send_ref[...] = acc_ref[pl.ds(pl.multiple_of((1 - core) * block, block), block), :].astype(BF16)
    keep_ref[...] = acc_ref[pl.ds(pl.multiple_of(core * block, block), block), :]


def far_kernel(n_tower, *refs):
    wd_ref, wu_ref, wo_ref, bias_ref, x_own, ht_own, gg_own, cr_own, x_ref = refs[:9]
    pieces = refs[9 : 9 + n_tower]
    ht_ref, gg_ref, cr_ref, bg_ref, send_ref, keep_ref, g_ref, lhs_ref, acc_ref = refs[9 + n_tower :]
    gather_rows(pieces, 1, g_ref)
    tower_rows(x_ref, g_ref, wd_ref, wu_ref, wo_ref, bias_ref, ht_ref, gg_ref, cr_ref, bg_ref, None)
    group = 1 - lax.div(lax.axis_index("shard"), 4)
    products(
        group, ht_own, ht_ref, x_own, x_ref, gg_own, gg_ref, cr_own, cr_ref, lhs_ref, acc_ref, send_ref, keep_ref
    )


def near_kernel(ht_own, ht_ref, x_own, x_ref, gg_own, gg_ref, cr_own, cr_ref, send_ref, keep_ref, lhs_ref, acc_ref):
    group = lax.div(lax.axis_index("shard"), 4)
    products(
        group, ht_own, ht_ref, x_own, x_ref, gg_own, gg_ref, cr_own, cr_ref, lhs_ref, acc_ref, send_ref, keep_ref
    )


def place_kernel(n_tower, assign_ref, *refs):
    pieces, out_ref = refs[:n_tower], refs[n_tower]
    me = lax.axis_index("tower")
    slots = pieces[0].shape[1] // EMB
    for k in range(n_tower):
        for j in range(slots):
            at = assign_ref[(me ^ k) * slots + j] * EMB
            out_ref[:, pl.ds(pl.multiple_of(at, EMB), EMB)] = pieces[k][:, j * EMB : (j + 1) * EMB]


def xor_pairs(n, k):
    return [(i, i ^ k) for i in range(n)]


def paired_body(out_grad, pooled, down_proj, up_proj, cross_bias, out_proj, assign):
    n_tower, n_shard = lax.axis_size("tower"), lax.axis_size("shard")
    sds = jax.ShapeDtypeStruct
    w_down, w_up, w_out, x = down_proj[0], up_proj[0], out_proj[0], pooled[0]
    n, width = x.shape
    rank, out = w_up.shape[0], w_out.shape[1]
    stack = 2 * rank + out
    block = stack // n_shard
    top_rows = out_grad.shape[0]

    grad_other = lax.ppermute(out_grad, "shard", xor_pairs(n_shard, 2))
    x_other = lax.ppermute(x, "shard", xor_pairs(n_shard, 2))
    pieces = call(
        functools.partial(split_kernel, n_tower),
        [sds((2 * top_rows, out), BF16)] * n_tower,
        [],
        0,
        [out_grad, grad_other],
        0,
        "split_columns",
    )
    pieces = [pieces[0]] + [
        lax.ppermute(pieces[k], "tower", xor_pairs(n_tower, k)) for k in range(1, n_tower)
    ]
    per_matmul = 2 * n * width * rank
    weights = [w_down, w_up, w_out, cross_bias]
    wide = sds((n, width), BF16)
    row = sds((1, width), F32)
    ht_own, gg_own, cr_own, bg_own, grad_inputs = call(
        functools.partial(own_kernel, n_tower),
        [sds((stack, n), BF16), wide, wide, row, wide],
        [pltpu.VMEM((n, out), BF16), pltpu.VMEM((n, width), F32)],
        0,
        [*weights, x, *pieces],
        5 * per_matmul,
        "own_rows",
    )
    returned = []
    me = lax.axis_index("tower")
    for k in range(n_tower):
        piece = lax.dynamic_slice_in_dim(grad_inputs, (me ^ k) * top_rows, top_rows, 0)
        returned.append(piece if k == 0 else lax.ppermute(piece, "tower", xor_pairs(n_tower, k)))
    (feature_grad,) = call(
        functools.partial(place_kernel, n_tower),
        [sds((top_rows, n_tower * width), BF16)],
        [],
        1,
        [assign, *returned],
        0,
        "place_features",
    )

    sums = [sds((block, width), BF16), sds((block, width), F32)]
    sum_scratch = [pltpu.VMEM((2 * block, 2 * n), BF16), pltpu.VMEM((2 * block, width), F32)]
    ht_other, gg_other, cr_other, bg_other, far_send, far_keep = call(
        functools.partial(far_kernel, n_tower),
        [sds((stack, n), BF16), wide, wide, row, *sums],
        [pltpu.VMEM((n, out), BF16), *sum_scratch],
        0,
        [*weights, x, ht_own, gg_own, cr_own, x_other, *pieces],
        6 * per_matmul,
        "far_sums",
    )
    far = far_keep + lax.ppermute(far_send, "shard", xor_pairs(n_shard, 1)).astype(F32)
    far = lax.ppermute(far.astype(BF16), "shard", xor_pairs(n_shard, 4))
    near_send, near_keep = call(
        near_kernel,
        sums,
        sum_scratch,
        0,
        [ht_own, ht_other, x, x_other, gg_own, gg_other, cr_own, cr_other],
        3 * per_matmul,
        "near_sums",
    )
    near = near_keep + lax.ppermute(near_send, "shard", xor_pairs(n_shard, 1)).astype(F32)
    scale = 1.0 / math.sqrt(n * n_shard)
    weight_grad = ((near + far.astype(F32)) * scale)[None]
    bias_grad = bg_own + bg_other
    bias_grad = bias_grad + lax.ppermute(bias_grad, "shard", xor_pairs(n_shard, 1))
    bias_grad = bias_grad + lax.ppermute(bias_grad, "shard", xor_pairs(n_shard, 4))
    return feature_grad, weight_grad, bias_grad


def general_body(out_grad, pooled, down_proj, up_proj, cross_bias, out_proj, assign):
    grad_out = lax.all_to_all(out_grad, "tower", split_axis=1, concat_axis=0, tiled=True)
    feature_in = pooled[0]
    w_down, w_up, w_out = down_proj[0], up_proj[0], out_proj[0]
    hidden_low = mm(feature_in, w_down).astype(BF16)
    factor = mm(hidden_low, w_up) + cross_bias + 1.0
    crossed = (feature_in * factor).astype(BF16)
    grad_crossed = mm_nt(grad_out, w_out).astype(BF16)
    grad_gate = grad_crossed.astype(F32) * feature_in
    grad_gate_low = grad_gate.astype(BF16)
    grad_hidden = mm_nt(grad_gate_low, w_up).astype(BF16)
    grad_inputs = (grad_crossed.astype(F32) * factor + mm_nt(grad_hidden, w_down)).astype(BF16)
    returned = lax.all_to_all(grad_inputs, "tower", split_axis=0, concat_axis=1, tiled=True)
    local_rows = returned.shape[0]
    blocks = returned.reshape(local_rows, -1, EMB)
    feature_grad = jnp.take(blocks, jnp.argsort(assign), axis=1).reshape(local_rows, -1)
    stacked = jnp.concatenate(
        [
            mm(grad_hidden.T, feature_in),
            mm(hidden_low.T, grad_gate_low),
            mm(grad_out.T, crossed),
        ],
        axis=0,
    )
    scale = 1.0 / math.sqrt(grad_out.shape[0] * lax.axis_size("shard"))
    summed = lax.psum_scatter(stacked, "shard", scatter_dimension=0, tiled=True)
    bias_grad = lax.psum(jnp.sum(grad_gate, axis=0), "shard")[None]
    return feature_grad, (summed * scale)[None], bias_grad


def solution(mesh):
    n_tower, n_shard = mesh.shape["tower"], mesh.shape["shard"]
    placed = (
        P(("tower", "shard"), None),
        P("tower", "shard", None),
        P("tower", None, None),
        P("tower", None, None),
        P("tower", None),
        P("tower", None, None),
        P(),
    )

    paired = n_shard == 2 * 4 and n_tower & (n_tower - 1) == 0
    return jax.shard_map(
        paired_body if paired else general_body,
        mesh=mesh,
        in_specs=placed,
        out_specs=(P(("tower", "shard"), None), P("tower", "shard", None), P("tower", None)),
        check_vma=False,
    )
```

time: 107 us -> 61.6 us (0.58)
  blocking collectives: 17.2 us -> 0 us
  between operations: 14.1 us -> 0.74 us
  waiting for transfers between devices: 43.4 us -> 31.2 us
  matrix products: 10.1 us -> 0 us
  Pallas kernels: 0 us -> 8.05 us
  other arithmetic: 8.11 us -> 1.72 us
  starting transfers between devices: 8.64 us -> 14 us
    reduce_scatter x1 -> x0, waiting for transfers between devices: 42.3 us -> none  [body(): summed = lax.psum_scatter(stacked, 'shard', scatter_dimension=0, tiled=True)]
    ppermute x0 -> x13, waiting for transfers between devices: none -> 31.2 us  [the longest x1 13.5 us: paired_body(): grad_other = lax.ppermute(out_grad, 'shard', xor_pairs(n_shard, 2))]
    psum x1 -> x0, blocking collectives: 17.2 us -> none  [body(): bias_grad = lax.psum(jnp.sum(grad_gate, axis=0), 'shard')[None]]
    ppermute x0 -> x13, starting transfers between devices: none -> 14 us  [the longest x3 3.55 us: paired_body(): lax.ppermute(piece, 'tower', xor_pairs(n_tower, k))]
    dot_general x8 -> x0, matrix products: 10.1 us -> none  [the longest x1 2.81 us: body(): jnp.einsum('nr,wr->nw', grad_hidden, w_down, preferred_element_type=jnp.f...]
    all_to_all x2 -> x0, starting transfers between devices: 8.64 us -> none  [the longest x1 5.16 us: body(): lax.all_to_all(out_grad, 'tower', split_axis=1, concat_axis=0, tiled=True)]
    pallas_call x0 -> x5, Pallas kernels: none -> 8.05 us  [call(): pl.pallas_call(kernel, out_shape=outs, in_specs=smem + vmem, out_specs=[p...]
    unnamed x8 -> x16, local copies, waits for them, and re-layouts: 1.4 us -> 5.57 us
  transfers between devices with their start and end apart: 3 -> 13, of which waited for: 2 -> 8; matrix products, arithmetic and copies ran while one was open for 11% -> 1% of each run, Pallas kernels for 0% -> 7%
where the time goes in v1:
time: 61.6 us; the launch traced here: 61.3 us
  waiting for transfers between devices  31.2 us (51%)
  starting transfers between devices  14 us (23%)
  Pallas kernels  8.05 us (13%)
  local copies, waits for them, and re-layouts  5.62 us (9%)
  other arithmetic  1.72 us (3%)
  between operations  0.74 us (1%)
    ppermute x1, waiting for transfers between devices, paired_body(): grad_other = lax.ppermute(out_grad, 'shard', xor_pairs(n_shard, 2))  13.5 us
    pallas_call x5, Pallas kernels, call(): pl.pallas_call(kernel, out_shape=outs, in_specs=smem + vmem, out_specs=[p...  8.05 us
    ppermute x1, waiting for transfers between devices, paired_body(): lax.ppermute(bias_grad, 'shard', xor_pairs(n_shard, 4))  7.98 us
    unnamed x16, local copies, waits for them, and re-layouts  5.57 us
    ppermute x3, waiting for transfers between devices, paired_body(): lax.ppermute(piece, 'tower', xor_pairs(n_tower, k))  4.69 us
    ppermute x3, waiting for transfers between devices, paired_body(): lax.ppermute(pieces[k], 'tower', xor_pairs(n_tower, k))  4.5 us
    ppermute x3, starting transfers between devices, paired_body(): lax.ppermute(piece, 'tower', xor_pairs(n_tower, k))  3.55 us
    ppermute x3, starting transfers between devices, paired_body(): lax.ppermute(pieces[k], 'tower', xor_pairs(n_tower, k))  3.55 us
  transfers between devices with their start and end apart: 13, of which 8 were waited for; matrix products, arithmetic and copies ran while one was open for 1% of the time, Pallas kernels for 7%

profile of v1, /device:TPU:0, one launch (start us, length us, event | category | flops | bytes accessed | tf_op | source)
XLA Modules:
  0.0 61.3 jit_solution(3060528339271017240)
XLA Ops:
  0.6 3.1 %collective-permute-start.7 = (bf16[128,2048]{1,0:T(8,128)(2,1)}, bf16[128,2048]{1,0:T(8,128)(2,1)S(1)}, u32[]{:S(2)}, u32[]{:S(2)}) collective-permute-start(bf16[128,2048]{1,0:T(8,128)(2,1)} %bitcast.6), channel_id=1, source_target_pairs={{0,2},{1,3},{2,0},{3,1},{4,6},{5,7},{6,4},{7,5},{8,10},{9,11},{10,... | collective-permute-start | bytes 1572872 | tf_op jit(solution)/shard_map/ppermute | solution.py:173
  3.7 0.1 collective-permute-start
  3.8 13.5 %collective-permute-done.other_ref = bf16[32,1024]{1,0:T(8,128)(2,1)S(1)} collective-permute-done((bf16[32,1024]{1,0:T(8,128)(2,1)}, bf16[32,1024]{1,0:T(8,128)(2,1)S(1)}, u32[]{:S(2)}, u32[]{:S(2)}) %collective-permute-start) | collective-permute-done | bytes 65568 | tf_op jit(solution)/shard_map/ppermute | solution.py:172
  17.3 0.8 %copy-done.5 = bf16[32,1024]{1,0:T(8,128)(2,1)S(1)} copy-done((bf16[32,1024]{1,0:T(8,128)(2,1)S(1)}, bf16[32,1024]{1,0:T(8,128)(2,1)}, u32[]{:S(2)}) %copy-start.5) | copy-done | bytes 65560
  18.1 1.7 %collective-permute-start.1 = (bf16[64,256]{1,0:T(8,128)(2,1)S(1)}, bf16[64,256]{1,0:T(8,128)(2,1)S(1)}, u32[]{:S(2)}, u32[]{:S(2)}) collective-permute-start(bf16[64,256]{1,0:T(8,128)(2,1)S(1)} %get-tuple-element.21), channel_id=1, source_target_pairs={{0,8},{8,0},{16,24},{24,16},{1,9},{9,1},{17,25},{25,17},{2,10},{10... | collective-permute-start | bytes 98312 | tf_op jit(solution)/shard_map/ppermute | solution.py:184
  19.9 1.5 %collective-permute-start.2 = (bf16[64,256]{1,0:T(8,128)(2,1)S(1)}, bf16[64,256]{1,0:T(8,128)(2,1)S(1)}, u32[]{:S(2)}, u32[]{:S(2)}) collective-permute-start(bf16[64,256]{1,0:T(8,128)(2,1)S(1)} %get-tuple-element.22), channel_id=1, source_target_pairs={{0,16},{8,24},{16,0},{24,8},{1,17},{9,25},{17,1},{25,9},{2,18},{10... | collective-permute-start | bytes 98312 | tf_op jit(solution)/shard_map/ppermute | solution.py:184
  21.4 0.3 collective-permute-start.3
  21.7 0.4 collective-permute-done.1.refs_6_.refs_10_
  22.1 1.9 %collective-permute-done.2.refs_7_.refs_11_ = bf16[64,256]{1,0:T(8,128)(2,1)S(1)} collective-permute-done((bf16[64,256]{1,0:T(8,128)(2,1)S(1)}, bf16[64,256]{1,0:T(8,128)(2,1)S(1)}, u32[]{:S(2)}, u32[]{:S(2)}) %collective-permute-start.2) | collective-permute-done | bytes 32800 | tf_op jit(solution)/shard_map/ppermute | solution.py:184
  24.0 2.2 %collective-permute-done.3.refs_8_.refs_12_ = bf16[64,256]{1,0:T(8,128)(2,1)S(1)} collective-permute-done((bf16[64,256]{1,0:T(8,128)(2,1)S(1)}, bf16[64,256]{1,0:T(8,128)(2,1)S(1)}, u32[]{:S(2)}, u32[]{:S(2)}) %collective-permute-start.3) | collective-permute-done | bytes 32800 | tf_op jit(solution)/shard_map/ppermute | solution.py:184
  26.2 1.0 %copy-done = bf16[1,128,2048]{2,1,0:T(8,128)(2,1)S(1)} copy-done((bf16[1,128,2048]{2,1,0:T(8,128)(2,1)S(1)}, bf16[1,128,2048]{2,1,0:T(8,128)(2,1)}, u32[]{:S(2)}) %copy-start) | copy-done | bytes 524312
  27.2 1.2 %copy-done.2 = bf16[1,2048,256]{2,1,0:T(8,128)(2,1)S(1)} copy-done((bf16[1,2048,256]{2,1,0:T(8,128)(2,1)S(1)}, bf16[1,2048,256]{2,1,0:T(8,128)(2,1)}, u32[]{:S(2)}) %copy-start.2) | copy-done | bytes 1048600
  28.5 1.2 %copy-done.3 = bf16[1,256,2048]{2,1,0:T(8,128)(2,1)S(1)} copy-done((bf16[1,256,2048]{2,1,0:T(8,128)(2,1)S(1)}, bf16[1,256,2048]{2,1,0:T(8,128)(2,1)}, u32[]{:S(2)}) %copy-start.3) | copy-done | bytes 1048600
  29.7 1.2 %copy-done.4 = bf16[1,2048,256]{2,1,0:T(8,128)(2,1)S(1)} copy-done((bf16[1,2048,256]{2,1,0:T(8,128)(2,1)S(1)}, bf16[1,2048,256]{2,1,0:T(8,128)(2,1)}, u32[]{:S(2)}) %copy-start.4) | copy-done | bytes 1048600
  30.9 1.9 %own_rows.1 = (bf16[768,128]{1,0:T(8,128)(2,1)S(1)}, bf16[128,2048]{1,0:T(8,128)(2,1)S(1)}, bf16[128,2048]{1,0:T(8,128)(2,1)S(1)}, f32[1,2048]{1,0:T(1,128)S(1)}, bf16[128,2048]{1,0:T(8,128)(2,1)S(1)}) custom-call(bf16[2048,256]{1,0:T(8,128)(2,1)S(1)} %bitcast.10, bf16[256,2048]{1,0:T(8,128)(2,1)S(1)} %bitcast.13, bf16[2048,256]{1,0:T(8,128)(2,1)S(1)} %bitcast.15, ...), custom_call_target="tpu_custom_call" | custom-call | flops 671088640 | bytes 5586944 | tf_op jit(solution)/shard_map/own_rows/pallas_call | solution.py:31
  32.8 4.1 %far_sums.1 = (bf16[768,128]{1,0:T(8,128)(2,1)S(1)}, bf16[128,2048]{1,0:T(8,128)(2,1)S(1)}, bf16[128,2048]{1,0:T(8,128)(2,1)S(1)}, f32[1,2048]{1,0:T(1,128)S(1)}...) custom-call(bf16[2048,256]{1,0:T(8,128)(2,1)S(1)} %bitcast.11, bf16[256,2048]{1,0:T(8,128)(2,1)} %bitcast.12, ...), custom_call_target="tpu_custom_call" | custom-call | flops 805306368 | bytes 8011776 | tf_op jit(solution)/shard_map/far_sums/pallas_call | solution.py:31
  36.9 0.1 collective-permute-start.9
  37.0 0.6 near_sums.1
  37.6 0.6 collective-permute-start.8
  38.1 0.6 collective-permute-done.9
  38.7 0.1 add_convert_fusion
  38.8 2.3 %collective-permute-start.10 = (bf16[96,2048]{1,0:T(8,128)(2,1)S(1)}, bf16[96,2048]{1,0:T(8,128)(2,1)S(1)}, u32[]{:S(2)}, u32[]{:S(2)}) collective-permute-start(bf16[96,2048]{1,0:T(8,128)(2,1)S(1)} %add_convert_fusion), channel_id=1, source_target_pairs={{0,4},{1,5},{2,6},{3,7},{4,0},{5,1},{6,2},{7,3},{8,12},{9,13},{10,... | collective-permute-start | bytes 1179656 | tf_op jit(solution)/shard_map/ppermute | solution.py:226
  41.2 0.6 collective-permute-start.4
  41.8 0.5 collective-permute-start.5
  42.3 2.4 %collective-permute-start.6 = (bf16[32,2048]{1,0:T(8,128)(2,1)S(1)}, bf16[32,2048]{1,0:T(8,128)(2,1)S(1)}, u32[]{:S(2)}, u32[]{:S(2)}) collective-permute-start(bf16[32,2048]{1,0:T(8,128)(2,1)S(1)} %get-tuple-element.37), channel_id=1, source_target_pairs={{0,24},{8,16},{16,8},{24,0},{1,25},{9,17},{17,9},{25,1},{2,26},{10... | collective-permute-start | bytes 393224 | tf_op jit(solution)/shard_map/ppermute | solution.py:203
  44.7 2.8 %collective-permute-done.4.refs_1_ = bf16[32,2048]{1,0:T(8,128)(2,1)S(1)} collective-permute-done((bf16[32,2048]{1,0:T(8,128)(2,1)S(1)}, bf16[32,2048]{1,0:T(8,128)(2,1)S(1)}, u32[]{:S(2)}, u32[]{:S(2)}) %collective-permute-start.4) | collective-permute-done | bytes 131104 | tf_op jit(solution)/shard_map/ppermute | solution.py:203
  47.5 0.7 %collective-permute-start.12 = (f32[1,2048]{1,0:T(1,128)S(1)}, f32[1,2048]{1,0:T(1,128)S(1)}, u32[]{:S(2)}, u32[]{:S(2)}) collective-permute-start(f32[1,2048]{1,0:T(1,128)S(1)} %add.38), channel_id=1, source_target_pairs={{0,4},{1,5},{2,6},{3,7},{4,0},{5,1},{6,2},{7,3},{8,12},{9,13},{10,... | collective-permute-start | bytes 24584 | tf_op jit(solution)/shard_map/ppermute | solution.py:241
  48.3 1.9 %collective-permute-done.5.refs_2_ = bf16[32,2048]{1,0:T(8,128)(2,1)S(1)} collective-permute-done((bf16[32,2048]{1,0:T(8,128)(2,1)S(1)}, bf16[32,2048]{1,0:T(8,128)(2,1)S(1)}, u32[]{:S(2)}, u32[]{:S(2)}) %collective-permute-start.5) | collective-permute-done | bytes 131104 | tf_op jit(solution)/shard_map/ppermute | solution.py:203
  50.2 1.5 %place_features.1 = bf16[32,8192]{1,0:T(8,128)(2,1)} custom-call(s32[64]{0:T(128)S(1)} %copy-done.7, bf16[32,2048]{1,0:T(8,128)(2,1)S(1)} %get-tuple-element.40.refs_0_, bf16[32,2048]{1,0:T(8,128)(2,1)S(1)} %collective-permute-done.4.refs_1_, bf16[32,2048]{1,0:T(8,128)(2,1)S(1)} %collective-permute-done.5.refs_2_, ...), custom_call_target="tpu_custom_call" | custom-call | bytes 1048832 | tf_op jit(solution)/shard_map/place_features/pallas_call | solution.py:31
  51.7 8.0 %collective-permute-done.12 = f32[1,2048]{1,0:T(1,128)S(1)} collective-permute-done((f32[1,2048]{1,0:T(1,128)S(1)}, f32[1,2048]{1,0:T(1,128)S(1)}, u32[]{:S(2)}, u32[]{:S(2)}) %collective-permute-start.12) | collective-permute-done | bytes 8224 | tf_op jit(solution)/shard_map/ppermute | solution.py:241
  59.7 0.6 add.39
  60.3 1.0 %multiply_bitcast_fusion = f32[1,96,2048]{2,1,0:T(8,128)} fusion(bf16[96,2048]{1,0:T(8,128)(2,1)S(1)} %collective-permute-done.10, f32[96,2048]{1,0:T(8,128)S(1)} %get-tuple-element.31, bf16[96,2048]{1,0:T(8,128)(2,1)S(1)} %collective-permute-done.8), kind=kLoop, calls=%fused_computation | loop fusion | flops 983040 | bytes 2359296 | tf_op jit(solution)/shard_map/broadcast_in_dim | solution.py:238
  (21 shorter events, 0.2 us)
Async XLA Ops:
  0.6 32.2 %collective-permute-start.7 = (bf16[128,2048]{1,0:T(8,128)(2,1)}, bf16[128,2048]{1,0:T(8,128)(2,1)S(1)}, u32[]{:S(2)}, u32[]{:S(2)}) collective-permute-start(bf16[128,2048]{1,0:T(8,128)(2,1)} %bitcast.6), channel_id=1, source_target_pairs={{0,2},{1,3},{2,0},{3,1},{4,6},{5,7},{6,4},{7,5},{8,10},{9,11},{10,... | collective-permute-start | bytes 1572872 | tf_op jit(solution)/shard_map/ppermute | solution.py:173
  3.7 13.5 %collective-permute-start = (bf16[32,1024]{1,0:T(8,128)(2,1)}, bf16[32,1024]{1,0:T(8,128)(2,1)S(1)}, u32[]{:S(2)}, u32[]{:S(2)}) collective-permute-start(bf16[32,1024]{1,0:T(8,128)(2,1)} %own_ref.1), channel_id=1, source_target_pairs={{0,2},{1,3},{2,0},{3,1},{4,6},{5,7},{6,4},{7,5},{8,10},{9,11},{10,... | collective-permute-start | bytes 196616 | tf_op jit(solution)/shard_map/ppermute | solution.py:172
  17.3 0.8 %copy-start.5 = (bf16[32,1024]{1,0:T(8,128)(2,1)S(1)}, bf16[32,1024]{1,0:T(8,128)(2,1)}, u32[]{:S(2)}) copy-start(bf16[32,1024]{1,0:T(8,128)(2,1)} %own_ref.1) | copy-start | bytes 196612
  18.1 8.1 %copy-start.6 = (f32[1,2048]{1,0:T(1,128)S(1)}, f32[1,2048]{1,0:T(1,128)}, u32[]{:S(2)}) copy-start(f32[1,2048]{1,0:T(1,128)} %refs_3_.3) | copy-start | bytes 24580
  18.1 4.0 %collective-permute-start.1 = (bf16[64,256]{1,0:T(8,128)(2,1)S(1)}, bf16[64,256]{1,0:T(8,128)(2,1)S(1)}, u32[]{:S(2)}, u32[]{:S(2)}) collective-permute-start(bf16[64,256]{1,0:T(8,128)(2,1)S(1)} %get-tuple-element.21), channel_id=1, source_target_pairs={{0,8},{8,0},{16,24},{24,16},{1,9},{9,1},{17,25},{25,17},{2,10},{10... | collective-permute-start | bytes 98312 | tf_op jit(solution)/shard_map/ppermute | solution.py:184
  19.9 4.1 %collective-permute-start.2 = (bf16[64,256]{1,0:T(8,128)(2,1)S(1)}, bf16[64,256]{1,0:T(8,128)(2,1)S(1)}, u32[]{:S(2)}, u32[]{:S(2)}) collective-permute-start(bf16[64,256]{1,0:T(8,128)(2,1)S(1)} %get-tuple-element.22), channel_id=1, source_target_pairs={{0,16},{8,24},{16,0},{24,8},{1,17},{9,25},{17,1},{25,9},{2,18},{10... | collective-permute-start | bytes 98312 | tf_op jit(solution)/shard_map/ppermute | solution.py:184
  21.4 4.8 %collective-permute-start.3 = (bf16[64,256]{1,0:T(8,128)(2,1)S(1)}, bf16[64,256]{1,0:T(8,128)(2,1)S(1)}, u32[]{:S(2)}, u32[]{:S(2)}) collective-permute-start(bf16[64,256]{1,0:T(8,128)(2,1)S(1)} %get-tuple-element.23), channel_id=1, source_target_pairs={{0,24},{8,16},{16,8},{24,0},{1,25},{9,17},{17,9},{25,1},{2,26},{10... | collective-permute-start | bytes 98312 | tf_op jit(solution)/shard_map/ppermute | solution.py:184
  26.2 1.0 %copy-start = (bf16[1,128,2048]{2,1,0:T(8,128)(2,1)S(1)}, bf16[1,128,2048]{2,1,0:T(8,128)(2,1)}, u32[]{:S(2)}) copy-start(bf16[1,128,2048]{2,1,0:T(8,128)(2,1)} %param.8) | copy-start | bytes 1572868
  27.2 1.2 %copy-start.2 = (bf16[1,2048,256]{2,1,0:T(8,128)(2,1)S(1)}, bf16[1,2048,256]{2,1,0:T(8,128)(2,1)}, u32[]{:S(2)}) copy-start(bf16[1,2048,256]{2,1,0:T(8,128)(2,1)} %param.9) | copy-start | bytes 3145732
  28.5 1.2 %copy-start.3 = (bf16[1,256,2048]{2,1,0:T(8,128)(2,1)S(1)}, bf16[1,256,2048]{2,1,0:T(8,128)(2,1)}, u32[]{:S(2)}) copy-start(bf16[1,256,2048]{2,1,0:T(8,128)(2,1)} %param.10) | copy-start | bytes 3145732
  29.7 1.2 %copy-start.4 = (bf16[1,2048,256]{2,1,0:T(8,128)(2,1)S(1)}, bf16[1,2048,256]{2,1,0:T(8,128)(2,1)}, u32[]{:S(2)}) copy-start(bf16[1,2048,256]{2,1,0:T(8,128)(2,1)} %param.12) | copy-start | bytes 3145732
  30.9 1.9 %copy-start.1 = (bf16[1,128,2048]{2,1,0:T(8,128)(2,1)S(1)}, bf16[1,128,2048]{2,1,0:T(8,128)(2,1)}, u32[]{:S(2)}) copy-start(bf16[1,128,2048]{2,1,0:T(8,128)(2,1)} %param.8) | copy-start | bytes 1572868
  36.9 1.8 %collective-permute-start.9 = (bf16[96,2048]{1,0:T(8,128)(2,1)S(1)}, bf16[96,2048]{1,0:T(8,128)(2,1)S(1)}, u32[]{:S(2)}, u32[]{:S(2)}) collective-permute-start(bf16[96,2048]{1,0:T(8,128)(2,1)S(1)} %get-tuple-element.34), channel_id=1, source_target_pairs={{0,1},{1,0},{2,3},{3,2},{4,5},{5,4},{6,7},{7,6},{8,9},{9,8},{10,11... | collective-permute-start | bytes 1179656 | tf_op jit(solution)/shard_map/ppermute | solution.py:225
  37.6 22.7 %collective-permute-start.8 = (bf16[96,2048]{1,0:T(8,128)(2,1)S(1)}, bf16[96,2048]{1,0:T(8,128)(2,1)S(1)}, u32[]{:S(2)}, u32[]{:S(2)}) collective-permute-start(bf16[96,2048]{1,0:T(8,128)(2,1)S(1)} %get-tuple-element.32), channel_id=1, source_target_pairs={{0,1},{1,0},{2,3},{3,2},{4,5},{5,4},{6,7},{7,6},{8,9},{9,8},{10,11... | collective-permute-start | bytes 1179656 | tf_op jit(solution)/shard_map/ppermute | solution.py:236
  38.8 21.5 %collective-permute-start.10 = (bf16[96,2048]{1,0:T(8,128)(2,1)S(1)}, bf16[96,2048]{1,0:T(8,128)(2,1)S(1)}, u32[]{:S(2)}, u32[]{:S(2)}) collective-permute-start(bf16[96,2048]{1,0:T(8,128)(2,1)S(1)} %add_convert_fusion), channel_id=1, source_target_pairs={{0,4},{1,5},{2,6},{3,7},{4,0},{5,1},{6,2},{7,3},{8,12},{9,13},{10,... | collective-permute-start | bytes 1179656 | tf_op jit(solution)/shard_map/ppermute | solution.py:226
  41.0 1.2 %collective-permute-start.11 = (f32[1,2048]{1,0:T(1,128)S(1)}, f32[1,2048]{1,0:T(1,128)S(1)}, u32[]{:S(2)}, u32[]{:S(2)}) collective-permute-start(f32[1,2048]{1,0:T(1,128)S(1)} %add.37), channel_id=1, source_target_pairs={{0,1},{1,0},{2,3},{3,2},{4,5},{5,4},{6,7},{7,6},{8,9},{9,8},{10,11... | collective-permute-start | bytes 24584 | tf_op jit(solution)/shard_map/ppermute | solution.py:240
  41.2 6.4 %collective-permute-start.4 = (bf16[32,2048]{1,0:T(8,128)(2,1)S(1)}, bf16[32,2048]{1,0:T(8,128)(2,1)S(1)}, u32[]{:S(2)}, u32[]{:S(2)}) collective-permute-start(bf16[32,2048]{1,0:T(8,128)(2,1)S(1)} %get-tuple-element.39), channel_id=1, source_target_pairs={{0,8},{8,0},{16,24},{24,16},{1,9},{9,1},{17,25},{25,17},{2,10},{10... | collective-permute-start | bytes 393224 | tf_op jit(solution)/shard_map/ppermute | solution.py:203
  41.8 8.4 %collective-permute-start.5 = (bf16[32,2048]{1,0:T(8,128)(2,1)S(1)}, bf16[32,2048]{1,0:T(8,128)(2,1)S(1)}, u32[]{:S(2)}, u32[]{:S(2)}) collective-permute-start(bf16[32,2048]{1,0:T(8,128)(2,1)S(1)} %get-tuple-element.38), channel_id=1, source_target_pairs={{0,16},{8,24},{16,0},{24,8},{1,17},{9,25},{17,1},{25,9},{2,18},{10... | collective-permute-start | bytes 393224 | tf_op jit(solution)/shard_map/ppermute | solution.py:203
  42.3 7.9 %collective-permute-start.6 = (bf16[32,2048]{1,0:T(8,128)(2,1)S(1)}, bf16[32,2048]{1,0:T(8,128)(2,1)S(1)}, u32[]{:S(2)}, u32[]{:S(2)}) collective-permute-start(bf16[32,2048]{1,0:T(8,128)(2,1)S(1)} %get-tuple-element.37), channel_id=1, source_target_pairs={{0,24},{8,16},{16,8},{24,0},{1,25},{9,17},{17,9},{25,1},{2,26},{10... | collective-permute-start | bytes 393224 | tf_op jit(solution)/shard_map/ppermute | solution.py:203
  44.7 5.4 %copy-start.7 = (s32[64]{0:T(128)S(1)}, s32[64]{0:T(128)}, u32[]{:S(2)}) copy-start(s32[64]{0:T(128)} %assign_ref.1) | copy-start | bytes 772
  47.5 12.1 %collective-permute-start.12 = (f32[1,2048]{1,0:T(1,128)S(1)}, f32[1,2048]{1,0:T(1,128)S(1)}, u32[]{:S(2)}, u32[]{:S(2)}) collective-permute-start(f32[1,2048]{1,0:T(1,128)S(1)} %add.38), channel_id=1, source_target_pairs={{0,4},{1,5},{2,6},{3,7},{4,0},{5,1},{6,2},{7,3},{8,12},{9,13},{10,... | collective-permute-start | bytes 24584 | tf_op jit(solution)/shard_map/ppermute | solution.py:241

commit v2 on v1

v2 whole, which is shorter than its diff:
```python
import functools
import math

import jax
import jax.numpy as jnp
from jax import lax
from jax.experimental import pallas as pl
from jax.experimental.pallas import tpu as pltpu
from jax.sharding import PartitionSpec as P

EMB = 128
MIB = 1024 * 1024
VM = 48
COST = 10**10
VMEM_LIMIT = 24 * MIB
BF16 = jnp.bfloat16
F32 = jnp.float32
HBM, VMEM, SMEM = pltpu.HBM, pltpu.VMEM, pltpu.SMEM


def mm(a, b):
    return jnp.dot(a, b, preferred_element_type=F32)


def mm_nt(a, b):
    return lax.dot_general(a, b, (((1,), (1,)), ((), ())), preferred_element_type=F32)


def call(kernel, outs, scratch, spaces, args, name, vmem=VMEM_LIMIT, cost=COST):
    return pl.pallas_call(
        kernel,
        out_shape=outs,
        in_specs=[pl.BlockSpec(memory_space=space) for space in spaces],
        out_specs=[pl.BlockSpec(memory_space=pltpu.VMEM)] * len(outs),
        scratch_shapes=scratch,
        compiler_params=pltpu.CompilerParams(vmem_limit_bytes=vmem),
        cost_estimate=pl.CostEstimate(flops=cost, bytes_accessed=1, transcendentals=0),
        name=name,
    )(*args)


def column_chunks(width):
    step = 512 if width % 512 == 0 else width
    return [slice(c, c + step) for c in range(0, width, step)]


def copy_all(pairs, sem_ref):
    copies = [pltpu.make_async_copy(a, b, sem_ref.at[i]) for i, (a, b) in enumerate(pairs)]
    for copy in copies:
        copy.start()
    return copies


def cut_kernel(n_tower, grad_ref, *refs):
    pieces, sem_ref = refs[:n_tower], refs[n_tower]
    me = lax.axis_index("tower")
    out = pieces[0].shape[1]
    pairs = [
        (grad_ref.at[:, pl.ds(pl.multiple_of((me ^ k) * out, out), out)], piece)
        for k, piece in enumerate(pieces)
    ]
    for copy in copy_all(pairs, sem_ref):
        copy.wait()


def forward_rows(x_ref, wd_ref, wu_ref, bias_ref, low_ref, cr_ref, factor_ref, ready=None):
    low = mm(x_ref[...], wd_ref[...]).astype(BF16)
    low_ref[...] = low
    if ready is not None:
        ready.wait()
    for c in column_chunks(x_ref.shape[1]):
        factor = (mm(low, wu_ref[:, c]) + bias_ref[:, c]) + 1.0
        cr_ref[:, c] = (x_ref[:, c].astype(F32) * factor).astype(BF16)
        if factor_ref is not None:
            factor_ref[:, c] = factor


def backward_rows(x_ref, g, low_ref, wu_ref, wo_ref, gg_ref, bg_ref, ht_ref, factor_ref, direct_ref):
    rank = wu_ref.shape[0]
    grad_hidden = jnp.zeros((x_ref.shape[0], rank), F32)
    for c in column_chunks(x_ref.shape[1]):
        x = x_ref[:, c].astype(F32)
        grad_crossed = mm_nt(g, wo_ref[c, :]).astype(BF16).astype(F32)
        grad_gate = grad_crossed * x
        bg_ref[:, c] = jnp.sum(grad_gate, axis=0, keepdims=True)
        low = grad_gate.astype(BF16)
        gg_ref[:, c] = low
        grad_hidden += mm_nt(low, wu_ref[:, c])
        if direct_ref is not None:
            direct_ref[:, c] = grad_crossed * factor_ref[:, c]
    grad_hidden = grad_hidden.astype(BF16)
    ht_ref[0:rank, :] = grad_hidden.T
    ht_ref[rank : 2 * rank, :] = low_ref[...].T
    ht_ref[2 * rank :, :] = g.T
    return grad_hidden


def forward_kernel(wd_hbm, wu_hbm, wo_hbm, x_hbm, bias_ref, wd_ref, wu_ref, wo_ref, x_ref, low_ref, cr_ref, factor_ref, sem_ref):
    copies = copy_all([(x_hbm, x_ref), (wd_hbm, wd_ref), (wu_hbm, wu_ref), (wo_hbm, wo_ref)], sem_ref)
    copies[0].wait()
    copies[1].wait()
    forward_rows(x_ref, wd_ref, wu_ref, bias_ref, low_ref, cr_ref, factor_ref, copies[2])
    copies[3].wait()


def forward_other_kernel(wd_ref, wu_ref, bias_ref, x_ref, low_ref, cr_ref):
    forward_rows(x_ref, wd_ref, wu_ref, bias_ref, low_ref, cr_ref, None)


def backward_kernel(n_tower, wu_ref, wo_ref, x_ref, low_ref, factor_ref, *refs):
    pieces = refs[:n_tower]
    g_ref, gh_ref, ht_ref, gg_ref, bg_ref, direct_ref = refs[n_tower:]
    me = lax.axis_index("tower")
    rows = pieces[0].shape[0]
    for k, piece in enumerate(pieces):
        g_ref[pl.ds(pl.multiple_of((me ^ k) * rows, rows), rows), :] = piece[...]
    gh_ref[...] = backward_rows(
        x_ref, g_ref[...], low_ref, wu_ref, wo_ref, gg_ref, bg_ref, ht_ref, factor_ref, direct_ref
    )


def inputs_kernel(n_tower, wd_ref, gh_ref, direct_ref, *refs):
    pieces, gi_ref = refs[:n_tower], refs[n_tower]
    me = lax.axis_index("tower")
    rows = pieces[0].shape[0]
    grad_hidden = gh_ref[...]
    for c in column_chunks(gi_ref.shape[1]):
        gi_ref[:, c] = (direct_ref[:, c] + mm_nt(grad_hidden, wd_ref[c, :])).astype(BF16)
    for k, piece in enumerate(pieces):
        piece[...] = gi_ref[pl.ds(pl.multiple_of((me ^ k) * rows, rows), rows), :]


def products(group, ht_a, ht_b, operands, lhs_ref, acc_ref, send_refs, keep_ref):
    shard = lax.axis_index("shard")
    block = keep_ref.shape[0]
    rank = ht_a.shape[0] // 3
    rows_a = ht_a.shape[1]
    core = lax.rem(shard, 2)
    first = (group * 4 + (lax.rem(shard, 4) - core)) * block
    picked = pl.ds(pl.multiple_of(first, 2 * block), 2 * block)
    lhs_ref[:, :rows_a] = ht_a[picked, :]
    lhs_ref[:, rows_a:] = ht_b[picked, :]
    acc_ref[...] = jnp.zeros_like(acc_ref)
    for part, (a_ref, b_ref) in enumerate(operands):

        @pl.when((first < (part + 1) * rank) & (first + 2 * block > part * rank))
        def _():
            at = first + lax.broadcasted_iota(jnp.int32, lhs_ref.shape, 0)
            inside = (at >= part * rank) & (at < (part + 1) * rank)
            lhs = jnp.where(inside, lhs_ref[...].astype(F32), 0.0).astype(BF16)
            for c in column_chunks(acc_ref.shape[1]):
                rhs = jnp.concatenate([a_ref[:, c], b_ref[:, c]], axis=0)
                acc_ref[:, c] += mm(lhs, rhs)

    other = pl.ds(pl.multiple_of((1 - core) * block, block), block)
    width = send_refs[0].shape[1]
    for i, send_ref in enumerate(send_refs):
        send_ref[...] = acc_ref[other, i * width : (i + 1) * width].astype(BF16)
    keep_ref[...] = acc_ref[pl.ds(pl.multiple_of(core * block, block), block), :]


def far_kernel(n_cuts, wu_ref, wo_ref, x_own, gg_own, cr_own, ht_own, bg_own, x_ref, low_ref, cr_ref, g_ref, *refs):
    gg_ref, ht_ref, bg_ref, keep_ref = refs[:4]
    send_refs = refs[4 : 4 + n_cuts]
    lhs_ref, acc_ref = refs[4 + n_cuts :]
    backward_rows(x_ref, g_ref[...], low_ref, wu_ref, wo_ref, gg_ref, bg_ref, ht_ref, None, None)
    bg_ref[...] = bg_own[...] + bg_ref[...]
    group = 1 - lax.div(lax.axis_index("shard"), 4)
    operands = ((x_own, x_ref), (gg_own, gg_ref), (cr_own, cr_ref))
    products(group, ht_own, ht_ref, operands, lhs_ref, acc_ref, send_refs, keep_ref)


def near_kernel(x_own, gg_own, cr_own, ht_own, x_ref, gg_ref, cr_ref, ht_ref, send_ref, keep_ref, lhs_ref, acc_ref):
    group = lax.div(lax.axis_index("shard"), 4)
    operands = ((x_own, x_ref), (gg_own, gg_ref), (cr_own, cr_ref))
    products(group, ht_own, ht_ref, operands, lhs_ref, acc_ref, [send_ref], keep_ref)


def round_kernel(at, keep_ref, recv_ref, out_ref):
    width = out_ref.shape[1]
    out_ref[...] = (keep_ref[:, at * width : (at + 1) * width] + recv_ref[...].astype(F32)).astype(BF16)


def final_kernel(scale, keep_ref, near_ref, bias_ref, bias_far_ref, *refs):
    fars, out_ref, bg_ref = refs[:-2], refs[-2], refs[-1]
    bg_ref[...] = bias_ref[...] + bias_far_ref[...]
    width = fars[0].shape[1]
    for i, far in enumerate(fars):
        c = slice(i * width, (i + 1) * width)
        out_ref[:, c] = ((keep_ref[:, c] + near_ref[:, c].astype(F32)) + far[...].astype(F32)) * scale


def place_kernel(n_tower, assign_ref, *refs):
    pieces, out_ref = refs[:n_tower], refs[n_tower]
    me = lax.axis_index("tower")
    slots = pieces[0].shape[1] // EMB
    for k in range(n_tower):
        for j in range(slots):
            at = assign_ref[(me ^ k) * slots + j] * EMB
            out_ref[:, pl.ds(pl.multiple_of(at, EMB), EMB)] = pieces[k][:, j * EMB : (j + 1) * EMB]


def xor_pairs(n, k):
    return [(i, i ^ k) for i in range(n)]


def after(value, *earlier):
    return lax.optimization_barrier((value, *earlier))[0]


def paired_body(out_grad, pooled, down_proj, up_proj, cross_bias, out_proj, assign):
    n_tower, n_shard = lax.axis_size("tower"), lax.axis_size("shard")
    sds = jax.ShapeDtypeStruct
    w_down, w_up, w_out, x = down_proj[0], up_proj[0], out_proj[0], pooled[0]
    n, width = x.shape
    rank, out = w_up.shape[0], w_out.shape[1]
    stack = 2 * rank + out
    block = stack // n_shard
    top_rows = out_grad.shape[0]
    n_cuts = 1
    cut = width // n_cuts
    wide = sds((n, width), BF16)
    tall = sds((stack, n), BF16)
    low = sds((n, rank), BF16)
    row = sds((1, width), F32)

    def across(value, axis, k):
        return lax.ppermute(value, axis, xor_pairs(lax.axis_size(axis), k))

    x_other = across(x, "shard", 2)
    pieces = call(
        functools.partial(cut_kernel, n_tower),
        [sds((top_rows, out), BF16)] * n_tower,
        [pltpu.SemaphoreType.DMA((n_tower,))],
        [HBM],
        [out_grad],
        "cut_columns",
        60 * MIB,
        1,
    )
    pieces = [pieces[0]] + [across(pieces[k], "tower", k) for k in range(1, n_tower)]
    wd, wu, wo, x_own, low_own, cr_own, factor = call(
        forward_kernel,
        [sds(w.shape, BF16) for w in (w_down, w_up, w_out)] + [wide, low, wide, sds((n, width), F32)],
        [pltpu.SemaphoreType.DMA((4,))],
        [HBM] * 4 + [VMEM],
        [w_down, w_up, w_out, x, cross_bias],
        "forward_own",
        VM * MIB,
        1,
    )
    g_own, gh_own, ht_own, gg_own, bg_own, direct = call(
        functools.partial(backward_kernel, n_tower),
        [sds((n, out), BF16), low, tall, wide, row, sds((n, width), F32)],
        [],
        [VMEM] * (5 + n_tower),
        [wu, wo, x_own, low_own, factor, *pieces],
        "backward_own",
        cost=1,
    )
    g_other = across(g_own, "shard", 2)
    grad_inputs = call(
        functools.partial(inputs_kernel, n_tower),
        [sds((top_rows, width), BF16)] * n_tower,
        [pltpu.VMEM((n, width), BF16)],
        [VMEM] * 3,
        [wd, gh_own, direct],
        "grad_inputs",
    )
    returned = [grad_inputs[0]] + [across(grad_inputs[k], "tower", k) for k in range(1, n_tower)]
    low_other, cr_other = call(
        forward_other_kernel,
        [low, wide],
        [],
        [VMEM] * 4,
        [wd, wu, cross_bias, x_other],
        "forward_other",
    )
    gg_other, ht_other, bias_sum, far_keep, *far_sends = call(
        functools.partial(far_kernel, n_cuts),
        [wide, tall, row, sds((block, width), F32)] + [sds((block, cut), BF16)] * n_cuts,
        [pltpu.VMEM((2 * block, 2 * n), BF16), pltpu.VMEM((2 * block, width), F32)],
        [VMEM] * 11,
        [wu, wo, x_own, gg_own, cr_own, ht_own, bg_own, x_other, low_other, cr_other, g_other],
        "far_sums",
    )
    fars = []
    for i, send in enumerate(far_sends):
        (far,) = call(
            functools.partial(round_kernel, i),
            [sds((block, cut), BF16)],
            [],
            [VMEM] * 2,
            [far_keep, across(send, "shard", 1)],
            "far_round",
            cost=1,
        )
        fars.append(across(far, "shard", 4))
    near_send, near_keep = call(
        near_kernel,
        [sds((block, width), BF16), sds((block, width), F32)],
        [pltpu.VMEM((2 * block, 2 * n), BF16), pltpu.VMEM((2 * block, width), F32)],
        [VMEM] * 8,
        [x_own, gg_own, cr_own, ht_own, x_other, gg_other, cr_other, after(ht_other, far)],
        "near_sums",
    )
    near_other = across(near_send, "shard", 1)
    bias_sum = bias_sum + across(bias_sum, "shard", 1)
    bias_far = across(bias_sum, "shard", 4)
    (feature_grad,) = call(
        functools.partial(place_kernel, n_tower),
        [sds((top_rows, n_tower * width), BF16)],
        [],
        [SMEM] + [VMEM] * n_tower,
        [assign, *returned],
        "place_features",
        cost=1,
    )
    weight_grad, bias_grad = call(
        functools.partial(final_kernel, 1.0 / math.sqrt(n * n_shard)),
        [sds((block, width), F32), row],
        [],
        [VMEM] * (4 + n_cuts),
        [near_keep, near_other, bias_sum, bias_far, *fars],
        "add_up",
    )
    return feature_grad, weight_grad[None], bias_grad


def general_body(out_grad, pooled, down_proj, up_proj, cross_bias, out_proj, assign):
    grad_out = lax.all_to_all(out_grad, "tower", split_axis=1, concat_axis=0, tiled=True)
    feature_in = pooled[0]
    w_down, w_up, w_out = down_proj[0], up_proj[0], out_proj[0]
    hidden_low = mm(feature_in, w_down).astype(BF16)
    factor = mm(hidden_low, w_up) + cross_bias + 1.0
    crossed = (feature_in * factor).astype(BF16)
    grad_crossed = mm_nt(grad_out, w_out).astype(BF16)
    grad_gate = grad_crossed.astype(F32) * feature_in
    grad_gate_low = grad_gate.astype(BF16)
    grad_hidden = mm_nt(grad_gate_low, w_up).astype(BF16)
    grad_inputs = (grad_crossed.astype(F32) * factor + mm_nt(grad_hidden, w_down)).astype(BF16)
    returned = lax.all_to_all(grad_inputs, "tower", split_axis=0, concat_axis=1, tiled=True)
    local_rows = returned.shape[0]
    blocks = returned.reshape(local_rows, -1, EMB)
    feature_grad = jnp.take(blocks, jnp.argsort(assign), axis=1).reshape(local_rows, -1)
    stacked = jnp.concatenate(
        [
            mm(grad_hidden.T, feature_in),
            mm(hidden_low.T, grad_gate_low),
            mm(grad_out.T, crossed),
        ],
        axis=0,
    )
    scale = 1.0 / math.sqrt(grad_out.shape[0] * lax.axis_size("shard"))
    summed = lax.psum_scatter(stacked, "shard", scatter_dimension=0, tiled=True)
    bias_grad = lax.psum(jnp.sum(grad_gate, axis=0), "shard")[None]
    return feature_grad, (summed * scale)[None], bias_grad


def solution(mesh):
    n_tower, n_shard = mesh.shape["tower"], mesh.shape["shard"]
    placed = (
        P(("tower", "shard"), None),
        P("tower", "shard", None),
        P("tower", None, None),
        P("tower", None, None),
        P("tower", None),
        P("tower", None, None),
        P(),
    )

    paired = n_shard == 2 * 4 and n_tower & (n_tower - 1) == 0
    return jax.shard_map(
        paired_body if paired else general_body,
        mesh=mesh,
        in_specs=placed,
        out_specs=(P(("tower", "shard"), None), P("tower", "shard", None), P("tower", None)),
        check_vma=False,
    )
```

time: 61.6 us -> 44.5 us (0.72)
  waiting for transfers between devices: 31.2 us -> 16.6 us
  local copies, waits for them, and re-layouts: 5.62 us -> 1.06 us
  Pallas kernels: 8.05 us -> 11.1 us
  other arithmetic: 1.72 us -> 0.01 us
  starting transfers between devices: 14 us -> 14.7 us
    ppermute x13, waiting for transfers between devices: 31.2 us -> 16.6 us  [across(): return lax.ppermute(value, axis, xor_pairs(lax.axis_size(axis), k))]
    unnamed x16 -> x8, local copies, waits for them, and re-layouts: 5.57 us -> 1.06 us
    pallas_call x5 -> x10, Pallas kernels: 8.05 us -> 11.1 us  [call(): pl.pallas_call(kernel, out_shape=outs, in_specs=[pl.BlockSpec(memory_spac...]
    broadcast_in_dim x1 -> x0, other arithmetic: 1.02 us -> none  [paired_body(): weight_grad = ((near + far.astype(F32)) * scale)[None]]
    ppermute x13, starting transfers between devices: 14 us -> 14.7 us  [across(): return lax.ppermute(value, axis, xor_pairs(lax.axis_size(axis), k))]
    add x3 -> x1, other arithmetic: 0.63 us -> 0.01 us  [paired_body(): bias_sum = bias_sum + across(bias_sum, 'shard', 1)]
  transfers between devices with their start and end apart: 13 -> 13, of which waited for: 8 -> 7; matrix products, arithmetic and copies ran while one was open for 1% -> 0% of each run, Pallas kernels for 7% -> 18%
where the time goes in v2:
time: 44.5 us; the launch traced here: 44.2 us
  waiting for transfers between devices  16.6 us (37%)
  starting transfers between devices  14.7 us (33%)
  Pallas kernels  11.1 us (25%)
  local copies, waits for them, and re-layouts  1.06 us (2%)
  between operations  0.75 us (2%)
    ppermute x13, waiting for transfers between devices, across(): return lax.ppermute(value, axis, xor_pairs(lax.axis_size(axis), k))  16.6 us
    ppermute x13, starting transfers between devices, across(): return lax.ppermute(value, axis, xor_pairs(lax.axis_size(axis), k))  14.7 us
    pallas_call x10, Pallas kernels, call(): pl.pallas_call(kernel, out_shape=outs, in_specs=[pl.BlockSpec(memory_spac...  11.1 us
    unnamed x8, local copies, waits for them, and re-layouts  1.06 us
  transfers between devices with their start and end apart: 13, of which 7 were waited for; matrix products, arithmetic and copies ran while one was open for 0% of the time, Pallas kernels for 18%

profile of v2, /device:TPU:0, one launch (start us, length us, event | category | flops | bytes accessed | tf_op | source)
XLA Modules:
  0.0 44.2 jit_solution(12398411967023307669)
XLA Ops:
  0.6 3.1 %collective-permute-start.6 = (bf16[128,2048]{1,0:T(8,128)(2,1)}, bf16[128,2048]{1,0:T(8,128)(2,1)S(1)}, u32[]{:S(2)}, u32[]{:S(2)}) collective-permute-start(bf16[128,2048]{1,0:T(8,128)(2,1)} %bitcast.5), channel_id=1, source_target_pairs={{0,2},{1,3},{2,0},{3,1},{4,6},{5,7},{6,4},{7,5},{8,10},{9,11},{10,... | collective-permute-start | bytes 1572872 | tf_op jit(solution)/shard_map/ppermute | solution.py:228
  3.7 1.4 %cut_columns.1 = (bf16[32,256]{1,0:T(8,128)(2,1)}, bf16[32,256]{1,0:T(8,128)(2,1)}, bf16[32,256]{1,0:T(8,128)(2,1)}, bf16[32,256]{1,0:T(8,128)(2,1)}) custom-call(bf16[32,1024]{1,0:T(8,128)(2,1)} %grad_ref.1), custom_call_target="tpu_custom_call" | custom-call | flops 1 | bytes 1 | tf_op jit(solution)/shard_map/cut_columns/pallas_call | solution.py:30
  5.2 1.6 %collective-permute-start = (bf16[32,256]{1,0:T(8,128)(2,1)}, bf16[32,256]{1,0:T(8,128)(2,1)S(1)}, u32[]{:S(2)}, u32[]{:S(2)}) collective-permute-start(bf16[32,256]{1,0:T(8,128)(2,1)} %get-tuple-element.43), channel_id=1, source_target_pairs={{0,8},{8,0},{16,24},{24,16},{1,9},{9,1},{17,25},{25,17},{2,10},{10... | collective-permute-start | bytes 49160 | tf_op jit(solution)/shard_map/ppermute | solution.py:228
  6.7 1.5 %collective-permute-start.1 = (bf16[32,256]{1,0:T(8,128)(2,1)}, bf16[32,256]{1,0:T(8,128)(2,1)S(1)}, u32[]{:S(2)}, u32[]{:S(2)}) collective-permute-start(bf16[32,256]{1,0:T(8,128)(2,1)} %get-tuple-element.44), channel_id=1, source_target_pairs={{0,16},{8,24},{16,0},{24,8},{1,17},{9,25},{17,1},{25,9},{2,18},{10... | collective-permute-start | bytes 49160 | tf_op jit(solution)/shard_map/ppermute | solution.py:228
  8.2 0.5 %collective-permute-start.2 = (bf16[32,256]{1,0:T(8,128)(2,1)}, bf16[32,256]{1,0:T(8,128)(2,1)S(1)}, u32[]{:S(2)}, u32[]{:S(2)}) collective-permute-start(bf16[32,256]{1,0:T(8,128)(2,1)} %get-tuple-element.45), channel_id=1, source_target_pairs={{0,24},{8,16},{16,8},{24,0},{1,25},{9,17},{17,9},{25,1},{2,26},{10... | collective-permute-start | bytes 49160 | tf_op jit(solution)/shard_map/ppermute | solution.py:228
  8.7 1.0 %copy-done = bf16[1,128,2048]{2,1,0:T(8,128)(2,1)S(1)} copy-done((bf16[1,128,2048]{2,1,0:T(8,128)(2,1)S(1)}, bf16[1,128,2048]{2,1,0:T(8,128)(2,1)}, u32[]{:S(2)}) %copy-start) | copy-done | bytes 524312
  9.8 2.1 %forward_own.1 = (bf16[2048,256]{1,0:T(8,128)(2,1)S(1)}, bf16[256,2048]{1,0:T(8,128)(2,1)S(1)}, bf16[2048,256]{1,0:T(8,128)(2,1)S(1)}, bf16[128,2048]{1,0:T(8,12...) custom-call(bf16[2048,256]{1,0:T(8,128)(2,1)} %bitcast.7, ...), custom_call_target="tpu_custom_call" | custom-call | flops 1 | bytes 1 | tf_op jit(solution)/shard_map/forward_own/pallas_call | solution.py:30
  11.9 1.2 %collective-permute-done.2.refs_3_ = bf16[32,256]{1,0:T(8,128)(2,1)S(1)} collective-permute-done((bf16[32,256]{1,0:T(8,128)(2,1)}, bf16[32,256]{1,0:T(8,128)(2,1)S(1)}, u32[]{:S(2)}, u32[]{:S(2)}) %collective-permute-start.2) | collective-permute-done | bytes 16416 | tf_op jit(solution)/shard_map/ppermute | solution.py:228
  13.1 1.1 %backward_own.1 = (bf16[128,256]{1,0:T(8,128)(2,1)S(1)}, bf16[128,256]{1,0:T(8,128)(2,1)S(1)}, bf16[768,128]{1,0:T(8,128)(2,1)S(1)}, bf16[128,2048]{1,0:T(8,128)...) custom-call(bf16[256,2048]{1,0:T(8,128)(2,1)S(1)} %get-tuple-element.37.wu_ref, ...), custom_call_target="tpu_custom_call" | custom-call | flops 1 | bytes 1 | tf_op jit(solution)/shard_map/backward_own/pallas_call | solution.py:30
  14.2 0.5 %collective-permute-start.7 = (bf16[128,256]{1,0:T(8,128)(2,1)S(1)}, bf16[128,256]{1,0:T(8,128)(2,1)S(1)}, u32[]{:S(2)}, u32[]{:S(2)}) collective-permute-start(bf16[128,256]{1,0:T(8,128)(2,1)S(1)} %get-tuple-element.58), channel_id=1, source_target_pairs={{0,2},{1,3},{2,0},{3,1},{4,6},{5,7},{6,4},{7,5},{8,10},{9,11},{10,... | collective-permute-start | bytes 196616 | tf_op jit(solution)/shard_map/ppermute | solution.py:228
  14.7 1.9 %collective-permute-done.6.x_ref = bf16[128,2048]{1,0:T(8,128)(2,1)S(1)} collective-permute-done((bf16[128,2048]{1,0:T(8,128)(2,1)}, bf16[128,2048]{1,0:T(8,128)(2,1)S(1)}, u32[]{:S(2)}, u32[]{:S(2)}) %collective-permute-start.6) | collective-permute-done | bytes 524320 | tf_op jit(solution)/shard_map/ppermute | solution.py:228
  16.6 0.8 %forward_other.1 = (bf16[128,256]{1,0:T(8,128)(2,1)S(1)}, bf16[128,2048]{1,0:T(8,128)(2,1)S(1)}) custom-call(bf16[2048,256]{1,0:T(8,128)(2,1)S(1)} %get-tuple-element.36.wd_ref, bf16[256,2048]{1,0:T(8,128)(2,1)S(1)} %get-tuple-element.37.wu_ref, f32[1,2048]{1,0:T(1,128)S(1)} %copy-done.2, bf16[128,2048]{1,0:T(8,128)(2,1)S(1)} %collective-permute-done.6.x_ref), custom_call_target="tpu_custom_call" | custom-call | flops 10000000000 | bytes 1 | tf_op jit(solution)/shard_map/forward_other/pallas_call | solution.py:30
  17.3 1.2 %collective-permute-done.7.g_ref = bf16[128,256]{1,0:T(8,128)(2,1)S(1)} collective-permute-done((bf16[128,256]{1,0:T(8,128)(2,1)S(1)}, bf16[128,256]{1,0:T(8,128)(2,1)S(1)}, u32[]{:S(2)}, u32[]{:S(2)}) %collective-permute-start.7) | collective-permute-done | bytes 65568 | tf_op jit(solution)/shard_map/ppermute | solution.py:228
  18.5 2.0 %far_sums.1 = (bf16[128,2048]{1,0:T(8,128)(2,1)S(1)}, bf16[768,128]{1,0:T(8,128)(2,1)S(1)}, f32[1,2048]{1,0:T(1,128)S(1)}, f32[96,2048]{1,0:T(8,128)S(1)}, bf16[96,2048]{1,0:T(8,128)(2,1)S(1)}) custom-call(bf16[256,2048]{1,0:T(8,128)(2,1)S(1)} %get-tuple-element.37.wu_ref, bf16[2048,256]{1,0:T(8,128)(2,1)S(1)} %get-tuple-element.38.wo_ref, ...), custom_call_target="tpu_custom_call" | custom-call | flops 10000000000 | bytes 1 | tf_op jit(solution)/shard_map/far_sums/pallas_call | solution.py:30
  20.5 0.1 collective-permute-start.8
  20.6 0.5 %collective-permute-start.10 = (f32[1,2048]{1,0:T(1,128)S(1)}, f32[1,2048]{1,0:T(1,128)S(1)}, u32[]{:S(2)}, u32[]{:S(2)}) collective-permute-start(f32[1,2048]{1,0:T(1,128)S(1)} %get-tuple-element.66), channel_id=1, source_target_pairs={{0,1},{1,0},{2,3},{3,2},{4,5},{5,4},{6,7},{7,6},{8,9},{9,8},{10,11... | collective-permute-start | bytes 24584 | tf_op jit(solution)/shard_map/ppermute | solution.py:228
  21.1 1.2 %collective-permute-done.8.recv_ref = bf16[96,2048]{1,0:T(8,128)(2,1)S(1)} collective-permute-done((bf16[96,2048]{1,0:T(8,128)(2,1)S(1)}, bf16[96,2048]{1,0:T(8,128)(2,1)S(1)}, u32[]{:S(2)}, u32[]{:S(2)}) %collective-permute-start.8) | collective-permute-done | bytes 393248 | tf_op jit(solution)/shard_map/ppermute | solution.py:228
  22.3 0.1 far_round.1
  22.4 2.3 %collective-permute-start.12 = (bf16[96,2048]{1,0:T(8,128)(2,1)S(1)}, bf16[96,2048]{1,0:T(8,128)(2,1)S(1)}, u32[]{:S(2)}, u32[]{:S(2)}) collective-permute-start(bf16[96,2048]{1,0:T(8,128)(2,1)S(1)} %far_round.1), channel_id=1, source_target_pairs={{0,4},{1,5},{2,6},{3,7},{4,0},{5,1},{6,2},{7,3},{8,12},{9,13},{10,... | collective-permute-start | bytes 1179656 | tf_op jit(solution)/shard_map/ppermute | solution.py:228
  24.6 0.6 %near_sums.1 = (bf16[96,2048]{1,0:T(8,128)(2,1)S(1)}, f32[96,2048]{1,0:T(8,128)S(1)}) custom-call(bf16[128,2048]{1,0:T(8,128)(2,1)S(1)} %get-tuple-element.39.x_ref.x_own, bf16[128,2048]{1,0:T(8,128)(2,1)S(1)} %get-tuple-element.52.gg_own, bf16[128,2048]{1,0:T(8,128)(2,1)S(1)} %get-tuple-element.53.cr_own, bf16[768,128]{1,0:T(8,128)(2,1)S(1)} %get-tuple-element.54.ht_own, ...), custom_call_target="tpu_custom_call" | custom-call | flops 10000000000 | bytes 1 | tf_op jit(solution)/shard_map/near_sums/pallas_call | solution.py:30
  25.2 0.1 collective-permute-start.9
  25.3 0.5 %grad_inputs.1 = (bf16[32,2048]{1,0:T(8,128)(2,1)S(1)}, bf16[32,2048]{1,0:T(8,128)(2,1)S(1)}, bf16[32,2048]{1,0:T(8,128)(2,1)S(1)}, bf16[32,2048]{1,0:T(8,128)(2,1)S(1)}) custom-call(bf16[2048,256]{1,0:T(8,128)(2,1)S(1)} %get-tuple-element.36.wd_ref, bf16[128,256]{1,0:T(8,128)(2,1)S(1)} %get-tuple-element.46.gh_ref, f32[128,2048]{1,0:T(8,128)S(1)} %get-tuple-element.47.direct_ref), custom_call_target="tpu_custom_call" | custom-call | flops 10000000000 | bytes 1 | tf_op jit(solution)/shard_map/grad_inputs/pallas_call | solution.py:30
  25.8 0.6 %collective-permute-start.3 = (bf16[32,2048]{1,0:T(8,128)(2,1)S(1)}, bf16[32,2048]{1,0:T(8,128)(2,1)S(1)}, u32[]{:S(2)}, u32[]{:S(2)}) collective-permute-start(bf16[32,2048]{1,0:T(8,128)(2,1)S(1)} %get-tuple-element.49), channel_id=1, source_target_pairs={{0,8},{8,0},{16,24},{24,16},{1,9},{9,1},{17,25},{25,17},{2,10},{10... | collective-permute-start | bytes 393224 | tf_op jit(solution)/shard_map/ppermute | solution.py:228
  26.4 1.5 %collective-permute-start.4 = (bf16[32,2048]{1,0:T(8,128)(2,1)S(1)}, bf16[32,2048]{1,0:T(8,128)(2,1)S(1)}, u32[]{:S(2)}, u32[]{:S(2)}) collective-permute-start(bf16[32,2048]{1,0:T(8,128)(2,1)S(1)} %get-tuple-element.50), channel_id=1, source_target_pairs={{0,16},{8,24},{16,0},{24,8},{1,17},{9,25},{17,1},{25,9},{2,18},{10... | collective-permute-start | bytes 393224 | tf_op jit(solution)/shard_map/ppermute | solution.py:228
  27.9 1.4 %collective-permute-start.5 = (bf16[32,2048]{1,0:T(8,128)(2,1)S(1)}, bf16[32,2048]{1,0:T(8,128)(2,1)S(1)}, u32[]{:S(2)}, u32[]{:S(2)}) collective-permute-start(bf16[32,2048]{1,0:T(8,128)(2,1)S(1)} %get-tuple-element.51), channel_id=1, source_target_pairs={{0,24},{8,16},{16,8},{24,0},{1,25},{9,17},{17,9},{25,1},{2,26},{10... | collective-permute-start | bytes 393224 | tf_op jit(solution)/shard_map/ppermute | solution.py:228
  29.4 0.0 copy-start.3
  29.4 2.8 %collective-permute-done.3.refs_1_ = bf16[32,2048]{1,0:T(8,128)(2,1)S(1)} collective-permute-done((bf16[32,2048]{1,0:T(8,128)(2,1)S(1)}, bf16[32,2048]{1,0:T(8,128)(2,1)S(1)}, u32[]{:S(2)}, u32[]{:S(2)}) %collective-permute-start.3) | collective-permute-done | bytes 131104 | tf_op jit(solution)/shard_map/ppermute | solution.py:228
  32.2 1.1 %collective-permute-start.11 = (f32[1,2048]{1,0:T(1,128)S(1)}, f32[1,2048]{1,0:T(1,128)S(1)}, u32[]{:S(2)}, u32[]{:S(2)}) collective-permute-start(f32[1,2048]{1,0:T(1,128)S(1)} %add.3.bias_ref), channel_id=1, source_target_pairs={{0,4},{1,5},{2,6},{3,7},{4,0},{5,1},{6,2},{7,3},{8,12},{9,13},{10,... | collective-permute-start | bytes 24584 | tf_op jit(solution)/shard_map/ppermute | solution.py:228
  33.3 1.6 %collective-permute-done.4.refs_2_ = bf16[32,2048]{1,0:T(8,128)(2,1)S(1)} collective-permute-done((bf16[32,2048]{1,0:T(8,128)(2,1)S(1)}, bf16[32,2048]{1,0:T(8,128)(2,1)S(1)}, u32[]{:S(2)}, u32[]{:S(2)}) %collective-permute-start.4) | collective-permute-done | bytes 131104 | tf_op jit(solution)/shard_map/ppermute | solution.py:228
  34.8 1.5 %place_features.1 = bf16[32,8192]{1,0:T(8,128)(2,1)} custom-call(s32[64]{0:T(128)S(1)} %copy-done.3, bf16[32,2048]{1,0:T(8,128)(2,1)S(1)} %get-tuple-element.48.refs_0_, bf16[32,2048]{1,0:T(8,128)(2,1)S(1)} %collective-permute-done.3.refs_1_, bf16[32,2048]{1,0:T(8,128)(2,1)S(1)} %collective-permute-done.4.refs_2_, ...), custom_call_target="tpu_custom_call" | custom-call | flops 1 | bytes 1 | tf_op jit(solution)/shard_map/place_features/pallas_call | solution.py:30
  36.3 6.9 %collective-permute-done.11.bias_far_ref = f32[1,2048]{1,0:T(1,128)S(1)} collective-permute-done((f32[1,2048]{1,0:T(1,128)S(1)}, f32[1,2048]{1,0:T(1,128)S(1)}, u32[]{:S(2)}, u32[]{:S(2)}) %collective-permute-start.11) | collective-permute-done | bytes 8224 | tf_op jit(solution)/shard_map/ppermute | solution.py:228
  43.2 1.0 %add_up.1 = (f32[96,2048]{1,0:T(8,128)}, f32[1,2048]{1,0:T(1,128)}) custom-call(f32[96,2048]{1,0:T(8,128)S(1)} %get-tuple-element.64.keep_ref, bf16[96,2048]{1,0:T(8,128)(2,1)S(1)} %collective-permute-done.9.near_ref, f32[1,2048]{1,0:T(1,128)S(1)} %add.3.bias_ref, f32[1,2048]{1,0:T(1,128)S(1)} %collective-permute-done.11.bias_far_ref, ...), custom_call_target="tpu_custom_call" | custom-call | flops 10000000000 | bytes 1 | tf_op jit(solution)/shard_map/add_up/pallas_call | solution.py:30
  (13 shorter events, 0.0 us)
Async XLA Ops:
  0.6 15.9 %collective-permute-start.6 = (bf16[128,2048]{1,0:T(8,128)(2,1)}, bf16[128,2048]{1,0:T(8,128)(2,1)S(1)}, u32[]{:S(2)}, u32[]{:S(2)}) collective-permute-start(bf16[128,2048]{1,0:T(8,128)(2,1)} %bitcast.5), channel_id=1, source_target_pairs={{0,2},{1,3},{2,0},{3,1},{4,6},{5,7},{6,4},{7,5},{8,10},{9,11},{10,... | collective-permute-start | bytes 1572872 | tf_op jit(solution)/shard_map/ppermute | solution.py:228
  5.1 3.6 %copy-start.2 = (f32[1,2048]{1,0:T(1,128)S(1)}, f32[1,2048]{1,0:T(1,128)}, u32[]{:S(2)}) copy-start(f32[1,2048]{1,0:T(1,128)} %bias_ref.3) | copy-start | bytes 24580
  5.2 6.8 %collective-permute-start = (bf16[32,256]{1,0:T(8,128)(2,1)}, bf16[32,256]{1,0:T(8,128)(2,1)S(1)}, u32[]{:S(2)}, u32[]{:S(2)}) collective-permute-start(bf16[32,256]{1,0:T(8,128)(2,1)} %get-tuple-element.43), channel_id=1, source_target_pairs={{0,8},{8,0},{16,24},{24,16},{1,9},{9,1},{17,25},{25,17},{2,10},{10... | collective-permute-start | bytes 49160 | tf_op jit(solution)/shard_map/ppermute | solution.py:228
  6.7 5.2 %collective-permute-start.1 = (bf16[32,256]{1,0:T(8,128)(2,1)}, bf16[32,256]{1,0:T(8,128)(2,1)S(1)}, u32[]{:S(2)}, u32[]{:S(2)}) collective-permute-start(bf16[32,256]{1,0:T(8,128)(2,1)} %get-tuple-element.44), channel_id=1, source_target_pairs={{0,16},{8,24},{16,0},{24,8},{1,17},{9,25},{17,1},{25,9},{2,18},{10... | collective-permute-start | bytes 49160 | tf_op jit(solution)/shard_map/ppermute | solution.py:228
  8.2 4.8 %collective-permute-start.2 = (bf16[32,256]{1,0:T(8,128)(2,1)}, bf16[32,256]{1,0:T(8,128)(2,1)S(1)}, u32[]{:S(2)}, u32[]{:S(2)}) collective-permute-start(bf16[32,256]{1,0:T(8,128)(2,1)} %get-tuple-element.45), channel_id=1, source_target_pairs={{0,24},{8,16},{16,8},{24,0},{1,25},{9,17},{17,9},{25,1},{2,26},{10... | collective-permute-start | bytes 49160 | tf_op jit(solution)/shard_map/ppermute | solution.py:228
  8.7 1.0 %copy-start = (bf16[1,128,2048]{2,1,0:T(8,128)(2,1)S(1)}, bf16[1,128,2048]{2,1,0:T(8,128)(2,1)}, u32[]{:S(2)}) copy-start(bf16[1,128,2048]{2,1,0:T(8,128)(2,1)} %param.8) | copy-start | bytes 1572868
  9.8 3.3 %copy-start.1 = (bf16[32,256]{1,0:T(8,128)(2,1)S(1)}, bf16[32,256]{1,0:T(8,128)(2,1)}, u32[]{:S(2)}) copy-start(bf16[32,256]{1,0:T(8,128)(2,1)} %get-tuple-element.42.refs_0_) | copy-start | bytes 49156
  14.2 4.3 %collective-permute-start.7 = (bf16[128,256]{1,0:T(8,128)(2,1)S(1)}, bf16[128,256]{1,0:T(8,128)(2,1)S(1)}, u32[]{:S(2)}, u32[]{:S(2)}) collective-permute-start(bf16[128,256]{1,0:T(8,128)(2,1)S(1)} %get-tuple-element.58), channel_id=1, source_target_pairs={{0,2},{1,3},{2,0},{3,1},{4,6},{5,7},{6,4},{7,5},{8,10},{9,11},{10,... | collective-permute-start | bytes 196616 | tf_op jit(solution)/shard_map/ppermute | solution.py:228
  20.5 1.8 %collective-permute-start.8 = (bf16[96,2048]{1,0:T(8,128)(2,1)S(1)}, bf16[96,2048]{1,0:T(8,128)(2,1)S(1)}, u32[]{:S(2)}, u32[]{:S(2)}) collective-permute-start(bf16[96,2048]{1,0:T(8,128)(2,1)S(1)} %get-tuple-element.62), channel_id=1, source_target_pairs={{0,1},{1,0},{2,3},{3,2},{4,5},{5,4},{6,7},{7,6},{8,9},{9,8},{10,11... | collective-permute-start | bytes 1179656 | tf_op jit(solution)/shard_map/ppermute | solution.py:228
  20.6 7.4 %collective-permute-start.10 = (f32[1,2048]{1,0:T(1,128)S(1)}, f32[1,2048]{1,0:T(1,128)S(1)}, u32[]{:S(2)}, u32[]{:S(2)}) collective-permute-start(f32[1,2048]{1,0:T(1,128)S(1)} %get-tuple-element.66), channel_id=1, source_target_pairs={{0,1},{1,0},{2,3},{3,2},{4,5},{5,4},{6,7},{7,6},{8,9},{9,8},{10,11... | collective-permute-start | bytes 24584 | tf_op jit(solution)/shard_map/ppermute | solution.py:228
  22.4 20.9 %collective-permute-start.12 = (bf16[96,2048]{1,0:T(8,128)(2,1)S(1)}, bf16[96,2048]{1,0:T(8,128)(2,1)S(1)}, u32[]{:S(2)}, u32[]{:S(2)}) collective-permute-start(bf16[96,2048]{1,0:T(8,128)(2,1)S(1)} %far_round.1), channel_id=1, source_target_pairs={{0,4},{1,5},{2,6},{3,7},{4,0},{5,1},{6,2},{7,3},{8,12},{9,13},{10,... | collective-permute-start | bytes 1179656 | tf_op jit(solution)/shard_map/ppermute | solution.py:228
  25.2 18.0 %collective-permute-start.9 = (bf16[96,2048]{1,0:T(8,128)(2,1)S(1)}, bf16[96,2048]{1,0:T(8,128)(2,1)S(1)}, u32[]{:S(2)}, u32[]{:S(2)}) collective-permute-start(bf16[96,2048]{1,0:T(8,128)(2,1)S(1)} %get-tuple-element.65), channel_id=1, source_target_pairs={{0,1},{1,0},{2,3},{3,2},{4,5},{5,4},{6,7},{7,6},{8,9},{9,8},{10,11... | collective-permute-start | bytes 1179656 | tf_op jit(solution)/shard_map/ppermute | solution.py:228
  25.8 6.4 %collective-permute-start.3 = (bf16[32,2048]{1,0:T(8,128)(2,1)S(1)}, bf16[32,2048]{1,0:T(8,128)(2,1)S(1)}, u32[]{:S(2)}, u32[]{:S(2)}) collective-permute-start(bf16[32,2048]{1,0:T(8,128)(2,1)S(1)} %get-tuple-element.49), channel_id=1, source_target_pairs={{0,8},{8,0},{16,24},{24,16},{1,9},{9,1},{17,25},{25,17},{2,10},{10... | collective-permute-start | bytes 393224 | tf_op jit(solution)/shard_map/ppermute | solution.py:228
  26.4 8.4 %collective-permute-start.4 = (bf16[32,2048]{1,0:T(8,128)(2,1)S(1)}, bf16[32,2048]{1,0:T(8,128)(2,1)S(1)}, u32[]{:S(2)}, u32[]{:S(2)}) collective-permute-start(bf16[32,2048]{1,0:T(8,128)(2,1)S(1)} %get-tuple-element.50), channel_id=1, source_target_pairs={{0,16},{8,24},{16,0},{24,8},{1,17},{9,25},{17,1},{25,9},{2,18},{10... | collective-permute-start | bytes 393224 | tf_op jit(solution)/shard_map/ppermute | solution.py:228
  27.9 6.9 %collective-permute-start.5 = (bf16[32,2048]{1,0:T(8,128)(2,1)S(1)}, bf16[32,2048]{1,0:T(8,128)(2,1)S(1)}, u32[]{:S(2)}, u32[]{:S(2)}) collective-permute-start(bf16[32,2048]{1,0:T(8,128)(2,1)S(1)} %get-tuple-element.51), channel_id=1, source_target_pairs={{0,24},{8,16},{16,8},{24,0},{1,25},{9,17},{17,9},{25,1},{2,26},{10... | collective-permute-start | bytes 393224 | tf_op jit(solution)/shard_map/ppermute | solution.py:228
  29.4 5.5 %copy-start.3 = (s32[64]{0:T(128)S(1)}, s32[64]{0:T(128)}, u32[]{:S(2)}) copy-start(s32[64]{0:T(128)} %assign_ref.1) | copy-start | bytes 772
  32.2 11.1 %collective-permute-start.11 = (f32[1,2048]{1,0:T(1,128)S(1)}, f32[1,2048]{1,0:T(1,128)S(1)}, u32[]{:S(2)}, u32[]{:S(2)}) collective-permute-start(f32[1,2048]{1,0:T(1,128)S(1)} %add.3.bias_ref), channel_id=1, source_target_pairs={{0,4},{1,5},{2,6},{3,7},{4,0},{5,1},{6,2},{7,3},{8,12},{9,13},{10,... | collective-permute-start | bytes 24584 | tf_op jit(solution)/shard_map/ppermute | solution.py:228

commit v3 on v2

--- a/solution.py
+++ b/solution.py
@@ -9,9 +9,12 @@
 from jax.sharding import PartitionSpec as P
 
 EMB = 128
+SLAB = 256
+TILE = 16
 MIB = 1024 * 1024
 VM = 48
 COST = 10**10
+FAR = 6
 VMEM_LIMIT = 24 * MIB
 BF16 = jnp.bfloat16
 F32 = jnp.float32
@@ -26,12 +29,13 @@
     return lax.dot_general(a, b, (((1,), (1,)), ((), ())), preferred_element_type=F32)
 
 
-def call(kernel, outs, scratch, spaces, args, name, vmem=VMEM_LIMIT, cost=COST):
+def call(kernel, outs, scratch, spaces, args, name, vmem=VMEM_LIMIT, cost=COST, out_space=None, aliases={}):
     return pl.pallas_call(
         kernel,
         out_shape=outs,
         in_specs=[pl.BlockSpec(memory_space=space) for space in spaces],
-        out_specs=[pl.BlockSpec(memory_space=pltpu.VMEM)] * len(outs),
+        out_specs=[pl.BlockSpec(memory_space=out_space or VMEM)] * len(outs),
+        input_output_aliases=aliases,
         scratch_shapes=scratch,
         compiler_params=pltpu.CompilerParams(vmem_limit_bytes=vmem),
         cost_estimate=pl.CostEstimate(flops=cost, bytes_accessed=1, transcendentals=0),
@@ -63,7 +67,7 @@
         copy.wait()
 
 
-def forward_rows(x_ref, wd_ref, wu_ref, bias_ref, low_ref, cr_ref, factor_ref, ready=None):
+def forward_rows(x_ref, wd_ref, wu_ref, bias_ref, low_ref, cr_ref, factor_ref=None, ready=None):
     low = mm(x_ref[...], wd_ref[...]).astype(BF16)
     low_ref[...] = low
     if ready is not None:
@@ -103,10 +107,6 @@
     copies[3].wait()
 
 
-def forward_other_kernel(wd_ref, wu_ref, bias_ref, x_ref, low_ref, cr_ref):
-    forward_rows(x_ref, wd_ref, wu_ref, bias_ref, low_ref, cr_ref, None)
-
-
 def backward_kernel(n_tower, wu_ref, wo_ref, x_ref, low_ref, factor_ref, *refs):
     pieces = refs[:n_tower]
     g_ref, gh_ref, ht_ref, gg_ref, bg_ref, direct_ref = refs[n_tower:]
@@ -130,13 +130,13 @@
         piece[...] = gi_ref[pl.ds(pl.multiple_of((me ^ k) * rows, rows), rows), :]
 
 
-def products(group, ht_a, ht_b, operands, lhs_ref, acc_ref, send_refs, keep_ref):
-    shard = lax.axis_index("shard")
-    block = keep_ref.shape[0]
+def products(flip, start, ht_a, ht_b, operands, lhs_ref, acc_ref):
+    shard = lax.axis_index("shard") ^ flip
+    block = acc_ref.shape[0] // 2
     rank = ht_a.shape[0] // 3
     rows_a = ht_a.shape[1]
     core = lax.rem(shard, 2)
-    first = (group * 4 + (lax.rem(shard, 4) - core)) * block
+    first = (shard - core) * block
     picked = pl.ds(pl.multiple_of(first, 2 * block), 2 * block)
     lhs_ref[:, :rows_a] = ht_a[picked, :]
     lhs_ref[:, rows_a:] = ht_b[picked, :]
@@ -149,45 +149,88 @@
             inside = (at >= part * rank) & (at < (part + 1) * rank)
             lhs = jnp.where(inside, lhs_ref[...].astype(F32), 0.0).astype(BF16)
             for c in column_chunks(acc_ref.shape[1]):
-                rhs = jnp.concatenate([a_ref[:, c], b_ref[:, c]], axis=0)
-                acc_ref[:, c] += mm(lhs, rhs)
-
-    other = pl.ds(pl.multiple_of((1 - core) * block, block), block)
-    width = send_refs[0].shape[1]
-    for i, send_ref in enumerate(send_refs):
-        send_ref[...] = acc_ref[other, i * width : (i + 1) * width].astype(BF16)
-    keep_ref[...] = acc_ref[pl.ds(pl.multiple_of(core * block, block), block), :]
-
-
-def far_kernel(n_cuts, wu_ref, wo_ref, x_own, gg_own, cr_own, ht_own, bg_own, x_ref, low_ref, cr_ref, g_ref, *refs):
-    gg_ref, ht_ref, bg_ref, keep_ref = refs[:4]
-    send_refs = refs[4 : 4 + n_cuts]
-    lhs_ref, acc_ref = refs[4 + n_cuts :]
+                at_c = slice(start + c.start, start + c.stop)
+                acc_ref[:, c] += mm(lhs, jnp.concatenate([a_ref[:, at_c], b_ref[:, at_c]], axis=0))
+
+    theirs = pl.ds(pl.multiple_of((1 - core) * block, block), block)
+    ours = pl.ds(pl.multiple_of(core * block, block), block)
+    return theirs, ours
+
+
+def bias_rows(bias):
+    high = bias.astype(BF16).astype(F32)
+    rest = bias - high
+    slabs = [slice(c, c + SLAB) for c in range(0, bias.shape[1], SLAB)]
+    filler = [jnp.zeros((1, SLAB), F32)] * (TILE - 2 * len(slabs))
+    return jnp.concatenate([high[:, c] for c in slabs] + [rest[:, c] for c in slabs] + filler, axis=0)
+
+
+def bias_of(rows, n_slabs):
+    return jnp.concatenate([rows[j : j + 1] + rows[n_slabs + j : n_slabs + j + 1] for j in range(n_slabs)], axis=1)
+
+
+def backward_other_kernel(wu_ref, wo_ref, bg_own, x_ref, low_ref, g_ref, gg_ref, ht_ref, bg_ref):
     backward_rows(x_ref, g_ref[...], low_ref, wu_ref, wo_ref, gg_ref, bg_ref, ht_ref, None, None)
     bg_ref[...] = bg_own[...] + bg_ref[...]
-    group = 1 - lax.div(lax.axis_index("shard"), 4)
-    operands = ((x_own, x_ref), (gg_own, gg_ref), (cr_own, cr_ref))
-    products(group, ht_own, ht_ref, operands, lhs_ref, acc_ref, send_refs, keep_ref)
-
-
-def near_kernel(x_own, gg_own, cr_own, ht_own, x_ref, gg_ref, cr_ref, ht_ref, send_ref, keep_ref, lhs_ref, acc_ref):
-    group = lax.div(lax.axis_index("shard"), 4)
-    operands = ((x_own, x_ref), (gg_own, gg_ref), (cr_own, cr_ref))
-    products(group, ht_own, ht_ref, operands, lhs_ref, acc_ref, [send_ref], keep_ref)
-
-
-def round_kernel(at, keep_ref, recv_ref, out_ref):
-    width = out_ref.shape[1]
-    out_ref[...] = (keep_ref[:, at * width : (at + 1) * width] + recv_ref[...].astype(F32)).astype(BF16)
-
-
-def final_kernel(scale, keep_ref, near_ref, bias_ref, bias_far_ref, *refs):
-    fars, out_ref, bg_ref = refs[:-2], refs[-2], refs[-1]
-    bg_ref[...] = bias_ref[...] + bias_far_ref[...]
-    width = fars[0].shape[1]
-    for i, far in enumerate(fars):
-        c = slice(i * width, (i + 1) * width)
-        out_ref[:, c] = ((keep_ref[:, c] + near_ref[:, c].astype(F32)) + far[...].astype(F32)) * scale
+
+
+def far_sums(flip, start, own, other, bg_ref, send_ref, keep_ref, lhs_ref, acc_ref):
+    theirs, ours = products(flip, start, own[3], other[3], list(zip(own[:3], other[:3])), lhs_ref, acc_ref)
+    block, width = acc_ref.shape[0] // 2, acc_ref.shape[1]
+    for j in range(width // SLAB):
+        c, rows = slice(j * SLAB, (j + 1) * SLAB), slice(j * block, (j + 1) * block)
+        send_ref[rows, :] = acc_ref[theirs, c].astype(BF16)
+        keep_ref[rows, :] = acc_ref[ours, c]
+    rows = bias_rows(bg_ref[:, start : start + width])
+    send_ref[-TILE:, :] = rows.astype(BF16)
+    keep_ref[-TILE:, :] = rows.astype(BF16).astype(F32)
+
+
+def far_more_kernel(flip, start, *refs):
+    far_sums(flip, start, refs[:4], refs[4:8], *refs[8:])
+
+
+def far_kernel(flip, wu_ref, wo_ref, bg_own, x_own, gg_own, cr_own, ht_own, x_ref, low_ref, cr_ref, g_ref, *refs):
+    gg_ref, ht_ref, bg_ref = refs[:3]
+    backward_other_kernel(wu_ref, wo_ref, bg_own, x_ref, low_ref, g_ref, gg_ref, ht_ref, bg_ref)
+    far_sums(flip, 0, (x_own, gg_own, cr_own, ht_own), (x_ref, gg_ref, cr_ref, ht_ref), bg_ref, *refs[3:])
+
+
+def near_kernel(*refs):
+    own, other = refs[:4], refs[4:8]
+    send_ref, keep_ref, lhs_ref, acc_ref = refs[8:]
+    theirs, ours = products(0, 0, own[3], other[3], list(zip(own[:3], other[:3])), lhs_ref, acc_ref)
+    send_ref[...] = acc_ref[theirs, :].astype(BF16)
+    keep_ref[...] = acc_ref[ours, :]
+
+
+def round_kernel(n_slabs, keep_ref, recv_ref, out_ref):
+    out_ref[:-TILE, :] = (keep_ref[:-TILE, :] + recv_ref[:-TILE, :].astype(F32)).astype(BF16)
+    rows = keep_ref[-TILE:, :] + recv_ref[-TILE:, :].astype(F32)
+    out_ref[-TILE:, :] = bias_rows(bias_of(rows, n_slabs)).astype(BF16)
+
+
+def final_kernel(scale, start, keep_ref, near_ref, sent_ref, far_ref, *refs):
+    out_ref, bg_out, total_ref, bg_ref, sem_ref = refs[-5:]
+    block, width = total_ref.shape
+    n_slabs = width // SLAB
+    copies = []
+
+    def write(source, target, i):
+        copies.append(pltpu.make_async_copy(source, target, sem_ref.at[i]))
+        copies[-1].start()
+
+    for j in range(n_slabs):
+        w = slice(start + j * SLAB, start + (j + 1) * SLAB)
+        total = keep_ref[:, w] + near_ref[:, w].astype(F32)
+        total = total + far_ref[j * block : (j + 1) * block, :].astype(F32)
+        total_ref[:, j * SLAB : (j + 1) * SLAB] = total * scale
+        write(total_ref.at[:, pl.ds(j * SLAB, SLAB)], out_ref.at[:, pl.ds(w.start, SLAB)], j)
+    ours, theirs = sent_ref[-TILE:, :].astype(F32), far_ref[-TILE:, :].astype(F32)
+    bg_ref[...] = bias_of(ours, n_slabs) + bias_of(theirs, n_slabs)
+    write(bg_ref, bg_out.at[:, pl.ds(start, width)], n_slabs)
+    for copy in copies:
+        copy.wait()
 
 
 def place_kernel(n_tower, assign_ref, *refs):
@@ -217,8 +260,8 @@
     stack = 2 * rank + out
     block = stack // n_shard
     top_rows = out_grad.shape[0]
-    n_cuts = 1
-    cut = width // n_cuts
+    cuts = (0, width // 2, width)
+    n_cuts = len(cuts) - 1
     wide = sds((n, width), BF16)
     tall = sds((stack, n), BF16)
     low = sds((n, rank), BF16)
@@ -235,7 +278,7 @@
         [HBM],
         [out_grad],
         "cut_columns",
-        60 * MIB,
+        48 * MIB,
         1,
     )
     pieces = [pieces[0]] + [across(pieces[k], "tower", k) for k in range(1, n_tower)]
@@ -259,54 +302,78 @@
         cost=1,
     )
     g_other = across(g_own, "shard", 2)
+    low_other, cr_other = call(
+        forward_rows,
+        [low, wide],
+        [],
+        [VMEM] * 4,
+        [x_other, wd, wu, cross_bias],
+        "forward_other",
+    )
+
+    def slab_outs(cut):
+        shape = (block * cut // SLAB + TILE, SLAB)
+        return [sds(shape, BF16), sds(shape, F32)]
+
+    def sum_scratch(cut):
+        return [pltpu.VMEM((2 * block, 2 * n), BF16), pltpu.VMEM((2 * block, cut), F32)]
+
+    own = [x_own, gg_own, cr_own, ht_own]
+    gg_other, ht_other, bias_sum, *far = call(
+        functools.partial(far_kernel, FAR),
+        [wide, tall, row] + slab_outs(cuts[1]),
+        sum_scratch(cuts[1]),
+        [VMEM] * 11,
+        [wu, wo, bg_own, *own, x_other, low_other, cr_other, g_other],
+        "far_sums",
+    )
+    other = [x_other, gg_other, cr_other, ht_other]
+    far_parts = [far]
+    for i in range(1, n_cuts):
+        far_parts.append(
+            call(
+                functools.partial(far_more_kernel, FAR, cuts[i]),
+                slab_outs(cuts[i + 1] - cuts[i]),
+                sum_scratch(cuts[i + 1] - cuts[i]),
+                [VMEM] * 9,
+                [*own, *other, bias_sum],
+                "far_sums_more",
+            )
+        )
+    rounded, fars = [], []
+    for i, (send, keep) in enumerate(far_parts):
+        rounded += call(
+            functools.partial(round_kernel, (cuts[i + 1] - cuts[i]) // SLAB),
+            [sds(send.shape, BF16)],
+            [],
+            [VMEM] * 2,
+            [keep, across(send, "shard", 1)],
+            "far_round",
+            cost=1,
+        )
+        fars.append(across(rounded[-1], "shard", FAR))
+    (near_send, near_keep) = call(
+        near_kernel,
+        [sds((block, width), BF16), sds((block, width), F32)],
+        sum_scratch(width),
+        [VMEM] * 8,
+        [*own, *other[:3], after(ht_other, *rounded)],
+        "near_sums",
+        cost=1,
+    )
+    near_other = across(near_send, "shard", 1)
     grad_inputs = call(
         functools.partial(inputs_kernel, n_tower),
         [sds((top_rows, width), BF16)] * n_tower,
         [pltpu.VMEM((n, width), BF16)],
         [VMEM] * 3,
-        [wd, gh_own, direct],
+        [wd, gh_own, after(direct, *rounded)],
         "grad_inputs",
     )
-    returned = [grad_inputs[0]] + [across(grad_inputs[k], "tower", k) for k in range(1, n_tower)]
-    low_other, cr_other = call(
-        forward_other_kernel,
-        [low, wide],
-        [],
-        [VMEM] * 4,
-        [wd, wu, cross_bias, x_other],
-        "forward_other",
-    )
-    gg_other, ht_other, bias_sum, far_keep, *far_sends = call(
-        functools.partial(far_kernel, n_cuts),
-        [wide, tall, row, sds((block, width), F32)] + [sds((block, cut), BF16)] * n_cuts,
-        [pltpu.VMEM((2 * block, 2 * n), BF16), pltpu.VMEM((2 * block, width), F32)],
-        [VMEM] * 11,
-        [wu, wo, x_own, gg_own, cr_own, ht_own, bg_own, x_other, low_other, cr_other, g_other],
-        "far_sums",
-    )
-    fars = []
-    for i, send in enumerate(far_sends):
-        (far,) = call(
-            functools.partial(round_kernel, i),
-            [sds((block, cut), BF16)],
-            [],
-            [VMEM] * 2,
-            [far_keep, across(send, "shard", 1)],
-            "far_round",
-            cost=1,
-        )
-        fars.append(across(far, "shard", 4))
-    near_send, near_keep = call(
-        near_kernel,
-        [sds((block, width), BF16), sds((block, width), F32)],
-        [pltpu.VMEM((2 * block, 2 * n), BF16), pltpu.VMEM((2 * block, width), F32)],
-        [VMEM] * 8,
-        [x_own, gg_own, cr_own, ht_own, x_other, gg_other, cr_other, after(ht_other, far)],
-        "near_sums",
-    )
-    near_other = across(near_send, "shard", 1)
-    bias_sum = bias_sum + across(bias_sum, "shard", 1)
-    bias_far = across(bias_sum, "shard", 4)
+    returned = [grad_inputs[0]]
+    for k in range(1, n_tower):
+        piece = grad_inputs[k]
+        returned.append(across(piece, "tower", k))
     (feature_grad,) = call(
         functools.partial(place_kernel, n_tower),
         [sds((top_rows, n_tower * width), BF16)],
@@ -316,14 +383,24 @@
         "place_features",
         cost=1,
     )
-    weight_grad, bias_grad = call(
-        functools.partial(final_kernel, 1.0 / math.sqrt(n * n_shard)),
-        [sds((block, width), F32), row],
-        [],
-        [VMEM] * (4 + n_cuts),
-        [near_keep, near_other, bias_sum, bias_far, *fars],
-        "add_up",
-    )
+    results = []
+    for i, far in enumerate(fars):
+        cut = cuts[i + 1] - cuts[i]
+        results = call(
+            functools.partial(final_kernel, 1.0 / math.sqrt(n * n_shard), cuts[i]),
+            [sds((block, width), F32), row],
+            [
+                pltpu.VMEM((block, cut), F32),
+                pltpu.VMEM((1, cut), F32),
+                pltpu.SemaphoreType.DMA((cut // SLAB + 1,)),
+            ],
+            [VMEM] * 4 + [HBM] * len(results),
+            [near_keep, near_other, rounded[i], far, *results],
+            "add_up",
+            out_space=HBM,
+            aliases={4 + j: j for j in range(len(results))},
+        )
+    weight_grad, bias_grad = results
     return feature_grad, weight_grad[None], bias_grad
 
 

time: 44.5 us -> 41 us (0.921)
  waiting for transfers between devices: 16.6 us -> 12.6 us
  Pallas kernels: 11.1 us -> 10.2 us
  local copies, waits for them, and re-layouts: 1.06 us -> 1.89 us
  starting transfers between devices: 14.7 us -> 15.3 us
    ppermute x13, waiting for transfers between devices: 16.6 us -> 12.6 us  [across(): return lax.ppermute(value, axis, xor_pairs(lax.axis_size(axis), k))]
    pallas_call x10 -> x13, Pallas kernels: 11.1 us -> 10.2 us  [call(): pl.pallas_call(kernel, out_shape=outs, in_specs=[pl.BlockSpec(memory_spac...]
    unnamed x8, local copies, waits for them, and re-layouts: 1.06 us -> 1.89 us
    ppermute x13, starting transfers between devices: 14.7 us -> 15.3 us  [across(): return lax.ppermute(value, axis, xor_pairs(lax.axis_size(axis), k))]
  transfers between devices with their start and end apart: 13 -> 13, of which waited for: 7 -> 7; matrix products, arithmetic and copies ran while one was open for 0% -> 0% of each run, Pallas kernels for 18% -> 19%
where the time goes in v3:
time: 41 us; the launch traced here: 40.8 us
  starting transfers between devices  15.3 us (37%)
  waiting for transfers between devices  12.6 us (31%)
  Pallas kernels  10.2 us (25%)
  local copies, waits for them, and re-layouts  1.89 us (5%)
  between operations  0.76 us (2%)
    ppermute x13, starting transfers between devices, across(): return lax.ppermute(value, axis, xor_pairs(lax.axis_size(axis), k))  15.3 us
    ppermute x13, waiting for transfers between devices, across(): return lax.ppermute(value, axis, xor_pairs(lax.axis_size(axis), k))  12.6 us
    pallas_call x13, Pallas kernels, call(): pl.pallas_call(kernel, out_shape=outs, in_specs=[pl.BlockSpec(memory_spac...  10.2 us
    unnamed x8, local copies, waits for them, and re-layouts  1.89 us
  transfers between devices with their start and end apart: 13, of which 7 were waited for; matrix products, arithmetic and copies ran while one was open for 0% of the time, Pallas kernels for 19%

profile of v3, /device:TPU:0, one launch (start us, length us, event | category | flops | bytes accessed | tf_op | source)
XLA Modules:
  0.0 40.8 jit_solution(12440570336149487801)
XLA Ops:
  0.6 3.1 %collective-permute-start.3 = (bf16[128,2048]{1,0:T(8,128)(2,1)}, bf16[128,2048]{1,0:T(8,128)(2,1)S(1)}, u32[]{:S(2)}, u32[]{:S(2)}) collective-permute-start(bf16[128,2048]{1,0:T(8,128)(2,1)} %bitcast.5), channel_id=1, source_target_pairs={{0,2},{1,3},{2,0},{3,1},{4,6},{5,7},{6,4},{7,5},{8,10},{9,11},{10,... | collective-permute-start | bytes 1572872 | tf_op jit(solution)/shard_map/ppermute | solution.py:271
  3.7 0.8 %copy-done.1 = bf16[32,1024]{1,0:T(8,128)(2,1)S(1)} copy-done((bf16[32,1024]{1,0:T(8,128)(2,1)S(1)}, bf16[32,1024]{1,0:T(8,128)(2,1)}, u32[]{:S(2)}) %copy-start.1) | copy-done | bytes 65560
  4.6 1.6 %collective-permute-start = (bf16[32,256]{1,0:T(8,128)(2,1)S(1)}, bf16[32,256]{1,0:T(8,128)(2,1)S(1)}, u32[]{:S(2)}, u32[]{:S(2)}) collective-permute-start(bf16[32,256]{1,0:T(8,128)(2,1)S(1)} %get-tuple-element.48), channel_id=1, source_target_pairs={{0,8},{8,0},{16,24},{24,16},{1,9},{9,1},{17,25},{25,17},{2,10},{10... | collective-permute-start | bytes 49160 | tf_op jit(solution)/shard_map/ppermute | solution.py:271
  6.2 1.5 %collective-permute-start.1 = (bf16[32,256]{1,0:T(8,128)(2,1)S(1)}, bf16[32,256]{1,0:T(8,128)(2,1)S(1)}, u32[]{:S(2)}, u32[]{:S(2)}) collective-permute-start(bf16[32,256]{1,0:T(8,128)(2,1)S(1)} %get-tuple-element.49), channel_id=1, source_target_pairs={{0,16},{8,24},{16,0},{24,8},{1,17},{9,25},{17,1},{25,9},{2,18},{10... | collective-permute-start | bytes 49160 | tf_op jit(solution)/shard_map/ppermute | solution.py:271
  7.7 0.5 %collective-permute-start.2 = (bf16[32,256]{1,0:T(8,128)(2,1)S(1)}, bf16[32,256]{1,0:T(8,128)(2,1)S(1)}, u32[]{:S(2)}, u32[]{:S(2)}) collective-permute-start(bf16[32,256]{1,0:T(8,128)(2,1)S(1)} %get-tuple-element.50), channel_id=1, source_target_pairs={{0,24},{8,16},{16,8},{24,0},{1,25},{9,17},{17,9},{25,1},{2,26},{10... | collective-permute-start | bytes 49160 | tf_op jit(solution)/shard_map/ppermute | solution.py:271
  8.2 1.0 %copy-done = bf16[1,128,2048]{2,1,0:T(8,128)(2,1)S(1)} copy-done((bf16[1,128,2048]{2,1,0:T(8,128)(2,1)S(1)}, bf16[1,128,2048]{2,1,0:T(8,128)(2,1)}, u32[]{:S(2)}) %copy-start) | copy-done | bytes 524312
  9.2 2.1 %forward_own.1 = (bf16[2048,256]{1,0:T(8,128)(2,1)S(1)}, bf16[256,2048]{1,0:T(8,128)(2,1)S(1)}, bf16[2048,256]{1,0:T(8,128)(2,1)S(1)}, bf16[128,2048]{1,0:T(8,12...) custom-call(bf16[2048,256]{1,0:T(8,128)(2,1)} %bitcast.7, ...), custom_call_target="tpu_custom_call" | custom-call | flops 1 | bytes 1 | tf_op jit(solution)/shard_map/forward_own/pallas_call | solution.py:33
  11.4 0.9 %collective-permute-done.2.refs_3_ = bf16[32,256]{1,0:T(8,128)(2,1)S(1)} collective-permute-done((bf16[32,256]{1,0:T(8,128)(2,1)S(1)}, bf16[32,256]{1,0:T(8,128)(2,1)S(1)}, u32[]{:S(2)}, u32[]{:S(2)}) %collective-permute-start.2) | collective-permute-done | bytes 16416 | tf_op jit(solution)/shard_map/ppermute | solution.py:271
  12.3 1.1 %backward_own.1 = (bf16[128,256]{1,0:T(8,128)(2,1)S(1)}, bf16[128,256]{1,0:T(8,128)(2,1)S(1)}, bf16[768,128]{1,0:T(8,128)(2,1)S(1)}, bf16[128,2048]{1,0:T(8,128)...) custom-call(bf16[256,2048]{1,0:T(8,128)(2,1)S(1)} %get-tuple-element.42.wu_ref, ...), custom_call_target="tpu_custom_call" | custom-call | flops 1 | bytes 1 | tf_op jit(solution)/shard_map/backward_own/pallas_call | solution.py:33
  13.4 0.5 %collective-permute-start.4 = (bf16[128,256]{1,0:T(8,128)(2,1)S(1)}, bf16[128,256]{1,0:T(8,128)(2,1)S(1)}, u32[]{:S(2)}, u32[]{:S(2)}) collective-permute-start(bf16[128,256]{1,0:T(8,128)(2,1)S(1)} %get-tuple-element.59), channel_id=1, source_target_pairs={{0,2},{1,3},{2,0},{3,1},{4,6},{5,7},{6,4},{7,5},{8,10},{9,11},{10,... | collective-permute-start | bytes 196616 | tf_op jit(solution)/shard_map/ppermute | solution.py:271
  13.9 2.6 %collective-permute-done.3.x_ref.refs_4_ = bf16[128,2048]{1,0:T(8,128)(2,1)S(1)} collective-permute-done((bf16[128,2048]{1,0:T(8,128)(2,1)}, bf16[128,2048]{1,0:T(8,128)(2,1)S(1)}, u32[]{:S(2)}, u32[]{:S(2)}) %collective-permute-start.3) | collective-permute-done | bytes 524320 | tf_op jit(solution)/shard_map/ppermute | solution.py:271
  16.6 0.8 %forward_other.1 = (bf16[128,256]{1,0:T(8,128)(2,1)S(1)}, bf16[128,2048]{1,0:T(8,128)(2,1)S(1)}) custom-call(bf16[128,2048]{1,0:T(8,128)(2,1)S(1)} %collective-permute-done.3.x_ref.refs_4_, bf16[2048,256]{1,0:T(8,128)(2,1)S(1)} %get-tuple-element.41.wd_ref, bf16[256,2048]{1,0:T(8,128)(2,1)S(1)} %get-tuple-element.42.wu_ref, f32[1,2048]{1,0:T(1,128)S(1)} %copy-done.2), custom_call_target="tpu_custom_call" | custom-call | flops 10000000000 | bytes 1 | tf_op jit(solution)/shard_map/forward_other/pallas_call | solution.py:33
  17.3 0.4 %collective-permute-done.4.g_ref = bf16[128,256]{1,0:T(8,128)(2,1)S(1)} collective-permute-done((bf16[128,256]{1,0:T(8,128)(2,1)S(1)}, bf16[128,256]{1,0:T(8,128)(2,1)S(1)}, u32[]{:S(2)}, u32[]{:S(2)}) %collective-permute-start.4) | collective-permute-done | bytes 65568 | tf_op jit(solution)/shard_map/ppermute | solution.py:271
  17.8 1.4 %far_sums.1 = (bf16[128,2048]{1,0:T(8,128)(2,1)S(1)}, bf16[768,128]{1,0:T(8,128)(2,1)S(1)}, f32[1,2048]{1,0:T(1,128)S(1)}, bf16[400,256]{1,0:T(8,128)(2,1)S(1)}, f32[400,256]{1,0:T(8,128)S(1)}) custom-call(bf16[256,2048]{1,0:T(8,128)(2,1)S(1)} %get-tuple-element.42.wu_ref, bf16[2048,256]{1,0:T(8,128)(2,1)S(1)} %get-tuple-element.43.wo_ref, ...), custom_call_target="tpu_custom_call" | custom-call | flops 10000000000 | bytes 1 | tf_op jit(solution)/shard_map/far_sums/pallas_call | solution.py:33
  19.2 0.1 collective-permute-start.5
  19.3 0.4 far_sums_more.1
  19.7 0.6 %collective-permute-start.6 = (bf16[400,256]{1,0:T(8,128)(2,1)S(1)}, bf16[400,256]{1,0:T(8,128)(2,1)S(1)}, u32[]{:S(2)}, u32[]{:S(2)}) collective-permute-start(bf16[400,256]{1,0:T(8,128)(2,1)S(1)} %get-tuple-element.66), channel_id=1, source_target_pairs={{0,1},{1,0},{2,3},{3,2},{4,5},{5,4},{6,7},{7,6},{8,9},{9,8},{10,11... | collective-permute-start | bytes 614408 | tf_op jit(solution)/shard_map/ppermute | solution.py:271
  20.2 0.5 %collective-permute-done.5.recv_ref = bf16[400,256]{1,0:T(8,128)(2,1)S(1)} collective-permute-done((bf16[400,256]{1,0:T(8,128)(2,1)S(1)}, bf16[400,256]{1,0:T(8,128)(2,1)S(1)}, u32[]{:S(2)}, u32[]{:S(2)}) %collective-permute-start.5) | collective-permute-done | bytes 204832 | tf_op jit(solution)/shard_map/ppermute | solution.py:271
  20.7 3.4 %collective-permute-start.12 = (bf16[400,256]{1,0:T(8,128)(2,1)S(1)}, bf16[400,256]{1,0:T(8,128)(2,1)S(1)}, u32[]{:S(2)}, u32[]{:S(2)}) collective-permute-start(bf16[400,256]{1,0:T(8,128)(2,1)S(1)} %far_round.2.sent_ref), channel_id=1, source_target_pairs={{0,6},{1,7},{2,4},{3,5},{4,2},{5,3},{6,0},{7,1},{8,14},{9,15},{10,... | collective-permute-start | bytes 614408 | tf_op jit(solution)/shard_map/ppermute | solution.py:271
  24.2 0.6 %near_sums.1 = (bf16[96,2048]{1,0:T(8,128)(2,1)S(1)}, f32[96,2048]{1,0:T(8,128)S(1)}) custom-call(bf16[128,2048]{1,0:T(8,128)(2,1)S(1)} %get-tuple-element.44.x_ref.x_own.refs_0_, bf16[128,2048]{1,0:T(8,128)(2,1)S(1)} %get-tuple-element.54.gg_own.refs_1_, bf16[128,2048]{1,0:T(8,128)(2,1)S(1)} %get-tuple-element.55.cr_own.refs_2_, ...), custom_call_target="tpu_custom_call" | custom-call | flops 1 | bytes 1 | tf_op jit(solution)/shard_map/near_sums/pallas_call | solution.py:33
  24.8 0.1 collective-permute-start.10
  24.9 0.5 %grad_inputs.1 = (bf16[32,2048]{1,0:T(8,128)(2,1)S(1)}, bf16[32,2048]{1,0:T(8,128)(2,1)S(1)}, bf16[32,2048]{1,0:T(8,128)(2,1)S(1)}, bf16[32,2048]{1,0:T(8,128)(2,1)S(1)}) custom-call(bf16[2048,256]{1,0:T(8,128)(2,1)S(1)} %get-tuple-element.41.wd_ref, bf16[128,256]{1,0:T(8,128)(2,1)S(1)} %get-tuple-element.51.gh_ref, f32[128,2048]{1,0:T(8,128)S(1)} %get-tuple-element.67.direct_ref), custom_call_target="tpu_custom_call" | custom-call | flops 10000000000 | bytes 1 | tf_op jit(solution)/shard_map/grad_inputs/pallas_call | solution.py:33
  25.4 1.6 %collective-permute-start.7 = (bf16[32,2048]{1,0:T(8,128)(2,1)S(1)}, bf16[32,2048]{1,0:T(8,128)(2,1)S(1)}, u32[]{:S(2)}, u32[]{:S(2)}) collective-permute-start(bf16[32,2048]{1,0:T(8,128)(2,1)S(1)} %get-tuple-element.69), channel_id=1, source_target_pairs={{0,8},{8,0},{16,24},{24,16},{1,9},{9,1},{17,25},{25,17},{2,10},{10... | collective-permute-start | bytes 393224 | tf_op jit(solution)/shard_map/ppermute | solution.py:271
  27.0 1.5 %collective-permute-start.8 = (bf16[32,2048]{1,0:T(8,128)(2,1)S(1)}, bf16[32,2048]{1,0:T(8,128)(2,1)S(1)}, u32[]{:S(2)}, u32[]{:S(2)}) collective-permute-start(bf16[32,2048]{1,0:T(8,128)(2,1)S(1)} %get-tuple-element.70), channel_id=1, source_target_pairs={{0,16},{8,24},{16,0},{24,8},{1,17},{9,25},{17,1},{25,9},{2,18},{10... | collective-permute-start | bytes 393224 | tf_op jit(solution)/shard_map/ppermute | solution.py:271
  28.5 0.5 %collective-permute-start.9 = (bf16[32,2048]{1,0:T(8,128)(2,1)S(1)}, bf16[32,2048]{1,0:T(8,128)(2,1)S(1)}, u32[]{:S(2)}, u32[]{:S(2)}) collective-permute-start(bf16[32,2048]{1,0:T(8,128)(2,1)S(1)} %get-tuple-element.71), channel_id=1, source_target_pairs={{0,24},{8,16},{16,8},{24,0},{1,25},{9,17},{17,9},{25,1},{2,26},{10... | collective-permute-start | bytes 393224 | tf_op jit(solution)/shard_map/ppermute | solution.py:271
  29.0 2.7 %collective-permute-done.7.refs_1_ = bf16[32,2048]{1,0:T(8,128)(2,1)S(1)} collective-permute-done((bf16[32,2048]{1,0:T(8,128)(2,1)S(1)}, bf16[32,2048]{1,0:T(8,128)(2,1)S(1)}, u32[]{:S(2)}, u32[]{:S(2)}) %collective-permute-start.7) | collective-permute-done | bytes 131104 | tf_op jit(solution)/shard_map/ppermute | solution.py:271
  31.7 0.5 %collective-permute-start.11 = (bf16[400,256]{1,0:T(8,128)(2,1)S(1)}, bf16[400,256]{1,0:T(8,128)(2,1)S(1)}, u32[]{:S(2)}, u32[]{:S(2)}) collective-permute-start(bf16[400,256]{1,0:T(8,128)(2,1)S(1)} %far_round.3.sent_ref), channel_id=1, source_target_pairs={{0,6},{1,7},{2,4},{3,5},{4,2},{5,3},{6,0},{7,1},{8,14},{9,15},{10,... | collective-permute-start | bytes 614408 | tf_op jit(solution)/shard_map/ppermute | solution.py:271
  32.2 3.2 %collective-permute-done.8.refs_2_ = bf16[32,2048]{1,0:T(8,128)(2,1)S(1)} collective-permute-done((bf16[32,2048]{1,0:T(8,128)(2,1)S(1)}, bf16[32,2048]{1,0:T(8,128)(2,1)S(1)}, u32[]{:S(2)}, u32[]{:S(2)}) %collective-permute-start.8) | collective-permute-done | bytes 131104 | tf_op jit(solution)/shard_map/ppermute | solution.py:271
  35.4 1.5 %place_features.1 = bf16[32,8192]{1,0:T(8,128)(2,1)} custom-call(s32[64]{0:T(128)S(1)} %copy-done.3, bf16[32,2048]{1,0:T(8,128)(2,1)S(1)} %get-tuple-element.68.refs_0_, bf16[32,2048]{1,0:T(8,128)(2,1)S(1)} %collective-permute-done.7.refs_1_, bf16[32,2048]{1,0:T(8,128)(2,1)S(1)} %collective-permute-done.8.refs_2_, ...), custom_call_target="tpu_custom_call" | custom-call | flops 1 | bytes 1 | tf_op jit(solution)/shard_map/place_features/pallas_call | solution.py:33
  36.9 0.8 %add_up.2 = (f32[96,2048]{1,0:T(8,128)}, f32[1,2048]{1,0:T(1,128)}) custom-call(f32[96,2048]{1,0:T(8,128)S(1)} %get-tuple-element.73.keep_ref, bf16[96,2048]{1,0:T(8,128)(2,1)S(1)} %collective-permute-done.10.near_ref, bf16[400,256]{1,0:T(8,128)(2,1)S(1)} %far_round.2.sent_ref, bf16[400,256]{1,0:T(8,128)(2,1)S(1)} %collective-permute-done.12.far_ref), custom_call_target="tpu_custom_call" | custom-call | flops 10000000000 | bytes 1 | tf_op jit(solution)/shard_map/add_up/pallas_call | solution.py:33
  37.7 2.2 %collective-permute-done.11.far_ref = bf16[400,256]{1,0:T(8,128)(2,1)S(1)} collective-permute-done((bf16[400,256]{1,0:T(8,128)(2,1)S(1)}, bf16[400,256]{1,0:T(8,128)(2,1)S(1)}, u32[]{:S(2)}, u32[]{:S(2)}) %collective-permute-start.11) | collective-permute-done | bytes 204832 | tf_op jit(solution)/shard_map/ppermute | solution.py:271
  40.0 0.8 %add_up.3 = (f32[96,2048]{1,0:T(8,128)}, f32[1,2048]{1,0:T(1,128)}) custom-call(f32[96,2048]{1,0:T(8,128)S(1)} %get-tuple-element.73.keep_ref, bf16[96,2048]{1,0:T(8,128)(2,1)S(1)} %collective-permute-done.10.near_ref, bf16[400,256]{1,0:T(8,128)(2,1)S(1)} %far_round.3.sent_ref, ...), custom_call_target="tpu_custom_call", output_to_operand_aliasing={{0}: (4, {}), {1}: (5, {})} | custom-call | flops 10000000000 | bytes 1 | tf_op jit(solution)/shard_map/add_up/pallas_call | solution.py:33
  (15 shorter events, 0.2 us)
Async XLA Ops:
  0.6 15.9 %collective-permute-start.3 = (bf16[128,2048]{1,0:T(8,128)(2,1)}, bf16[128,2048]{1,0:T(8,128)(2,1)S(1)}, u32[]{:S(2)}, u32[]{:S(2)}) collective-permute-start(bf16[128,2048]{1,0:T(8,128)(2,1)} %bitcast.5), channel_id=1, source_target_pairs={{0,2},{1,3},{2,0},{3,1},{4,6},{5,7},{6,4},{7,5},{8,10},{9,11},{10,... | collective-permute-start | bytes 1572872 | tf_op jit(solution)/shard_map/ppermute | solution.py:271
  3.7 0.8 %copy-start.1 = (bf16[32,1024]{1,0:T(8,128)(2,1)S(1)}, bf16[32,1024]{1,0:T(8,128)(2,1)}, u32[]{:S(2)}) copy-start(bf16[32,1024]{1,0:T(8,128)(2,1)} %grad_ref.1) | copy-start | bytes 196612
  4.6 3.6 %copy-start.2 = (f32[1,2048]{1,0:T(1,128)S(1)}, f32[1,2048]{1,0:T(1,128)}, u32[]{:S(2)}) copy-start(f32[1,2048]{1,0:T(1,128)} %bias_ref.3) | copy-start | bytes 24580
  4.6 6.8 %collective-permute-start = (bf16[32,256]{1,0:T(8,128)(2,1)S(1)}, bf16[32,256]{1,0:T(8,128)(2,1)S(1)}, u32[]{:S(2)}, u32[]{:S(2)}) collective-permute-start(bf16[32,256]{1,0:T(8,128)(2,1)S(1)} %get-tuple-element.48), channel_id=1, source_target_pairs={{0,8},{8,0},{16,24},{24,16},{1,9},{9,1},{17,25},{25,17},{2,10},{10... | collective-permute-start | bytes 49160 | tf_op jit(solution)/shard_map/ppermute | solution.py:271
  6.2 5.2 %collective-permute-start.1 = (bf16[32,256]{1,0:T(8,128)(2,1)S(1)}, bf16[32,256]{1,0:T(8,128)(2,1)S(1)}, u32[]{:S(2)}, u32[]{:S(2)}) collective-permute-start(bf16[32,256]{1,0:T(8,128)(2,1)S(1)} %get-tuple-element.49), channel_id=1, source_target_pairs={{0,16},{8,24},{16,0},{24,8},{1,17},{9,25},{17,1},{25,9},{2,18},{10... | collective-permute-start | bytes 49160 | tf_op jit(solution)/shard_map/ppermute | solution.py:271
  7.7 4.6 %collective-permute-start.2 = (bf16[32,256]{1,0:T(8,128)(2,1)S(1)}, bf16[32,256]{1,0:T(8,128)(2,1)S(1)}, u32[]{:S(2)}, u32[]{:S(2)}) collective-permute-start(bf16[32,256]{1,0:T(8,128)(2,1)S(1)} %get-tuple-element.50), channel_id=1, source_target_pairs={{0,24},{8,16},{16,8},{24,0},{1,25},{9,17},{17,9},{25,1},{2,26},{10... | collective-permute-start | bytes 49160 | tf_op jit(solution)/shard_map/ppermute | solution.py:271
  8.2 1.0 %copy-start = (bf16[1,128,2048]{2,1,0:T(8,128)(2,1)S(1)}, bf16[1,128,2048]{2,1,0:T(8,128)(2,1)}, u32[]{:S(2)}) copy-start(bf16[1,128,2048]{2,1,0:T(8,128)(2,1)} %param.8) | copy-start | bytes 1572868
  13.4 4.3 %collective-permute-start.4 = (bf16[128,256]{1,0:T(8,128)(2,1)S(1)}, bf16[128,256]{1,0:T(8,128)(2,1)S(1)}, u32[]{:S(2)}, u32[]{:S(2)}) collective-permute-start(bf16[128,256]{1,0:T(8,128)(2,1)S(1)} %get-tuple-element.59), channel_id=1, source_target_pairs={{0,2},{1,3},{2,0},{3,1},{4,6},{5,7},{6,4},{7,5},{8,10},{9,11},{10,... | collective-permute-start | bytes 196616 | tf_op jit(solution)/shard_map/ppermute | solution.py:271
  19.2 1.5 %collective-permute-start.5 = (bf16[400,256]{1,0:T(8,128)(2,1)S(1)}, bf16[400,256]{1,0:T(8,128)(2,1)S(1)}, u32[]{:S(2)}, u32[]{:S(2)}) collective-permute-start(bf16[400,256]{1,0:T(8,128)(2,1)S(1)} %get-tuple-element.61), channel_id=1, source_target_pairs={{0,1},{1,0},{2,3},{3,2},{4,5},{5,4},{6,7},{7,6},{8,9},{9,8},{10,11... | collective-permute-start | bytes 614408 | tf_op jit(solution)/shard_map/ppermute | solution.py:271
  19.7 4.5 %collective-permute-start.6 = (bf16[400,256]{1,0:T(8,128)(2,1)S(1)}, bf16[400,256]{1,0:T(8,128)(2,1)S(1)}, u32[]{:S(2)}, u32[]{:S(2)}) collective-permute-start(bf16[400,256]{1,0:T(8,128)(2,1)S(1)} %get-tuple-element.66), channel_id=1, source_target_pairs={{0,1},{1,0},{2,3},{3,2},{4,5},{5,4},{6,7},{7,6},{8,9},{9,8},{10,11... | collective-permute-start | bytes 614408 | tf_op jit(solution)/shard_map/ppermute | solution.py:271
  20.7 16.2 %collective-permute-start.12 = (bf16[400,256]{1,0:T(8,128)(2,1)S(1)}, bf16[400,256]{1,0:T(8,128)(2,1)S(1)}, u32[]{:S(2)}, u32[]{:S(2)}) collective-permute-start(bf16[400,256]{1,0:T(8,128)(2,1)S(1)} %far_round.2.sent_ref), channel_id=1, source_target_pairs={{0,6},{1,7},{2,4},{3,5},{4,2},{5,3},{6,0},{7,1},{8,14},{9,15},{10,... | collective-permute-start | bytes 614408 | tf_op jit(solution)/shard_map/ppermute | solution.py:271
  24.8 12.1 %collective-permute-start.10 = (bf16[96,2048]{1,0:T(8,128)(2,1)S(1)}, bf16[96,2048]{1,0:T(8,128)(2,1)S(1)}, u32[]{:S(2)}, u32[]{:S(2)}) collective-permute-start(bf16[96,2048]{1,0:T(8,128)(2,1)S(1)} %get-tuple-element.74), channel_id=1, source_target_pairs={{0,1},{1,0},{2,3},{3,2},{4,5},{5,4},{6,7},{7,6},{8,9},{9,8},{10,11... | collective-permute-start | bytes 1179656 | tf_op jit(solution)/shard_map/ppermute | solution.py:271
  25.4 6.3 %collective-permute-start.7 = (bf16[32,2048]{1,0:T(8,128)(2,1)S(1)}, bf16[32,2048]{1,0:T(8,128)(2,1)S(1)}, u32[]{:S(2)}, u32[]{:S(2)}) collective-permute-start(bf16[32,2048]{1,0:T(8,128)(2,1)S(1)} %get-tuple-element.69), channel_id=1, source_target_pairs={{0,8},{8,0},{16,24},{24,16},{1,9},{9,1},{17,25},{25,17},{2,10},{10... | collective-permute-start | bytes 393224 | tf_op jit(solution)/shard_map/ppermute | solution.py:271
  27.0 8.4 %collective-permute-start.8 = (bf16[32,2048]{1,0:T(8,128)(2,1)S(1)}, bf16[32,2048]{1,0:T(8,128)(2,1)S(1)}, u32[]{:S(2)}, u32[]{:S(2)}) collective-permute-start(bf16[32,2048]{1,0:T(8,128)(2,1)S(1)} %get-tuple-element.70), channel_id=1, source_target_pairs={{0,16},{8,24},{16,0},{24,8},{1,17},{9,25},{17,1},{25,9},{2,18},{10... | collective-permute-start | bytes 393224 | tf_op jit(solution)/shard_map/ppermute | solution.py:271
  28.5 6.9 %copy-start.3 = (s32[64]{0:T(128)S(1)}, s32[64]{0:T(128)}, u32[]{:S(2)}) copy-start(s32[64]{0:T(128)} %assign_ref.1) | copy-start | bytes 772
  28.5 6.9 %collective-permute-start.9 = (bf16[32,2048]{1,0:T(8,128)(2,1)S(1)}, bf16[32,2048]{1,0:T(8,128)(2,1)S(1)}, u32[]{:S(2)}, u32[]{:S(2)}) collective-permute-start(bf16[32,2048]{1,0:T(8,128)(2,1)S(1)} %get-tuple-element.71), channel_id=1, source_target_pairs={{0,24},{8,16},{16,8},{24,0},{1,25},{9,17},{17,9},{25,1},{2,26},{10... | collective-permute-start | bytes 393224 | tf_op jit(solution)/shard_map/ppermute | solution.py:271
  31.7 8.3 %collective-permute-start.11 = (bf16[400,256]{1,0:T(8,128)(2,1)S(1)}, bf16[400,256]{1,0:T(8,128)(2,1)S(1)}, u32[]{:S(2)}, u32[]{:S(2)}) collective-permute-start(bf16[400,256]{1,0:T(8,128)(2,1)S(1)} %far_round.3.sent_ref), channel_id=1, source_target_pairs={{0,6},{1,7},{2,4},{3,5},{4,2},{5,3},{6,0},{7,1},{8,14},{9,15},{10,... | collective-permute-start | bytes 614408 | tf_op jit(solution)/shard_map/ppermute | solution.py:271

commit v4 on v3

--- a/solution.py
+++ b/solution.py
@@ -14,7 +14,13 @@
 MIB = 1024 * 1024
 VM = 48
 COST = 10**10
-FAR = 6
+C1 = 1
+P2 = 2
+PN = 4
+CN = 10**9
+C2 = 10**9
+C3 = 1
+C4 = 1
 VMEM_LIMIT = 24 * MIB
 BF16 = jnp.bfloat16
 F32 = jnp.float32
@@ -77,6 +83,19 @@
         cr_ref[:, c] = (x_ref[:, c].astype(F32) * factor).astype(BF16)
         if factor_ref is not None:
             factor_ref[:, c] = factor
+
+
+def forward_inner_kernel(x_ref, wd_ref, wu_ref, bias_ref, low_ref, cr_ref):
+    outer = is_outer()
+
+    @pl.when(outer)
+    def _():
+        low_ref[...] = jnp.zeros_like(low_ref)
+        cr_ref[...] = jnp.zeros_like(cr_ref)
+
+    @pl.when(jnp.logical_not(outer))
+    def _():
+        forward_rows(x_ref, wd_ref, wu_ref, bias_ref, low_ref, cr_ref)
 
 
 def backward_rows(x_ref, g, low_ref, wu_ref, wo_ref, gg_ref, bg_ref, ht_ref, factor_ref, direct_ref):
@@ -130,18 +149,18 @@
         piece[...] = gi_ref[pl.ds(pl.multiple_of((me ^ k) * rows, rows), rows), :]
 
 
-def products(flip, start, ht_a, ht_b, operands, lhs_ref, acc_ref):
+def products(flip, start, blocks, lhs_ref, acc_ref):
     shard = lax.axis_index("shard") ^ flip
     block = acc_ref.shape[0] // 2
-    rank = ht_a.shape[0] // 3
-    rows_a = ht_a.shape[1]
+    rank = blocks[0][3].shape[0] // 3
+    n = blocks[0][3].shape[1]
     core = lax.rem(shard, 2)
     first = (shard - core) * block
     picked = pl.ds(pl.multiple_of(first, 2 * block), 2 * block)
-    lhs_ref[:, :rows_a] = ht_a[picked, :]
-    lhs_ref[:, rows_a:] = ht_b[picked, :]
+    for i, rows in enumerate(blocks):
+        lhs_ref[:, i * n : (i + 1) * n] = rows[3][picked, :]
     acc_ref[...] = jnp.zeros_like(acc_ref)
-    for part, (a_ref, b_ref) in enumerate(operands):
+    for part in range(3):
 
         @pl.when((first < (part + 1) * rank) & (first + 2 * block > part * rank))
         def _():
@@ -150,7 +169,8 @@
             lhs = jnp.where(inside, lhs_ref[...].astype(F32), 0.0).astype(BF16)
             for c in column_chunks(acc_ref.shape[1]):
                 at_c = slice(start + c.start, start + c.stop)
-                acc_ref[:, c] += mm(lhs, jnp.concatenate([a_ref[:, at_c], b_ref[:, at_c]], axis=0))
+                rhs = [rows[part][:, at_c] for rows in blocks]
+                acc_ref[:, c] += mm(lhs, jnp.concatenate(rhs, axis=0))
 
     theirs = pl.ds(pl.multiple_of((1 - core) * block, block), block)
     ours = pl.ds(pl.multiple_of(core * block, block), block)
@@ -169,49 +189,88 @@
     return jnp.concatenate([rows[j : j + 1] + rows[n_slabs + j : n_slabs + j + 1] for j in range(n_slabs)], axis=1)
 
 
-def backward_other_kernel(wu_ref, wo_ref, bg_own, x_ref, low_ref, g_ref, gg_ref, ht_ref, bg_ref):
+def is_outer():
+    chip = lax.div(lax.axis_index("shard"), 2)
+    return (chip == 0) | (chip == lax.div(lax.axis_size("shard"), 2) - 1)
+
+
+def store_slabs(acc_ref, theirs, ours, biases, send_refs, keep_ref):
+    block = acc_ref.shape[0] // 2
+    n_slabs = acc_ref.shape[1] // SLAB
+    each = n_slabs // len(send_refs)
+    for j in range(n_slabs):
+        c, at = slice(j * SLAB, (j + 1) * SLAB), j % each * block
+        send_refs[j // each][at : at + block, :] = acc_ref[theirs, c].astype(BF16)
+        keep_ref[j * block : (j + 1) * block, :] = acc_ref[ours, c]
+    for i, bias in enumerate(biases):
+        low = bias_rows(bias).astype(BF16)
+        at = each * block + i * TILE
+        send_refs[-1][at : at + TILE, :] = low
+        at = n_slabs * block + i * TILE
+        keep_ref[at : at + TILE, :] = low.astype(F32)
+
+
+def first_kernel(x_own, gg_own, cr_own, ht_own, bg_own, keep_ref, *refs):
+    send_refs, (lhs_ref, acc_ref) = refs[:-2], refs[-2:]
+    outer = is_outer()
+
+    @pl.when(outer)
+    def _():
+        theirs, ours = products(6, 0, [(x_own, gg_own, cr_own, ht_own)], lhs_ref, acc_ref)
+        store_slabs(acc_ref, theirs, ours, [bg_own[...]], send_refs, keep_ref)
+
+    @pl.when(jnp.logical_not(outer))
+    def _():
+        for ref in (*send_refs, keep_ref):
+            ref[...] = jnp.zeros_like(ref)
+
+
+def second_kernel(wu_ref, wo_ref, bg_own, x_own, gg_own, cr_own, ht_own, x_ref, low_ref, cr_ref, g_ref, *refs):
+    gg_ref, ht_ref, bg_ref, keep_ref = refs[:4]
+    send_refs, (lhs_ref, acc_ref) = refs[4:-2], refs[-2:]
+    outer = is_outer()
+
+    @pl.when(outer)
+    def _():
+        for ref in (gg_ref, bg_ref, ht_ref):
+            ref[...] = jnp.zeros_like(ref)
+        theirs, ours = products(4, 0, [(x_own, gg_own, cr_own, ht_own)], lhs_ref, acc_ref)
+        store_slabs(acc_ref, theirs, ours, [bg_own[...]], send_refs, keep_ref)
+
+    @pl.when(jnp.logical_not(outer))
+    def _():
+        backward_rows(x_ref, g_ref[...], low_ref, wu_ref, wo_ref, gg_ref, bg_ref, ht_ref, None, None)
+        theirs, ours = products(2, 0, [(x_ref, gg_ref, cr_ref, ht_ref)], lhs_ref, acc_ref)
+        store_slabs(acc_ref, theirs, ours, [bg_ref[...]], send_refs, keep_ref)
+
+
+def near_kernel(wu_ref, wo_ref, x_ref, low_ref, cr_ref, g_ref, *refs):
+    own, inner, bg_own, bg_inner, first_ref, keep_ref = refs[:4], refs[4:8], *refs[8:12]
+    send_refs, (gg_ref, ht_ref, bg_ref, lhs_ref, acc_ref) = refs[12:-5], refs[-5:]
     backward_rows(x_ref, g_ref[...], low_ref, wu_ref, wo_ref, gg_ref, bg_ref, ht_ref, None, None)
-    bg_ref[...] = bg_own[...] + bg_ref[...]
-
-
-def far_sums(flip, start, own, other, bg_ref, send_ref, keep_ref, lhs_ref, acc_ref):
-    theirs, ours = products(flip, start, own[3], other[3], list(zip(own[:3], other[:3])), lhs_ref, acc_ref)
-    block, width = acc_ref.shape[0] // 2, acc_ref.shape[1]
-    for j in range(width // SLAB):
-        c, rows = slice(j * SLAB, (j + 1) * SLAB), slice(j * block, (j + 1) * block)
-        send_ref[rows, :] = acc_ref[theirs, c].astype(BF16)
-        keep_ref[rows, :] = acc_ref[ours, c]
-    rows = bias_rows(bg_ref[:, start : start + width])
-    send_ref[-TILE:, :] = rows.astype(BF16)
-    keep_ref[-TILE:, :] = rows.astype(BF16).astype(F32)
-
-
-def far_more_kernel(flip, start, *refs):
-    far_sums(flip, start, refs[:4], refs[4:8], *refs[8:])
-
-
-def far_kernel(flip, wu_ref, wo_ref, bg_own, x_own, gg_own, cr_own, ht_own, x_ref, low_ref, cr_ref, g_ref, *refs):
-    gg_ref, ht_ref, bg_ref = refs[:3]
-    backward_other_kernel(wu_ref, wo_ref, bg_own, x_ref, low_ref, g_ref, gg_ref, ht_ref, bg_ref)
-    far_sums(flip, 0, (x_own, gg_own, cr_own, ht_own), (x_ref, gg_ref, cr_ref, ht_ref), bg_ref, *refs[3:])
-
-
-def near_kernel(*refs):
-    own, other = refs[:4], refs[4:8]
-    send_ref, keep_ref, lhs_ref, acc_ref = refs[8:]
-    theirs, ours = products(0, 0, own[3], other[3], list(zip(own[:3], other[:3])), lhs_ref, acc_ref)
-    send_ref[...] = acc_ref[theirs, :].astype(BF16)
-    keep_ref[...] = acc_ref[ours, :]
-
-
-def round_kernel(n_slabs, keep_ref, recv_ref, out_ref):
-    out_ref[:-TILE, :] = (keep_ref[:-TILE, :] + recv_ref[:-TILE, :].astype(F32)).astype(BF16)
-    rows = keep_ref[-TILE:, :] + recv_ref[-TILE:, :].astype(F32)
-    out_ref[-TILE:, :] = bias_rows(bias_of(rows, n_slabs)).astype(BF16)
-
-
-def final_kernel(scale, start, keep_ref, near_ref, sent_ref, far_ref, *refs):
-    out_ref, bg_out, total_ref, bg_ref, sem_ref = refs[-5:]
+    theirs, ours = products(0, 0, [own, (x_ref, gg_ref, cr_ref, ht_ref), inner], lhs_ref, acc_ref)
+    store_slabs(acc_ref, theirs, ours, [bg_own[...], bg_ref[...], bg_inner[...]], send_refs, keep_ref)
+    sums = slice(0, first_ref.shape[0] - TILE)
+    keep_ref[sums, :] += first_ref[sums, :].astype(F32)
+
+
+def joined_bias(rows, n_slabs):
+    return bias_rows(bias_of(rows, n_slabs)).astype(BF16)
+
+
+def round_kernel(n_slabs, keep_ref, *refs):
+    recv_refs, out_ref = refs[:-1], refs[-1]
+    at = 0
+    for recv_ref in recv_refs:
+        rows = slice(at, at + recv_ref.shape[0])
+        out_ref[rows, :] = (keep_ref[rows, :] + recv_ref[...].astype(F32)).astype(BF16)
+        at = rows.stop
+    out_ref[-TILE:, :] = joined_bias(keep_ref[-TILE:, :] + recv_refs[-1][-TILE:, :].astype(F32), n_slabs)
+
+
+def final_kernel(scale, keep_ref, first_ref, second_ref, *refs):
+    near_refs, (out_ref, bg_out, total_ref, bg_ref, sem_ref) = refs[:-5], refs[-5:]
+    each = total_ref.shape[1] // SLAB // len(near_refs)
     block, width = total_ref.shape
     n_slabs = width // SLAB
     copies = []
@@ -221,14 +280,21 @@
         copies[-1].start()
 
     for j in range(n_slabs):
-        w = slice(start + j * SLAB, start + (j + 1) * SLAB)
-        total = keep_ref[:, w] + near_ref[:, w].astype(F32)
-        total = total + far_ref[j * block : (j + 1) * block, :].astype(F32)
-        total_ref[:, j * SLAB : (j + 1) * SLAB] = total * scale
-        write(total_ref.at[:, pl.ds(j * SLAB, SLAB)], out_ref.at[:, pl.ds(w.start, SLAB)], j)
-    ours, theirs = sent_ref[-TILE:, :].astype(F32), far_ref[-TILE:, :].astype(F32)
-    bg_ref[...] = bias_of(ours, n_slabs) + bias_of(theirs, n_slabs)
-    write(bg_ref, bg_out.at[:, pl.ds(start, width)], n_slabs)
+        c, rows = slice(j * SLAB, (j + 1) * SLAB), slice(j * block, (j + 1) * block)
+        at = j % each * block
+        total = keep_ref[rows, :] + near_refs[j // each][at : at + block, :].astype(F32)
+        total = total + second_ref[rows, :].astype(F32)
+        total_ref[:, c] = total * scale
+        write(total_ref.at[:, pl.ds(j * SLAB, SLAB)], out_ref.at[:, pl.ds(j * SLAB, SLAB)], j)
+    here = []
+    for i in range(3):
+        rows = slice(n_slabs * block + i * TILE, n_slabs * block + (i + 1) * TILE)
+        at = each * block + i * TILE
+        joined = joined_bias(keep_ref[rows, :] + near_refs[-1][at : at + TILE, :].astype(F32), n_slabs)
+        here.append(bias_of(joined.astype(F32), n_slabs))
+    there = [bias_of(ref[-TILE:, :].astype(F32), n_slabs) for ref in (first_ref, second_ref)]
+    bg_ref[...] = (here[0] + here[1]) + ((here[2] + there[0]) + there[1])
+    write(bg_ref, bg_out, n_slabs)
     for copy in copies:
         copy.wait()
 
@@ -260,17 +326,42 @@
     stack = 2 * rank + out
     block = stack // n_shard
     top_rows = out_grad.shape[0]
-    cuts = (0, width // 2, width)
-    n_cuts = len(cuts) - 1
     wide = sds((n, width), BF16)
     tall = sds((stack, n), BF16)
     low = sds((n, rank), BF16)
     row = sds((1, width), F32)
+    slab_rows = block * width // SLAB
 
     def across(value, axis, k):
         return lax.ppermute(value, axis, xor_pairs(lax.axis_size(axis), k))
 
+    def slab_outs(n_bias, pieces):
+        rows = [slab_rows // pieces] * pieces
+        rows[-1] += n_bias * TILE
+        return [sds((sum(rows), SLAB), F32)] + [sds((r, SLAB), BF16) for r in rows]
+
+    def sum_scratch(n_blocks):
+        return [pltpu.VMEM((2 * block, n_blocks * n), BF16), pltpu.VMEM((2 * block, width), F32)]
+
+    def rounded(keep, *sends):
+        (out,) = call(
+            functools.partial(round_kernel, width // SLAB),
+            [sds(keep.shape, BF16)],
+            [],
+            [VMEM] * (1 + len(sends)),
+            [keep] + [across(send, "shard", 1) for send in sends],
+            "join_cores",
+            cost=1,
+        )
+        return out
+
+    inside = [2 <= i < n_shard - 2 for i in range(n_shard)]
+    inner = [(i, i ^ 6 if inside[i] else i ^ 1) for i in range(n_shard)]
+    outer = [(i, i ^ 1 if inside[i] else i ^ 6) for i in range(n_shard)]
+    second = [(i, i ^ 2 if inside[i] else i ^ 4) for i in range(n_shard)]
+
     x_other = across(x, "shard", 2)
+    x_inner = lax.ppermute(x, "shard", inner)
     pieces = call(
         functools.partial(cut_kernel, n_tower),
         [sds((top_rows, out), BF16)] * n_tower,
@@ -301,75 +392,49 @@
         "backward_own",
         cost=1,
     )
+    own = [x_own, gg_own, cr_own, ht_own]
+    g_inner = lax.ppermute(g_own, "shard", inner)
     g_other = across(g_own, "shard", 2)
+    first = rounded(
+        *call(first_kernel, slab_outs(1, 1), sum_scratch(1), [VMEM] * 5, [*own, bg_own], "first_sums", cost=C1)
+    )
+    from_first = lax.ppermute(first, "shard", outer)
+    low_inner, cr_inner = call(
+        forward_inner_kernel, [low, wide], [], [VMEM] * 4, [after(x_inner, first), wd, wu, cross_bias], "forward_inner", cost=C2
+    )
     low_other, cr_other = call(
-        forward_rows,
-        [low, wide],
-        [],
-        [VMEM] * 4,
-        [x_other, wd, wu, cross_bias],
-        "forward_other",
-    )
-
-    def slab_outs(cut):
-        shape = (block * cut // SLAB + TILE, SLAB)
-        return [sds(shape, BF16), sds(shape, F32)]
-
-    def sum_scratch(cut):
-        return [pltpu.VMEM((2 * block, 2 * n), BF16), pltpu.VMEM((2 * block, cut), F32)]
-
-    own = [x_own, gg_own, cr_own, ht_own]
-    gg_other, ht_other, bias_sum, *far = call(
-        functools.partial(far_kernel, FAR),
-        [wide, tall, row] + slab_outs(cuts[1]),
-        sum_scratch(cuts[1]),
+        forward_rows, [low, wide], [], [VMEM] * 4, [after(x_other, low_inner, g_other), wd, wu, cross_bias], "forward_other", cost=C2
+    )
+    gg_inner, ht_inner, bg_inner, *sums = call(
+        second_kernel,
+        [wide, tall, row] + slab_outs(1, P2),
+        sum_scratch(1),
         [VMEM] * 11,
-        [wu, wo, bg_own, *own, x_other, low_other, cr_other, g_other],
-        "far_sums",
-    )
-    other = [x_other, gg_other, cr_other, ht_other]
-    far_parts = [far]
-    for i in range(1, n_cuts):
-        far_parts.append(
-            call(
-                functools.partial(far_more_kernel, FAR, cuts[i]),
-                slab_outs(cuts[i + 1] - cuts[i]),
-                sum_scratch(cuts[i + 1] - cuts[i]),
-                [VMEM] * 9,
-                [*own, *other, bias_sum],
-                "far_sums_more",
-            )
-        )
-    rounded, fars = [], []
-    for i, (send, keep) in enumerate(far_parts):
-        rounded += call(
-            functools.partial(round_kernel, (cuts[i + 1] - cuts[i]) // SLAB),
-            [sds(send.shape, BF16)],
-            [],
-            [VMEM] * 2,
-            [keep, across(send, "shard", 1)],
-            "far_round",
-            cost=1,
-        )
-        fars.append(across(rounded[-1], "shard", FAR))
-    (near_send, near_keep) = call(
-        near_kernel,
-        [sds((block, width), BF16), sds((block, width), F32)],
-        sum_scratch(width),
-        [VMEM] * 8,
-        [*own, *other[:3], after(ht_other, *rounded)],
-        "near_sums",
-        cost=1,
-    )
-    near_other = across(near_send, "shard", 1)
+        [wu, wo, bg_own, *own, x_inner, after(low_inner, low_other), cr_inner, g_inner],
+        "second_sums",
+        cost=C2,
+    )
+    second_sum = rounded(*sums)
+    from_second = lax.ppermute(second_sum, "shard", second)
     grad_inputs = call(
         functools.partial(inputs_kernel, n_tower),
         [sds((top_rows, width), BF16)] * n_tower,
         [pltpu.VMEM((n, width), BF16)],
         [VMEM] * 3,
-        [wd, gh_own, after(direct, *rounded)],
+        [wd, gh_own, after(direct, second_sum)],
         "grad_inputs",
-    )
+        cost=C4,
+    )
+    near_keep, *near_sends = call(
+        near_kernel,
+        slab_outs(3, PN),
+        [pltpu.VMEM((n, width), BF16), pltpu.VMEM((stack, n), BF16), pltpu.VMEM((1, width), F32)] + sum_scratch(3),
+        [VMEM] * 17,
+        [wu, wo, x_other, after(low_other, *grad_inputs), cr_other, g_other, *own, x_inner, gg_inner, cr_inner, ht_inner, bg_own, bg_inner, from_first],
+        "near_sums",
+        cost=CN,
+    )
+    near_others = [across(send, "shard", 1) for send in near_sends]
     returned = [grad_inputs[0]]
     for k in range(1, n_tower):
         piece = grad_inputs[k]
@@ -383,24 +448,19 @@
         "place_features",
         cost=1,
     )
-    results = []
-    for i, far in enumerate(fars):
-        cut = cuts[i + 1] - cuts[i]
-        results = call(
-            functools.partial(final_kernel, 1.0 / math.sqrt(n * n_shard), cuts[i]),
-            [sds((block, width), F32), row],
-            [
-                pltpu.VMEM((block, cut), F32),
-                pltpu.VMEM((1, cut), F32),
-                pltpu.SemaphoreType.DMA((cut // SLAB + 1,)),
-            ],
-            [VMEM] * 4 + [HBM] * len(results),
-            [near_keep, near_other, rounded[i], far, *results],
-            "add_up",
-            out_space=HBM,
-            aliases={4 + j: j for j in range(len(results))},
-        )
-    weight_grad, bias_grad = results
+    weight_grad, bias_grad = call(
+        functools.partial(final_kernel, 1.0 / math.sqrt(n * n_shard)),
+        [sds((block, width), F32), row],
+        [
+            pltpu.VMEM((block, width), F32),
+            pltpu.VMEM((1, width), F32),
+            pltpu.SemaphoreType.DMA((width // SLAB + 1,)),
+        ],
+        [VMEM] * (3 + len(near_others)),
+        [near_keep, from_first, from_second, *near_others],
+        "add_up",
+        out_space=HBM,
+    )
     return feature_grad, weight_grad[None], bias_grad
 
 

time: 41 us -> 40.5 us (0.988)
  waiting for transfers between devices: 12.6 us -> 9.36 us
  starting transfers between devices: 15.3 us -> 17.3 us
  Pallas kernels: 10.2 us -> 10.8 us
    ppermute x13 -> x15, waiting for transfers between devices: 12.6 us -> 4.89 us  [across(): return lax.ppermute(value, axis, xor_pairs(lax.axis_size(axis), k))]
    ppermute x0 -> x4, waiting for transfers between devices: none -> 4.47 us  [the longest x1 2.32 us: paired_body(): from_second = lax.ppermute(second_sum, 'shard', second)]
    ppermute x0 -> x4, starting transfers between devices: none -> 3.6 us  [the longest x1 1.4 us: paired_body(): from_first = lax.ppermute(first, 'shard', outer)]
    ppermute x13 -> x15, starting transfers between devices: 15.3 us -> 13.7 us  [across(): return lax.ppermute(value, axis, xor_pairs(lax.axis_size(axis), k))]
    pallas_call x13, Pallas kernels: 10.2 us -> 10.8 us  [call(): pl.pallas_call(kernel, out_shape=outs, in_specs=[pl.BlockSpec(memory_spac...]
  transfers between devices with their start and end apart: 13 -> 19, of which waited for: 7 -> 7; matrix products, arithmetic and copies ran while one was open for 0% -> 0% of each run, Pallas kernels for 19% -> 24%
where the time goes in v4:
time: 40.5 us; the launch traced here: 40.3 us
  starting transfers between devices  17.3 us (43%)
  Pallas kernels  10.8 us (27%)
  waiting for transfers between devices  9.36 us (23%)
  local copies, waits for them, and re-layouts  2.03 us (5%)
  between operations  0.8 us (2%)
    ppermute x15, starting transfers between devices, across(): return lax.ppermute(value, axis, xor_pairs(lax.axis_size(axis), k))  13.7 us
    pallas_call x13, Pallas kernels, call(): pl.pallas_call(kernel, out_shape=outs, in_specs=[pl.BlockSpec(memory_spac...  10.8 us
    ppermute x15, waiting for transfers between devices, across(): return lax.ppermute(value, axis, xor_pairs(lax.axis_size(axis), k))  4.89 us
    ppermute x1, waiting for transfers between devices, paired_body(): from_second = lax.ppermute(second_sum, 'shard', second)  2.32 us
    ppermute x1, waiting for transfers between devices, paired_body(): from_first = lax.ppermute(first, 'shard', outer)  2.15 us
    unnamed x8, local copies, waits for them, and re-layouts  2.03 us
    ppermute x1, starting transfers between devices, paired_body(): from_first = lax.ppermute(first, 'shard', outer)  1.4 us
    ppermute x1, starting transfers between devices, paired_body(): from_second = lax.ppermute(second_sum, 'shard', second)  1.18 us
  transfers between devices with their start and end apart: 19, of which 7 were waited for; matrix products, arithmetic and copies ran while one was open for 0% of the time, Pallas kernels for 24%

profile of v4, /device:TPU:0, one launch (start us, length us, event | category | flops | bytes accessed | tf_op | source)
XLA Modules:
  0.0 40.3 jit_solution(7333486252055058838)
XLA Ops:
  0.6 0.5 %collective-permute-start.3 = (bf16[128,2048]{1,0:T(8,128)(2,1)}, bf16[128,2048]{1,0:T(8,128)(2,1)S(1)}, u32[]{:S(2)}, u32[]{:S(2)}) collective-permute-start(bf16[128,2048]{1,0:T(8,128)(2,1)} %bitcast.5), channel_id=1, source_target_pairs={{0,1},{1,0},{2,4},{3,5},{4,2},{5,3},{6,7},{7,6},{8,9},{9,8},{10,12... | collective-permute-start | bytes 1572872 | tf_op jit(solution)/shard_map/ppermute | solution.py:364
  1.1 4.1 %collective-permute-start.5 = (bf16[128,2048]{1,0:T(8,128)(2,1)}, bf16[128,2048]{1,0:T(8,128)(2,1)S(1)}, u32[]{:S(2)}, u32[]{:S(2)}) collective-permute-start(bf16[128,2048]{1,0:T(8,128)(2,1)} %bitcast.6), channel_id=1, source_target_pairs={{0,2},{1,3},{2,0},{3,1},{4,6},{5,7},{6,4},{7,5},{8,10},{9,11},{10,... | collective-permute-start | bytes 1572872 | tf_op jit(solution)/shard_map/ppermute | solution.py:336
  5.3 0.8 %copy-done.1 = bf16[32,1024]{1,0:T(8,128)(2,1)S(1)} copy-done((bf16[32,1024]{1,0:T(8,128)(2,1)S(1)}, bf16[32,1024]{1,0:T(8,128)(2,1)}, u32[]{:S(2)}) %copy-start.1) | copy-done | bytes 65560
  6.2 1.6 %collective-permute-start = (bf16[32,256]{1,0:T(8,128)(2,1)S(1)}, bf16[32,256]{1,0:T(8,128)(2,1)S(1)}, u32[]{:S(2)}, u32[]{:S(2)}) collective-permute-start(bf16[32,256]{1,0:T(8,128)(2,1)S(1)} %get-tuple-element.55), channel_id=1, source_target_pairs={{0,8},{8,0},{16,24},{24,16},{1,9},{9,1},{17,25},{25,17},{2,10},{10... | collective-permute-start | bytes 49160 | tf_op jit(solution)/shard_map/ppermute | solution.py:336
  7.8 1.5 %collective-permute-start.1 = (bf16[32,256]{1,0:T(8,128)(2,1)S(1)}, bf16[32,256]{1,0:T(8,128)(2,1)S(1)}, u32[]{:S(2)}, u32[]{:S(2)}) collective-permute-start(bf16[32,256]{1,0:T(8,128)(2,1)S(1)} %get-tuple-element.56), channel_id=1, source_target_pairs={{0,16},{8,24},{16,0},{24,8},{1,17},{9,25},{17,1},{25,9},{2,18},{10... | collective-permute-start | bytes 49160 | tf_op jit(solution)/shard_map/ppermute | solution.py:336
  9.8 1.0 %copy-done = bf16[1,128,2048]{2,1,0:T(8,128)(2,1)S(1)} copy-done((bf16[1,128,2048]{2,1,0:T(8,128)(2,1)S(1)}, bf16[1,128,2048]{2,1,0:T(8,128)(2,1)}, u32[]{:S(2)}) %copy-start) | copy-done | bytes 524312
  10.8 2.1 %forward_own.1 = (bf16[2048,256]{1,0:T(8,128)(2,1)S(1)}, bf16[256,2048]{1,0:T(8,128)(2,1)S(1)}, bf16[2048,256]{1,0:T(8,128)(2,1)S(1)}, bf16[128,2048]{1,0:T(8,12...) custom-call(bf16[2048,256]{1,0:T(8,128)(2,1)} %bitcast.8, ...), custom_call_target="tpu_custom_call" | custom-call | flops 1 | bytes 1 | tf_op jit(solution)/shard_map/forward_own/pallas_call | solution.py:39
  13.0 0.9 %collective-permute-done.2.refs_3_ = bf16[32,256]{1,0:T(8,128)(2,1)S(1)} collective-permute-done((bf16[32,256]{1,0:T(8,128)(2,1)S(1)}, bf16[32,256]{1,0:T(8,128)(2,1)S(1)}, u32[]{:S(2)}, u32[]{:S(2)}) %collective-permute-start.2) | collective-permute-done | bytes 16416 | tf_op jit(solution)/shard_map/ppermute | solution.py:336
  13.9 1.1 %backward_own.1 = (bf16[128,256]{1,0:T(8,128)(2,1)S(1)}, bf16[128,256]{1,0:T(8,128)(2,1)S(1)}, bf16[768,128]{1,0:T(8,128)(2,1)S(1)}, bf16[128,2048]{1,0:T(8,128)...) custom-call(bf16[256,2048]{1,0:T(8,128)(2,1)S(1)} %get-tuple-element.49.wu_ref, ...), custom_call_target="tpu_custom_call" | custom-call | flops 1 | bytes 1 | tf_op jit(solution)/shard_map/backward_own/pallas_call | solution.py:39
  15.0 0.6 %first_sums.1 = (f32[784,256]{1,0:T(8,128)S(1)}, bf16[784,256]{1,0:T(8,128)(2,1)S(1)}) custom-call(bf16[128,2048]{1,0:T(8,128)(2,1)S(1)} %get-tuple-element.51.x_ref.x_own.refs_0_, bf16[128,2048]{1,0:T(8,128)(2,1)S(1)} %get-tuple-element.61.gg_own.refs_1_, bf16[128,2048]{1,0:T(8,128)(2,1)S(1)} %get-tuple-element.62.cr_own.refs_2_, ...), custom_call_target="tpu_custom_call" | custom-call | flops 1 | bytes 1 | tf_op jit(solution)/shard_map/first_sums/pallas_call | solution.py:39
  15.7 0.5 %collective-permute-start.7 = (bf16[128,256]{1,0:T(8,128)(2,1)S(1)}, bf16[128,256]{1,0:T(8,128)(2,1)S(1)}, u32[]{:S(2)}, u32[]{:S(2)}) collective-permute-start(bf16[128,256]{1,0:T(8,128)(2,1)S(1)} %get-tuple-element.68), channel_id=1, source_target_pairs={{0,1},{1,0},{2,4},{3,5},{4,2},{5,3},{6,7},{7,6},{8,9},{9,8},{10,12... | collective-permute-start | bytes 196616 | tf_op jit(solution)/shard_map/ppermute | solution.py:396
  16.2 0.7 %collective-permute-start.6 = (bf16[128,256]{1,0:T(8,128)(2,1)S(1)}, bf16[128,256]{1,0:T(8,128)(2,1)S(1)}, u32[]{:S(2)}, u32[]{:S(2)}) collective-permute-start(bf16[128,256]{1,0:T(8,128)(2,1)S(1)} %get-tuple-element.68), channel_id=1, source_target_pairs={{0,2},{1,3},{2,0},{3,1},{4,6},{5,7},{6,4},{7,5},{8,10},{9,11},{10,... | collective-permute-start | bytes 196616 | tf_op jit(solution)/shard_map/ppermute | solution.py:336
  16.9 0.5 %collective-permute-done.4.refs_0_ = bf16[784,256]{1,0:T(8,128)(2,1)S(1)} collective-permute-done((bf16[784,256]{1,0:T(8,128)(2,1)S(1)}, bf16[784,256]{1,0:T(8,128)(2,1)S(1)}, u32[]{:S(2)}, u32[]{:S(2)}) %collective-permute-start.4) | collective-permute-done | bytes 401440 | tf_op jit(solution)/shard_map/ppermute | solution.py:336
  17.5 1.4 %collective-permute-start.13 = (bf16[784,256]{1,0:T(8,128)(2,1)S(1)}, bf16[784,256]{1,0:T(8,128)(2,1)S(1)}, u32[]{:S(2)}, u32[]{:S(2)}) collective-permute-start(bf16[784,256]{1,0:T(8,128)(2,1)S(1)} %join_cores.2), channel_id=1, source_target_pairs={{0,6},{1,7},{2,3},{3,2},{4,5},{5,4},{6,0},{7,1},{8,14},{9,15},{10,... | collective-permute-start | bytes 1204232 | tf_op jit(solution)/shard_map/ppermute | solution.py:401
  19.0 1.5 %collective-permute-done.6.g_ref = bf16[128,256]{1,0:T(8,128)(2,1)S(1)} collective-permute-done((bf16[128,256]{1,0:T(8,128)(2,1)S(1)}, bf16[128,256]{1,0:T(8,128)(2,1)S(1)}, u32[]{:S(2)}, u32[]{:S(2)}) %collective-permute-start.6) | collective-permute-done | bytes 65568 | tf_op jit(solution)/shard_map/ppermute | solution.py:336
  20.4 0.8 %forward_other.1 = (bf16[128,256]{1,0:T(8,128)(2,1)S(1)}, bf16[128,2048]{1,0:T(8,128)(2,1)S(1)}) custom-call(bf16[128,2048]{1,0:T(8,128)(2,1)S(1)} %collective-permute-done.5.x_ref, bf16[2048,256]{1,0:T(8,128)(2,1)S(1)} %get-tuple-element.48.wd_ref, bf16[256,2048]{1,0:T(8,128)(2,1)S(1)} %get-tuple-element.49.wu_ref, f32[1,2048]{1,0:T(1,128)S(1)} %copy-done.2), custom_call_target="tpu_custom_call" | custom-call | flops 1000000000 | bytes 1 | tf_op jit(solution)/shard_map/forward_other/pallas_call | solution.py:39
  21.2 1.0 %second_sums.1 = (bf16[128,2048]{1,0:T(8,128)(2,1)S(1)}, bf16[768,128]{1,0:T(8,128)(2,1)S(1)}, f32[1,2048]{1,0:T(1,128)S(1)}, f32[784,256]{1,0:T(8,128)S(1)}, bf...) custom-call(bf16[256,2048]{1,0:T(8,128)(2,1)S(1)} %get-tuple-element.49.wu_ref, ...), custom_call_target="tpu_custom_call" | custom-call | flops 1000000000 | bytes 1 | tf_op jit(solution)/shard_map/second_sums/pallas_call | solution.py:39
  22.3 0.5 %collective-permute-start.8 = (bf16[384,256]{1,0:T(8,128)(2,1)S(1)}, bf16[384,256]{1,0:T(8,128)(2,1)S(1)}, u32[]{:S(2)}, u32[]{:S(2)}) collective-permute-start(bf16[384,256]{1,0:T(8,128)(2,1)S(1)} %get-tuple-element.74), channel_id=1, source_target_pairs={{0,1},{1,0},{2,3},{3,2},{4,5},{5,4},{6,7},{7,6},{8,9},{9,8},{10,11... | collective-permute-start | bytes 589832 | tf_op jit(solution)/shard_map/ppermute | solution.py:336
  22.8 1.2 %collective-permute-done.8.refs_0_ = bf16[384,256]{1,0:T(8,128)(2,1)S(1)} collective-permute-done((bf16[384,256]{1,0:T(8,128)(2,1)S(1)}, bf16[384,256]{1,0:T(8,128)(2,1)S(1)}, u32[]{:S(2)}, u32[]{:S(2)}) %collective-permute-start.8) | collective-permute-done | bytes 196640 | tf_op jit(solution)/shard_map/ppermute | solution.py:336
  24.2 1.2 %collective-permute-start.14 = (bf16[784,256]{1,0:T(8,128)(2,1)S(1)}, bf16[784,256]{1,0:T(8,128)(2,1)S(1)}, u32[]{:S(2)}, u32[]{:S(2)}) collective-permute-start(bf16[784,256]{1,0:T(8,128)(2,1)S(1)} %join_cores.3), channel_id=1, source_target_pairs={{0,4},{1,5},{2,0},{3,1},{4,6},{5,7},{6,2},{7,3},{8,12},{9,13},{10,... | collective-permute-start | bytes 1204232 | tf_op jit(solution)/shard_map/ppermute | solution.py:418
  25.3 0.5 %grad_inputs.1 = (bf16[32,2048]{1,0:T(8,128)(2,1)S(1)}, bf16[32,2048]{1,0:T(8,128)(2,1)S(1)}, bf16[32,2048]{1,0:T(8,128)(2,1)S(1)}, bf16[32,2048]{1,0:T(8,128)(2,1)S(1)}) custom-call(bf16[2048,256]{1,0:T(8,128)(2,1)S(1)} %get-tuple-element.48.wd_ref, bf16[128,256]{1,0:T(8,128)(2,1)S(1)} %get-tuple-element.58.gh_ref, f32[128,2048]{1,0:T(8,128)S(1)} %get-tuple-element.76.direct_ref), custom_call_target="tpu_custom_call" | custom-call | flops 1 | bytes 1 | tf_op jit(solution)/shard_map/grad_inputs/pallas_call | solution.py:39
  25.8 1.1 %collective-permute-start.10 = (bf16[32,2048]{1,0:T(8,128)(2,1)S(1)}, bf16[32,2048]{1,0:T(8,128)(2,1)S(1)}, u32[]{:S(2)}, u32[]{:S(2)}) collective-permute-start(bf16[32,2048]{1,0:T(8,128)(2,1)S(1)} %get-tuple-element.78), channel_id=1, source_target_pairs={{0,8},{8,0},{16,24},{24,16},{1,9},{9,1},{17,25},{25,17},{2,10},{10... | collective-permute-start | bytes 393224 | tf_op jit(solution)/shard_map/ppermute | solution.py:336
  26.9 1.5 %collective-permute-start.11 = (bf16[32,2048]{1,0:T(8,128)(2,1)S(1)}, bf16[32,2048]{1,0:T(8,128)(2,1)S(1)}, u32[]{:S(2)}, u32[]{:S(2)}) collective-permute-start(bf16[32,2048]{1,0:T(8,128)(2,1)S(1)} %get-tuple-element.79), channel_id=1, source_target_pairs={{0,16},{8,24},{16,0},{24,8},{1,17},{9,25},{17,1},{25,9},{2,18},{10... | collective-permute-start | bytes 393224 | tf_op jit(solution)/shard_map/ppermute | solution.py:336
  28.5 0.9 %collective-permute-start.12 = (bf16[32,2048]{1,0:T(8,128)(2,1)S(1)}, bf16[32,2048]{1,0:T(8,128)(2,1)S(1)}, u32[]{:S(2)}, u32[]{:S(2)}) collective-permute-start(bf16[32,2048]{1,0:T(8,128)(2,1)S(1)} %get-tuple-element.80), channel_id=1, source_target_pairs={{0,24},{8,16},{16,8},{24,0},{1,25},{9,17},{17,9},{25,1},{2,26},{10... | collective-permute-start | bytes 393224 | tf_op jit(solution)/shard_map/ppermute | solution.py:336
  29.4 2.1 %collective-permute-done.13.refs_10_.first_ref = bf16[784,256]{1,0:T(8,128)(2,1)S(1)} collective-permute-done((bf16[784,256]{1,0:T(8,128)(2,1)S(1)}, bf16[784,256]{1,0:T(8,128)(2,1)S(1)}, u32[]{:S(2)}, u32[]{:S(2)}) %collective-permute-start.13) | collective-permute-done | bytes 401440 | tf_op jit(solution)/shard_map/ppermute | solution.py:401
  31.5 1.9 %near_sums.1 = (f32[816,256]{1,0:T(8,128)S(1)}, bf16[192,256]{1,0:T(8,128)(2,1)S(1)}, bf16[192,256]{1,0:T(8,128)(2,1)S(1)}, bf16[192,256]{1,0:T(8,128)(2,1)S(1)}, bf16[240,256]{1,0:T(8,128)(2,1)S(1)}) custom-call(bf16[256,2048]{1,0:T(8,128)(2,1)S(1)} %get-tuple-element.49.wu_ref, bf16[2048,256]{1,0:T(8,128)(2,1)S(1)} %get-tuple-element.50.wo_ref, ...), custom_call_target="tpu_custom_call" | custom-call | flops 1000000000 | bytes 1 | tf_op jit(solution)/shard_map/near_sums/pallas_call | solution.py:39
  33.6 0.5 %collective-permute-start.15 = (bf16[192,256]{1,0:T(8,128)(2,1)S(1)}, bf16[192,256]{1,0:T(8,128)(2,1)S(1)}, u32[]{:S(2)}, u32[]{:S(2)}) collective-permute-start(bf16[192,256]{1,0:T(8,128)(2,1)S(1)} %get-tuple-element.87), channel_id=1, source_target_pairs={{0,1},{1,0},{2,3},{3,2},{4,5},{5,4},{6,7},{7,6},{8,9},{9,8},{10,11... | collective-permute-start | bytes 294920 | tf_op jit(solution)/shard_map/ppermute | solution.py:336
  34.1 0.7 %collective-permute-done.11.refs_2_ = bf16[32,2048]{1,0:T(8,128)(2,1)S(1)} collective-permute-done((bf16[32,2048]{1,0:T(8,128)(2,1)S(1)}, bf16[32,2048]{1,0:T(8,128)(2,1)S(1)}, u32[]{:S(2)}, u32[]{:S(2)}) %collective-permute-start.11) | collective-permute-done | bytes 131104 | tf_op jit(solution)/shard_map/ppermute | solution.py:336
  34.8 0.5 %collective-permute-start.17 = (bf16[192,256]{1,0:T(8,128)(2,1)S(1)}, bf16[192,256]{1,0:T(8,128)(2,1)S(1)}, u32[]{:S(2)}, u32[]{:S(2)}) collective-permute-start(bf16[192,256]{1,0:T(8,128)(2,1)S(1)} %get-tuple-element.89), channel_id=1, source_target_pairs={{0,1},{1,0},{2,3},{3,2},{4,5},{5,4},{6,7},{7,6},{8,9},{9,8},{10,11... | collective-permute-start | bytes 294920 | tf_op jit(solution)/shard_map/ppermute | solution.py:336
  35.5 1.5 %place_features.1 = bf16[32,8192]{1,0:T(8,128)(2,1)} custom-call(s32[64]{0:T(128)S(1)} %copy-done.3, bf16[32,2048]{1,0:T(8,128)(2,1)S(1)} %get-tuple-element.77.refs_0_, bf16[32,2048]{1,0:T(8,128)(2,1)S(1)} %collective-permute-done.10.refs_1_, bf16[32,2048]{1,0:T(8,128)(2,1)S(1)} %collective-permute-done.11.refs_2_, ...), custom_call_target="tpu_custom_call" | custom-call | flops 1 | bytes 1 | tf_op jit(solution)/shard_map/place_features/pallas_call | solution.py:39
  37.0 2.3 %collective-permute-done.14.second_ref = bf16[784,256]{1,0:T(8,128)(2,1)S(1)} collective-permute-done((bf16[784,256]{1,0:T(8,128)(2,1)S(1)}, bf16[784,256]{1,0:T(8,128)(2,1)S(1)}, u32[]{:S(2)}, u32[]{:S(2)}) %collective-permute-start.14) | collective-permute-done | bytes 401440 | tf_op jit(solution)/shard_map/ppermute | solution.py:418
  39.3 1.0 %add_up.1 = (f32[96,2048]{1,0:T(8,128)}, f32[1,2048]{1,0:T(1,128)}) custom-call(f32[816,256]{1,0:T(8,128)S(1)} %get-tuple-element.86.keep_ref, bf16[784,256]{1,0:T(8,128)(2,1)S(1)} %collective-permute-done.13.refs_10_.first_ref, bf16[784,256]{1,0:T(8,128)(2,1)S(1)} %collective-permute-done.14.second_ref, ...), custom_call_target="tpu_custom_call" | custom-call | flops 10000000000 | bytes 1 | tf_op jit(solution)/shard_map/add_up/pallas_call | solution.py:39
  (27 shorter events, 1.2 us)
Async XLA Ops:
  0.6 18.3 %collective-permute-start.3 = (bf16[128,2048]{1,0:T(8,128)(2,1)}, bf16[128,2048]{1,0:T(8,128)(2,1)S(1)}, u32[]{:S(2)}, u32[]{:S(2)}) collective-permute-start(bf16[128,2048]{1,0:T(8,128)(2,1)} %bitcast.5), channel_id=1, source_target_pairs={{0,1},{1,0},{2,4},{3,5},{4,2},{5,3},{6,7},{7,6},{8,9},{9,8},{10,12... | collective-permute-start | bytes 1572872 | tf_op jit(solution)/shard_map/ppermute | solution.py:364
  1.1 19.3 %collective-permute-start.5 = (bf16[128,2048]{1,0:T(8,128)(2,1)}, bf16[128,2048]{1,0:T(8,128)(2,1)S(1)}, u32[]{:S(2)}, u32[]{:S(2)}) collective-permute-start(bf16[128,2048]{1,0:T(8,128)(2,1)} %bitcast.6), channel_id=1, source_target_pairs={{0,2},{1,3},{2,0},{3,1},{4,6},{5,7},{6,4},{7,5},{8,10},{9,11},{10,... | collective-permute-start | bytes 1572872 | tf_op jit(solution)/shard_map/ppermute | solution.py:336
  5.3 0.8 %copy-start.1 = (bf16[32,1024]{1,0:T(8,128)(2,1)S(1)}, bf16[32,1024]{1,0:T(8,128)(2,1)}, u32[]{:S(2)}) copy-start(bf16[32,1024]{1,0:T(8,128)(2,1)} %grad_ref.1) | copy-start | bytes 196612
  6.2 3.6 %copy-start.2 = (f32[1,2048]{1,0:T(1,128)S(1)}, f32[1,2048]{1,0:T(1,128)}, u32[]{:S(2)}) copy-start(f32[1,2048]{1,0:T(1,128)} %bias_ref.5) | copy-start | bytes 24580
  6.2 6.8 %collective-permute-start = (bf16[32,256]{1,0:T(8,128)(2,1)S(1)}, bf16[32,256]{1,0:T(8,128)(2,1)S(1)}, u32[]{:S(2)}, u32[]{:S(2)}) collective-permute-start(bf16[32,256]{1,0:T(8,128)(2,1)S(1)} %get-tuple-element.55), channel_id=1, source_target_pairs={{0,8},{8,0},{16,24},{24,16},{1,9},{9,1},{17,25},{25,17},{2,10},{10... | collective-permute-start | bytes 49160 | tf_op jit(solution)/shard_map/ppermute | solution.py:336
  7.8 5.2 %collective-permute-start.1 = (bf16[32,256]{1,0:T(8,128)(2,1)S(1)}, bf16[32,256]{1,0:T(8,128)(2,1)S(1)}, u32[]{:S(2)}, u32[]{:S(2)}) collective-permute-start(bf16[32,256]{1,0:T(8,128)(2,1)S(1)} %get-tuple-element.56), channel_id=1, source_target_pairs={{0,16},{8,24},{16,0},{24,8},{1,17},{9,25},{17,1},{25,9},{2,18},{10... | collective-permute-start | bytes 49160 | tf_op jit(solution)/shard_map/ppermute | solution.py:336
  9.3 4.6 %collective-permute-start.2 = (bf16[32,256]{1,0:T(8,128)(2,1)S(1)}, bf16[32,256]{1,0:T(8,128)(2,1)S(1)}, u32[]{:S(2)}, u32[]{:S(2)}) collective-permute-start(bf16[32,256]{1,0:T(8,128)(2,1)S(1)} %get-tuple-element.57), channel_id=1, source_target_pairs={{0,24},{8,16},{16,8},{24,0},{1,25},{9,17},{17,9},{25,1},{2,26},{10... | collective-permute-start | bytes 49160 | tf_op jit(solution)/shard_map/ppermute | solution.py:336
  9.8 1.0 %copy-start = (bf16[1,128,2048]{2,1,0:T(8,128)(2,1)S(1)}, bf16[1,128,2048]{2,1,0:T(8,128)(2,1)}, u32[]{:S(2)}) copy-start(bf16[1,128,2048]{2,1,0:T(8,128)(2,1)} %param.8) | copy-start | bytes 1572868
  15.6 1.8 %collective-permute-start.4 = (bf16[784,256]{1,0:T(8,128)(2,1)S(1)}, bf16[784,256]{1,0:T(8,128)(2,1)S(1)}, u32[]{:S(2)}, u32[]{:S(2)}) collective-permute-start(bf16[784,256]{1,0:T(8,128)(2,1)S(1)} %get-tuple-element.65), channel_id=1, source_target_pairs={{0,1},{1,0},{2,3},{3,2},{4,5},{5,4},{6,7},{7,6},{8,9},{9,8},{10,11... | collective-permute-start | bytes 1204232 | tf_op jit(solution)/shard_map/ppermute | solution.py:336
  15.7 5.6 %collective-permute-start.7 = (bf16[128,256]{1,0:T(8,128)(2,1)S(1)}, bf16[128,256]{1,0:T(8,128)(2,1)S(1)}, u32[]{:S(2)}, u32[]{:S(2)}) collective-permute-start(bf16[128,256]{1,0:T(8,128)(2,1)S(1)} %get-tuple-element.68), channel_id=1, source_target_pairs={{0,1},{1,0},{2,4},{3,5},{4,2},{5,3},{6,7},{7,6},{8,9},{9,8},{10,12... | collective-permute-start | bytes 196616 | tf_op jit(solution)/shard_map/ppermute | solution.py:396
  16.2 4.3 %collective-permute-start.6 = (bf16[128,256]{1,0:T(8,128)(2,1)S(1)}, bf16[128,256]{1,0:T(8,128)(2,1)S(1)}, u32[]{:S(2)}, u32[]{:S(2)}) collective-permute-start(bf16[128,256]{1,0:T(8,128)(2,1)S(1)} %get-tuple-element.68), channel_id=1, source_target_pairs={{0,2},{1,3},{2,0},{3,1},{4,6},{5,7},{6,4},{7,5},{8,10},{9,11},{10,... | collective-permute-start | bytes 196616 | tf_op jit(solution)/shard_map/ppermute | solution.py:336
  17.5 14.0 %collective-permute-start.13 = (bf16[784,256]{1,0:T(8,128)(2,1)S(1)}, bf16[784,256]{1,0:T(8,128)(2,1)S(1)}, u32[]{:S(2)}, u32[]{:S(2)}) collective-permute-start(bf16[784,256]{1,0:T(8,128)(2,1)S(1)} %join_cores.2), channel_id=1, source_target_pairs={{0,6},{1,7},{2,3},{3,2},{4,5},{5,4},{6,0},{7,1},{8,14},{9,15},{10,... | collective-permute-start | bytes 1204232 | tf_op jit(solution)/shard_map/ppermute | solution.py:401
  22.2 1.8 %collective-permute-start.9 = (bf16[400,256]{1,0:T(8,128)(2,1)S(1)}, bf16[400,256]{1,0:T(8,128)(2,1)S(1)}, u32[]{:S(2)}, u32[]{:S(2)}) collective-permute-start(bf16[400,256]{1,0:T(8,128)(2,1)S(1)} %get-tuple-element.75), channel_id=1, source_target_pairs={{0,1},{1,0},{2,3},{3,2},{4,5},{5,4},{6,7},{7,6},{8,9},{9,8},{10,11... | collective-permute-start | bytes 614408 | tf_op jit(solution)/shard_map/ppermute | solution.py:336
  22.3 1.7 %collective-permute-start.8 = (bf16[384,256]{1,0:T(8,128)(2,1)S(1)}, bf16[384,256]{1,0:T(8,128)(2,1)S(1)}, u32[]{:S(2)}, u32[]{:S(2)}) collective-permute-start(bf16[384,256]{1,0:T(8,128)(2,1)S(1)} %get-tuple-element.74), channel_id=1, source_target_pairs={{0,1},{1,0},{2,3},{3,2},{4,5},{5,4},{6,7},{7,6},{8,9},{9,8},{10,11... | collective-permute-start | bytes 589832 | tf_op jit(solution)/shard_map/ppermute | solution.py:336
  24.2 15.1 %collective-permute-start.14 = (bf16[784,256]{1,0:T(8,128)(2,1)S(1)}, bf16[784,256]{1,0:T(8,128)(2,1)S(1)}, u32[]{:S(2)}, u32[]{:S(2)}) collective-permute-start(bf16[784,256]{1,0:T(8,128)(2,1)S(1)} %join_cores.3), channel_id=1, source_target_pairs={{0,4},{1,5},{2,0},{3,1},{4,6},{5,7},{6,2},{7,3},{8,12},{9,13},{10,... | collective-permute-start | bytes 1204232 | tf_op jit(solution)/shard_map/ppermute | solution.py:418
  25.8 7.7 %collective-permute-start.10 = (bf16[32,2048]{1,0:T(8,128)(2,1)S(1)}, bf16[32,2048]{1,0:T(8,128)(2,1)S(1)}, u32[]{:S(2)}, u32[]{:S(2)}) collective-permute-start(bf16[32,2048]{1,0:T(8,128)(2,1)S(1)} %get-tuple-element.78), channel_id=1, source_target_pairs={{0,8},{8,0},{16,24},{24,16},{1,9},{9,1},{17,25},{25,17},{2,10},{10... | collective-permute-start | bytes 393224 | tf_op jit(solution)/shard_map/ppermute | solution.py:336
  26.9 7.9 %collective-permute-start.11 = (bf16[32,2048]{1,0:T(8,128)(2,1)S(1)}, bf16[32,2048]{1,0:T(8,128)(2,1)S(1)}, u32[]{:S(2)}, u32[]{:S(2)}) collective-permute-start(bf16[32,2048]{1,0:T(8,128)(2,1)S(1)} %get-tuple-element.79), channel_id=1, source_target_pairs={{0,16},{8,24},{16,0},{24,8},{1,17},{9,25},{17,1},{25,9},{2,18},{10... | collective-permute-start | bytes 393224 | tf_op jit(solution)/shard_map/ppermute | solution.py:336
  28.5 6.4 %collective-permute-start.12 = (bf16[32,2048]{1,0:T(8,128)(2,1)S(1)}, bf16[32,2048]{1,0:T(8,128)(2,1)S(1)}, u32[]{:S(2)}, u32[]{:S(2)}) collective-permute-start(bf16[32,2048]{1,0:T(8,128)(2,1)S(1)} %get-tuple-element.80), channel_id=1, source_target_pairs={{0,24},{8,16},{16,8},{24,0},{1,25},{9,17},{17,9},{25,1},{2,26},{10... | collective-permute-start | bytes 393224 | tf_op jit(solution)/shard_map/ppermute | solution.py:336
  33.5 3.5 %collective-permute-start.18 = (bf16[240,256]{1,0:T(8,128)(2,1)S(1)}, bf16[240,256]{1,0:T(8,128)(2,1)S(1)}, u32[]{:S(2)}, u32[]{:S(2)}) collective-permute-start(bf16[240,256]{1,0:T(8,128)(2,1)S(1)} %get-tuple-element.90), channel_id=1, source_target_pairs={{0,1},{1,0},{2,3},{3,2},{4,5},{5,4},{6,7},{7,6},{8,9},{9,8},{10,11... | collective-permute-start | bytes 368648 | tf_op jit(solution)/shard_map/ppermute | solution.py:336
  33.6 3.4 %collective-permute-start.15 = (bf16[192,256]{1,0:T(8,128)(2,1)S(1)}, bf16[192,256]{1,0:T(8,128)(2,1)S(1)}, u32[]{:S(2)}, u32[]{:S(2)}) collective-permute-start(bf16[192,256]{1,0:T(8,128)(2,1)S(1)} %get-tuple-element.87), channel_id=1, source_target_pairs={{0,1},{1,0},{2,3},{3,2},{4,5},{5,4},{6,7},{7,6},{8,9},{9,8},{10,11... | collective-permute-start | bytes 294920 | tf_op jit(solution)/shard_map/ppermute | solution.py:336
  34.8 0.7 %copy-start.3 = (s32[64]{0:T(128)S(1)}, s32[64]{0:T(128)}, u32[]{:S(2)}) copy-start(s32[64]{0:T(128)} %assign_ref.1) | copy-start | bytes 772
  34.8 2.2 %collective-permute-start.16 = (bf16[192,256]{1,0:T(8,128)(2,1)S(1)}, bf16[192,256]{1,0:T(8,128)(2,1)S(1)}, u32[]{:S(2)}, u32[]{:S(2)}) collective-permute-start(bf16[192,256]{1,0:T(8,128)(2,1)S(1)} %get-tuple-element.88), channel_id=1, source_target_pairs={{0,1},{1,0},{2,3},{3,2},{4,5},{5,4},{6,7},{7,6},{8,9},{9,8},{10,11... | collective-permute-start | bytes 294920 | tf_op jit(solution)/shard_map/ppermute | solution.py:336
  34.8 2.2 %collective-permute-start.17 = (bf16[192,256]{1,0:T(8,128)(2,1)S(1)}, bf16[192,256]{1,0:T(8,128)(2,1)S(1)}, u32[]{:S(2)}, u32[]{:S(2)}) collective-permute-start(bf16[192,256]{1,0:T(8,128)(2,1)S(1)} %get-tuple-element.89), channel_id=1, source_target_pairs={{0,1},{1,0},{2,3},{3,2},{4,5},{5,4},{6,7},{7,6},{8,9},{9,8},{10,11... | collective-permute-start | bytes 294920 | tf_op jit(solution)/shard_map/ppermute | solution.py:336

commit v5 on v4

--- a/solution.py
+++ b/solution.py
@@ -131,7 +131,7 @@
     g_ref, gh_ref, ht_ref, gg_ref, bg_ref, direct_ref = refs[n_tower:]
     me = lax.axis_index("tower")
     rows = pieces[0].shape[0]
-    for k, piece in enumerate(pieces):
+    for k, piece in zip(range(len(pieces) - 1, -1, -1), pieces):
         g_ref[pl.ds(pl.multiple_of((me ^ k) * rows, rows), rows), :] = piece[...]
     gh_ref[...] = backward_rows(
         x_ref, g_ref[...], low_ref, wu_ref, wo_ref, gg_ref, bg_ref, ht_ref, factor_ref, direct_ref
@@ -370,9 +370,10 @@
         [out_grad],
         "cut_columns",
         48 * MIB,
-        1,
-    )
-    pieces = [pieces[0]] + [across(pieces[k], "tower", k) for k in range(1, n_tower)]
+        10**9,
+    )
+    received = [across(pieces[k], "tower", k) for k in range(n_tower - 1, 0, -1)]
+    pieces = [pieces[0]] + received[::-1]
     wd, wu, wo, x_own, low_own, cr_own, factor = call(
         forward_kernel,
         [sds(w.shape, BF16) for w in (w_down, w_up, w_out)] + [wide, low, wide, sds((n, width), F32)],
@@ -388,7 +389,7 @@
         [sds((n, out), BF16), low, tall, wide, row, sds((n, width), F32)],
         [],
         [VMEM] * (5 + n_tower),
-        [wu, wo, x_own, low_own, factor, *pieces],
+        [wu, wo, x_own, low_own, factor, *pieces[::-1]],
         "backward_own",
         cost=1,
     )

time: 40.5 us -> 39.5 us (0.975)
  local copies, waits for them, and re-layouts: 2.03 us -> 0.99 us
    unnamed x8, local copies, waits for them, and re-layouts: 2.03 us -> 0.99 us
    ppermute x15, waiting for transfers between devices: 4.89 us -> 5.92 us  [across(): return lax.ppermute(value, axis, xor_pairs(lax.axis_size(axis), k))]
    ppermute x1, waiting for transfers between devices: 2.32 us -> 1.37 us  [paired_body(): from_second = lax.ppermute(second_sum, 'shard', second)]
    ppermute x1, waiting for transfers between devices: 2.15 us -> 1.67 us  [paired_body(): from_first = lax.ppermute(first, 'shard', outer)]
    ppermute x1, starting transfers between devices: 1.18 us -> 1.63 us  [paired_body(): from_second = lax.ppermute(second_sum, 'shard', second)]
  transfers between devices with their start and end apart: 19 -> 19, of which waited for: 7 -> 8; matrix products, arithmetic and copies ran while one was open for 0% -> 0% of each run, Pallas kernels for 24% -> 25%
where the time goes in v5:
time: 39.5 us; the launch traced here: 39.3 us
  starting transfers between devices  17.7 us (45%)
  Pallas kernels  10.8 us (27%)
  waiting for transfers between devices  8.96 us (23%)
  local copies, waits for them, and re-layouts  0.99 us (3%)
  between operations  0.8 us (2%)
    ppermute x15, starting transfers between devices, across(): return lax.ppermute(value, axis, xor_pairs(lax.axis_size(axis), k))  13.7 us
    pallas_call x13, Pallas kernels, call(): pl.pallas_call(kernel, out_shape=outs, in_specs=[pl.BlockSpec(memory_spac...  10.8 us
    ppermute x15, waiting for transfers between devices, across(): return lax.ppermute(value, axis, xor_pairs(lax.axis_size(axis), k))  5.92 us
    ppermute x1, waiting for transfers between devices, paired_body(): from_first = lax.ppermute(first, 'shard', outer)  1.67 us
    ppermute x1, starting transfers between devices, paired_body(): from_second = lax.ppermute(second_sum, 'shard', second)  1.63 us
    ppermute x1, starting transfers between devices, paired_body(): from_first = lax.ppermute(first, 'shard', outer)  1.41 us
    ppermute x1, waiting for transfers between devices, paired_body(): from_second = lax.ppermute(second_sum, 'shard', second)  1.37 us
    unnamed x8, local copies, waits for them, and re-layouts  0.99 us
  transfers between devices with their start and end apart: 19, of which 8 were waited for; matrix products, arithmetic and copies ran while one was open for 0% of the time, Pallas kernels for 25%

profile of v5, /device:TPU:0, one launch (start us, length us, event | category | flops | bytes accessed | tf_op | source)
XLA Modules:
  0.0 39.3 jit_solution(837694267841955990)
XLA Ops:
  0.6 0.5 %collective-permute-start.3 = (bf16[128,2048]{1,0:T(8,128)(2,1)}, bf16[128,2048]{1,0:T(8,128)(2,1)S(1)}, u32[]{:S(2)}, u32[]{:S(2)}) collective-permute-start(bf16[128,2048]{1,0:T(8,128)(2,1)} %bitcast.5), channel_id=1, source_target_pairs={{0,1},{1,0},{2,4},{3,5},{4,2},{5,3},{6,7},{7,6},{8,9},{9,8},{10,12... | collective-permute-start | bytes 1572872 | tf_op jit(solution)/shard_map/ppermute | solution.py:364
  1.2 4.1 %collective-permute-start.5 = (bf16[128,2048]{1,0:T(8,128)(2,1)}, bf16[128,2048]{1,0:T(8,128)(2,1)S(1)}, u32[]{:S(2)}, u32[]{:S(2)}) collective-permute-start(bf16[128,2048]{1,0:T(8,128)(2,1)} %bitcast.6), channel_id=1, source_target_pairs={{0,2},{1,3},{2,0},{3,1},{4,6},{5,7},{6,4},{7,5},{8,10},{9,11},{10,... | collective-permute-start | bytes 1572872 | tf_op jit(solution)/shard_map/ppermute | solution.py:336
  5.3 0.8 %copy-done.3 = bf16[32,1024]{1,0:T(8,128)(2,1)S(1)} copy-done((bf16[32,1024]{1,0:T(8,128)(2,1)S(1)}, bf16[32,1024]{1,0:T(8,128)(2,1)}, u32[]{:S(2)}) %copy-start.3) | copy-done | bytes 65560
  6.2 2.5 %collective-permute-start = (bf16[32,256]{1,0:T(8,128)(2,1)S(1)}, bf16[32,256]{1,0:T(8,128)(2,1)S(1)}, u32[]{:S(2)}, u32[]{:S(2)}) collective-permute-start(bf16[32,256]{1,0:T(8,128)(2,1)S(1)} %get-tuple-element.54), channel_id=1, source_target_pairs={{0,24},{8,16},{16,8},{24,0},{1,25},{9,17},{17,9},{25,1},{2,26},{10... | collective-permute-start | bytes 49160 | tf_op jit(solution)/shard_map/ppermute | solution.py:336
  8.7 0.5 %collective-permute-start.1 = (bf16[32,256]{1,0:T(8,128)(2,1)S(1)}, bf16[32,256]{1,0:T(8,128)(2,1)S(1)}, u32[]{:S(2)}, u32[]{:S(2)}) collective-permute-start(bf16[32,256]{1,0:T(8,128)(2,1)S(1)} %get-tuple-element.55), channel_id=1, source_target_pairs={{0,16},{8,24},{16,0},{24,8},{1,17},{9,25},{17,1},{25,9},{2,18},{10... | collective-permute-start | bytes 49160 | tf_op jit(solution)/shard_map/ppermute | solution.py:336
  9.2 0.5 %collective-permute-start.2 = (bf16[32,256]{1,0:T(8,128)(2,1)S(1)}, bf16[32,256]{1,0:T(8,128)(2,1)S(1)}, u32[]{:S(2)}, u32[]{:S(2)}) collective-permute-start(bf16[32,256]{1,0:T(8,128)(2,1)S(1)} %get-tuple-element.56), channel_id=1, source_target_pairs={{0,8},{8,0},{16,24},{24,16},{1,9},{9,1},{17,25},{25,17},{2,10},{10... | collective-permute-start | bytes 49160 | tf_op jit(solution)/shard_map/ppermute | solution.py:336
  9.8 2.1 %forward_own.1 = (bf16[2048,256]{1,0:T(8,128)(2,1)S(1)}, bf16[256,2048]{1,0:T(8,128)(2,1)S(1)}, bf16[2048,256]{1,0:T(8,128)(2,1)S(1)}, bf16[128,2048]{1,0:T(8,12...) custom-call(bf16[2048,256]{1,0:T(8,128)(2,1)} %bitcast.8, ...), custom_call_target="tpu_custom_call" | custom-call | flops 1 | bytes 1 | tf_op jit(solution)/shard_map/forward_own/pallas_call | solution.py:39
  11.9 0.5 %collective-permute-done.1.refs_1_ = bf16[32,256]{1,0:T(8,128)(2,1)S(1)} collective-permute-done((bf16[32,256]{1,0:T(8,128)(2,1)S(1)}, bf16[32,256]{1,0:T(8,128)(2,1)S(1)}, u32[]{:S(2)}, u32[]{:S(2)}) %collective-permute-start.1) | collective-permute-done | bytes 16416 | tf_op jit(solution)/shard_map/ppermute | solution.py:336
  12.5 0.5 %collective-permute-done.2.refs_2_ = bf16[32,256]{1,0:T(8,128)(2,1)S(1)} collective-permute-done((bf16[32,256]{1,0:T(8,128)(2,1)S(1)}, bf16[32,256]{1,0:T(8,128)(2,1)S(1)}, u32[]{:S(2)}, u32[]{:S(2)}) %collective-permute-start.2) | collective-permute-done | bytes 16416 | tf_op jit(solution)/shard_map/ppermute | solution.py:336
  13.0 1.1 %backward_own.1 = (bf16[128,256]{1,0:T(8,128)(2,1)S(1)}, bf16[128,256]{1,0:T(8,128)(2,1)S(1)}, bf16[768,128]{1,0:T(8,128)(2,1)S(1)}, bf16[128,2048]{1,0:T(8,128)...) custom-call(bf16[256,2048]{1,0:T(8,128)(2,1)S(1)} %get-tuple-element.49.wu_ref, ...), custom_call_target="tpu_custom_call" | custom-call | flops 1 | bytes 1 | tf_op jit(solution)/shard_map/backward_own/pallas_call | solution.py:39
  14.1 0.6 %first_sums.1 = (f32[784,256]{1,0:T(8,128)S(1)}, bf16[784,256]{1,0:T(8,128)(2,1)S(1)}) custom-call(bf16[128,2048]{1,0:T(8,128)(2,1)S(1)} %get-tuple-element.51.x_ref.x_own.refs_0_, bf16[128,2048]{1,0:T(8,128)(2,1)S(1)} %get-tuple-element.61.gg_own.refs_1_, bf16[128,2048]{1,0:T(8,128)(2,1)S(1)} %get-tuple-element.62.cr_own.refs_2_, ...), custom_call_target="tpu_custom_call" | custom-call | flops 1 | bytes 1 | tf_op jit(solution)/shard_map/first_sums/pallas_call | solution.py:39
  14.7 0.5 %collective-permute-start.7 = (bf16[128,256]{1,0:T(8,128)(2,1)S(1)}, bf16[128,256]{1,0:T(8,128)(2,1)S(1)}, u32[]{:S(2)}, u32[]{:S(2)}) collective-permute-start(bf16[128,256]{1,0:T(8,128)(2,1)S(1)} %get-tuple-element.68), channel_id=1, source_target_pairs={{0,1},{1,0},{2,4},{3,5},{4,2},{5,3},{6,7},{7,6},{8,9},{9,8},{10,12... | collective-permute-start | bytes 196616 | tf_op jit(solution)/shard_map/ppermute | solution.py:397
  15.2 0.7 %collective-permute-start.6 = (bf16[128,256]{1,0:T(8,128)(2,1)S(1)}, bf16[128,256]{1,0:T(8,128)(2,1)S(1)}, u32[]{:S(2)}, u32[]{:S(2)}) collective-permute-start(bf16[128,256]{1,0:T(8,128)(2,1)S(1)} %get-tuple-element.68), channel_id=1, source_target_pairs={{0,2},{1,3},{2,0},{3,1},{4,6},{5,7},{6,4},{7,5},{8,10},{9,11},{10,... | collective-permute-start | bytes 196616 | tf_op jit(solution)/shard_map/ppermute | solution.py:336
  16.0 0.5 %collective-permute-done.4.refs_0_ = bf16[784,256]{1,0:T(8,128)(2,1)S(1)} collective-permute-done((bf16[784,256]{1,0:T(8,128)(2,1)S(1)}, bf16[784,256]{1,0:T(8,128)(2,1)S(1)}, u32[]{:S(2)}, u32[]{:S(2)}) %collective-permute-start.4) | collective-permute-done | bytes 401440 | tf_op jit(solution)/shard_map/ppermute | solution.py:336
  16.6 1.4 %collective-permute-start.13 = (bf16[784,256]{1,0:T(8,128)(2,1)S(1)}, bf16[784,256]{1,0:T(8,128)(2,1)S(1)}, u32[]{:S(2)}, u32[]{:S(2)}) collective-permute-start(bf16[784,256]{1,0:T(8,128)(2,1)S(1)} %join_cores.2), channel_id=1, source_target_pairs={{0,6},{1,7},{2,3},{3,2},{4,5},{5,4},{6,0},{7,1},{8,14},{9,15},{10,... | collective-permute-start | bytes 1204232 | tf_op jit(solution)/shard_map/ppermute | solution.py:402
  18.0 1.5 %collective-permute-done.6.g_ref = bf16[128,256]{1,0:T(8,128)(2,1)S(1)} collective-permute-done((bf16[128,256]{1,0:T(8,128)(2,1)S(1)}, bf16[128,256]{1,0:T(8,128)(2,1)S(1)}, u32[]{:S(2)}, u32[]{:S(2)}) %collective-permute-start.6) | collective-permute-done | bytes 65568 | tf_op jit(solution)/shard_map/ppermute | solution.py:336
  19.5 0.8 %forward_other.1 = (bf16[128,256]{1,0:T(8,128)(2,1)S(1)}, bf16[128,2048]{1,0:T(8,128)(2,1)S(1)}) custom-call(bf16[128,2048]{1,0:T(8,128)(2,1)S(1)} %collective-permute-done.5.x_ref, bf16[2048,256]{1,0:T(8,128)(2,1)S(1)} %get-tuple-element.48.wd_ref, bf16[256,2048]{1,0:T(8,128)(2,1)S(1)} %get-tuple-element.49.wu_ref, f32[1,2048]{1,0:T(1,128)S(1)} %copy-done.1), custom_call_target="tpu_custom_call" | custom-call | flops 1000000000 | bytes 1 | tf_op jit(solution)/shard_map/forward_other/pallas_call | solution.py:39
  20.3 1.0 %second_sums.1 = (bf16[128,2048]{1,0:T(8,128)(2,1)S(1)}, bf16[768,128]{1,0:T(8,128)(2,1)S(1)}, f32[1,2048]{1,0:T(1,128)S(1)}, f32[784,256]{1,0:T(8,128)S(1)}, bf...) custom-call(bf16[256,2048]{1,0:T(8,128)(2,1)S(1)} %get-tuple-element.49.wu_ref, ...), custom_call_target="tpu_custom_call" | custom-call | flops 1000000000 | bytes 1 | tf_op jit(solution)/shard_map/second_sums/pallas_call | solution.py:39
  21.4 0.5 %collective-permute-start.8 = (bf16[384,256]{1,0:T(8,128)(2,1)S(1)}, bf16[384,256]{1,0:T(8,128)(2,1)S(1)}, u32[]{:S(2)}, u32[]{:S(2)}) collective-permute-start(bf16[384,256]{1,0:T(8,128)(2,1)S(1)} %get-tuple-element.74), channel_id=1, source_target_pairs={{0,1},{1,0},{2,3},{3,2},{4,5},{5,4},{6,7},{7,6},{8,9},{9,8},{10,11... | collective-permute-start | bytes 589832 | tf_op jit(solution)/shard_map/ppermute | solution.py:336
  21.9 1.2 %collective-permute-done.8.refs_0_ = bf16[384,256]{1,0:T(8,128)(2,1)S(1)} collective-permute-done((bf16[384,256]{1,0:T(8,128)(2,1)S(1)}, bf16[384,256]{1,0:T(8,128)(2,1)S(1)}, u32[]{:S(2)}, u32[]{:S(2)}) %collective-permute-start.8) | collective-permute-done | bytes 196640 | tf_op jit(solution)/shard_map/ppermute | solution.py:336
  23.2 1.6 %collective-permute-start.14 = (bf16[784,256]{1,0:T(8,128)(2,1)S(1)}, bf16[784,256]{1,0:T(8,128)(2,1)S(1)}, u32[]{:S(2)}, u32[]{:S(2)}) collective-permute-start(bf16[784,256]{1,0:T(8,128)(2,1)S(1)} %join_cores.3), channel_id=1, source_target_pairs={{0,4},{1,5},{2,0},{3,1},{4,6},{5,7},{6,2},{7,3},{8,12},{9,13},{10,... | collective-permute-start | bytes 1204232 | tf_op jit(solution)/shard_map/ppermute | solution.py:419
  24.9 0.5 %grad_inputs.1 = (bf16[32,2048]{1,0:T(8,128)(2,1)S(1)}, bf16[32,2048]{1,0:T(8,128)(2,1)S(1)}, bf16[32,2048]{1,0:T(8,128)(2,1)S(1)}, bf16[32,2048]{1,0:T(8,128)(2,1)S(1)}) custom-call(bf16[2048,256]{1,0:T(8,128)(2,1)S(1)} %get-tuple-element.48.wd_ref, bf16[128,256]{1,0:T(8,128)(2,1)S(1)} %get-tuple-element.58.gh_ref, f32[128,2048]{1,0:T(8,128)S(1)} %get-tuple-element.76.direct_ref), custom_call_target="tpu_custom_call" | custom-call | flops 1 | bytes 1 | tf_op jit(solution)/shard_map/grad_inputs/pallas_call | solution.py:39
  25.4 1.6 %collective-permute-start.10 = (bf16[32,2048]{1,0:T(8,128)(2,1)S(1)}, bf16[32,2048]{1,0:T(8,128)(2,1)S(1)}, u32[]{:S(2)}, u32[]{:S(2)}) collective-permute-start(bf16[32,2048]{1,0:T(8,128)(2,1)S(1)} %get-tuple-element.78), channel_id=1, source_target_pairs={{0,8},{8,0},{16,24},{24,16},{1,9},{9,1},{17,25},{25,17},{2,10},{10... | collective-permute-start | bytes 393224 | tf_op jit(solution)/shard_map/ppermute | solution.py:336
  27.0 1.5 %collective-permute-start.11 = (bf16[32,2048]{1,0:T(8,128)(2,1)S(1)}, bf16[32,2048]{1,0:T(8,128)(2,1)S(1)}, u32[]{:S(2)}, u32[]{:S(2)}) collective-permute-start(bf16[32,2048]{1,0:T(8,128)(2,1)S(1)} %get-tuple-element.79), channel_id=1, source_target_pairs={{0,16},{8,24},{16,0},{24,8},{1,17},{9,25},{17,1},{25,9},{2,18},{10... | collective-permute-start | bytes 393224 | tf_op jit(solution)/shard_map/ppermute | solution.py:336
  28.9 1.7 %collective-permute-done.13.refs_10_.first_ref = bf16[784,256]{1,0:T(8,128)(2,1)S(1)} collective-permute-done((bf16[784,256]{1,0:T(8,128)(2,1)S(1)}, bf16[784,256]{1,0:T(8,128)(2,1)S(1)}, u32[]{:S(2)}, u32[]{:S(2)}) %collective-permute-start.13) | collective-permute-done | bytes 401440 | tf_op jit(solution)/shard_map/ppermute | solution.py:402
  30.6 1.9 %near_sums.1 = (f32[816,256]{1,0:T(8,128)S(1)}, bf16[192,256]{1,0:T(8,128)(2,1)S(1)}, bf16[192,256]{1,0:T(8,128)(2,1)S(1)}, bf16[192,256]{1,0:T(8,128)(2,1)S(1)}, bf16[240,256]{1,0:T(8,128)(2,1)S(1)}) custom-call(bf16[256,2048]{1,0:T(8,128)(2,1)S(1)} %get-tuple-element.49.wu_ref, bf16[2048,256]{1,0:T(8,128)(2,1)S(1)} %get-tuple-element.50.wo_ref, ...), custom_call_target="tpu_custom_call" | custom-call | flops 1000000000 | bytes 1 | tf_op jit(solution)/shard_map/near_sums/pallas_call | solution.py:39
  32.7 0.5 %collective-permute-start.15 = (bf16[192,256]{1,0:T(8,128)(2,1)S(1)}, bf16[192,256]{1,0:T(8,128)(2,1)S(1)}, u32[]{:S(2)}, u32[]{:S(2)}) collective-permute-start(bf16[192,256]{1,0:T(8,128)(2,1)S(1)} %get-tuple-element.87), channel_id=1, source_target_pairs={{0,1},{1,0},{2,3},{3,2},{4,5},{5,4},{6,7},{7,6},{8,9},{9,8},{10,11... | collective-permute-start | bytes 294920 | tf_op jit(solution)/shard_map/ppermute | solution.py:336
  33.1 1.7 %collective-permute-done.11.refs_2_ = bf16[32,2048]{1,0:T(8,128)(2,1)S(1)} collective-permute-done((bf16[32,2048]{1,0:T(8,128)(2,1)S(1)}, bf16[32,2048]{1,0:T(8,128)(2,1)S(1)}, u32[]{:S(2)}, u32[]{:S(2)}) %collective-permute-start.11) | collective-permute-done | bytes 131104 | tf_op jit(solution)/shard_map/ppermute | solution.py:336
  34.8 0.5 %collective-permute-start.17 = (bf16[192,256]{1,0:T(8,128)(2,1)S(1)}, bf16[192,256]{1,0:T(8,128)(2,1)S(1)}, u32[]{:S(2)}, u32[]{:S(2)}) collective-permute-start(bf16[192,256]{1,0:T(8,128)(2,1)S(1)} %get-tuple-element.89), channel_id=1, source_target_pairs={{0,1},{1,0},{2,3},{3,2},{4,5},{5,4},{6,7},{7,6},{8,9},{9,8},{10,11... | collective-permute-start | bytes 294920 | tf_op jit(solution)/shard_map/ppermute | solution.py:336
  35.5 1.5 %place_features.1 = bf16[32,8192]{1,0:T(8,128)(2,1)} custom-call(s32[64]{0:T(128)S(1)} %copy-done.2, bf16[32,2048]{1,0:T(8,128)(2,1)S(1)} %get-tuple-element.77.refs_0_, bf16[32,2048]{1,0:T(8,128)(2,1)S(1)} %collective-permute-done.10.refs_1_, bf16[32,2048]{1,0:T(8,128)(2,1)S(1)} %collective-permute-done.11.refs_2_, ...), custom_call_target="tpu_custom_call" | custom-call | flops 1 | bytes 1 | tf_op jit(solution)/shard_map/place_features/pallas_call | solution.py:39
  37.0 1.4 %collective-permute-done.14.second_ref = bf16[784,256]{1,0:T(8,128)(2,1)S(1)} collective-permute-done((bf16[784,256]{1,0:T(8,128)(2,1)S(1)}, bf16[784,256]{1,0:T(8,128)(2,1)S(1)}, u32[]{:S(2)}, u32[]{:S(2)}) %collective-permute-start.14) | collective-permute-done | bytes 401440 | tf_op jit(solution)/shard_map/ppermute | solution.py:419
  38.4 1.0 %add_up.1 = (f32[96,2048]{1,0:T(8,128)}, f32[1,2048]{1,0:T(1,128)}) custom-call(f32[816,256]{1,0:T(8,128)S(1)} %get-tuple-element.86.keep_ref, bf16[784,256]{1,0:T(8,128)(2,1)S(1)} %collective-permute-done.13.refs_10_.first_ref, bf16[784,256]{1,0:T(8,128)(2,1)S(1)} %collective-permute-done.14.second_ref, ...), custom_call_target="tpu_custom_call" | custom-call | flops 10000000000 | bytes 1 | tf_op jit(solution)/shard_map/add_up/pallas_call | solution.py:39
  (27 shorter events, 1.2 us)
Async XLA Ops:
  0.6 9.1 %copy-start = (bf16[1,128,2048]{2,1,0:T(8,128)(2,1)S(1)}, bf16[1,128,2048]{2,1,0:T(8,128)(2,1)}, u32[]{:S(2)}) copy-start(bf16[1,128,2048]{2,1,0:T(8,128)(2,1)} %param.8) | copy-start | bytes 1572868
  0.6 17.3 %collective-permute-start.3 = (bf16[128,2048]{1,0:T(8,128)(2,1)}, bf16[128,2048]{1,0:T(8,128)(2,1)S(1)}, u32[]{:S(2)}, u32[]{:S(2)}) collective-permute-start(bf16[128,2048]{1,0:T(8,128)(2,1)} %bitcast.5), channel_id=1, source_target_pairs={{0,1},{1,0},{2,4},{3,5},{4,2},{5,3},{6,7},{7,6},{8,9},{9,8},{10,12... | collective-permute-start | bytes 1572872 | tf_op jit(solution)/shard_map/ppermute | solution.py:364
  1.2 18.3 %collective-permute-start.5 = (bf16[128,2048]{1,0:T(8,128)(2,1)}, bf16[128,2048]{1,0:T(8,128)(2,1)S(1)}, u32[]{:S(2)}, u32[]{:S(2)}) collective-permute-start(bf16[128,2048]{1,0:T(8,128)(2,1)} %bitcast.6), channel_id=1, source_target_pairs={{0,2},{1,3},{2,0},{3,1},{4,6},{5,7},{6,4},{7,5},{8,10},{9,11},{10,... | collective-permute-start | bytes 1572872 | tf_op jit(solution)/shard_map/ppermute | solution.py:336
  5.3 0.8 %copy-start.3 = (bf16[32,1024]{1,0:T(8,128)(2,1)S(1)}, bf16[32,1024]{1,0:T(8,128)(2,1)}, u32[]{:S(2)}) copy-start(bf16[32,1024]{1,0:T(8,128)(2,1)} %grad_ref.1) | copy-start | bytes 196612
  6.2 3.6 %copy-start.1 = (f32[1,2048]{1,0:T(1,128)S(1)}, f32[1,2048]{1,0:T(1,128)}, u32[]{:S(2)}) copy-start(f32[1,2048]{1,0:T(1,128)} %bias_ref.5) | copy-start | bytes 24580
  6.2 5.7 %collective-permute-start = (bf16[32,256]{1,0:T(8,128)(2,1)S(1)}, bf16[32,256]{1,0:T(8,128)(2,1)S(1)}, u32[]{:S(2)}, u32[]{:S(2)}) collective-permute-start(bf16[32,256]{1,0:T(8,128)(2,1)S(1)} %get-tuple-element.54), channel_id=1, source_target_pairs={{0,24},{8,16},{16,8},{24,0},{1,25},{9,17},{17,9},{25,1},{2,26},{10... | collective-permute-start | bytes 49160 | tf_op jit(solution)/shard_map/ppermute | solution.py:336
  8.7 3.7 %collective-permute-start.1 = (bf16[32,256]{1,0:T(8,128)(2,1)S(1)}, bf16[32,256]{1,0:T(8,128)(2,1)S(1)}, u32[]{:S(2)}, u32[]{:S(2)}) collective-permute-start(bf16[32,256]{1,0:T(8,128)(2,1)S(1)} %get-tuple-element.55), channel_id=1, source_target_pairs={{0,16},{8,24},{16,0},{24,8},{1,17},{9,25},{17,1},{25,9},{2,18},{10... | collective-permute-start | bytes 49160 | tf_op jit(solution)/shard_map/ppermute | solution.py:336
  9.2 3.7 %collective-permute-start.2 = (bf16[32,256]{1,0:T(8,128)(2,1)S(1)}, bf16[32,256]{1,0:T(8,128)(2,1)S(1)}, u32[]{:S(2)}, u32[]{:S(2)}) collective-permute-start(bf16[32,256]{1,0:T(8,128)(2,1)S(1)} %get-tuple-element.56), channel_id=1, source_target_pairs={{0,8},{8,0},{16,24},{24,16},{1,9},{9,1},{17,25},{25,17},{2,10},{10... | collective-permute-start | bytes 49160 | tf_op jit(solution)/shard_map/ppermute | solution.py:336
  14.7 1.8 %collective-permute-start.4 = (bf16[784,256]{1,0:T(8,128)(2,1)S(1)}, bf16[784,256]{1,0:T(8,128)(2,1)S(1)}, u32[]{:S(2)}, u32[]{:S(2)}) collective-permute-start(bf16[784,256]{1,0:T(8,128)(2,1)S(1)} %get-tuple-element.65), channel_id=1, source_target_pairs={{0,1},{1,0},{2,3},{3,2},{4,5},{5,4},{6,7},{7,6},{8,9},{9,8},{10,11... | collective-permute-start | bytes 1204232 | tf_op jit(solution)/shard_map/ppermute | solution.py:336
  14.7 5.6 %collective-permute-start.7 = (bf16[128,256]{1,0:T(8,128)(2,1)S(1)}, bf16[128,256]{1,0:T(8,128)(2,1)S(1)}, u32[]{:S(2)}, u32[]{:S(2)}) collective-permute-start(bf16[128,256]{1,0:T(8,128)(2,1)S(1)} %get-tuple-element.68), channel_id=1, source_target_pairs={{0,1},{1,0},{2,4},{3,5},{4,2},{5,3},{6,7},{7,6},{8,9},{9,8},{10,12... | collective-permute-start | bytes 196616 | tf_op jit(solution)/shard_map/ppermute | solution.py:397
  15.2 4.3 %collective-permute-start.6 = (bf16[128,256]{1,0:T(8,128)(2,1)S(1)}, bf16[128,256]{1,0:T(8,128)(2,1)S(1)}, u32[]{:S(2)}, u32[]{:S(2)}) collective-permute-start(bf16[128,256]{1,0:T(8,128)(2,1)S(1)} %get-tuple-element.68), channel_id=1, source_target_pairs={{0,2},{1,3},{2,0},{3,1},{4,6},{5,7},{6,4},{7,5},{8,10},{9,11},{10,... | collective-permute-start | bytes 196616 | tf_op jit(solution)/shard_map/ppermute | solution.py:336
  16.6 14.0 %collective-permute-start.13 = (bf16[784,256]{1,0:T(8,128)(2,1)S(1)}, bf16[784,256]{1,0:T(8,128)(2,1)S(1)}, u32[]{:S(2)}, u32[]{:S(2)}) collective-permute-start(bf16[784,256]{1,0:T(8,128)(2,1)S(1)} %join_cores.2), channel_id=1, source_target_pairs={{0,6},{1,7},{2,3},{3,2},{4,5},{5,4},{6,0},{7,1},{8,14},{9,15},{10,... | collective-permute-start | bytes 1204232 | tf_op jit(solution)/shard_map/ppermute | solution.py:402
  21.3 1.8 %collective-permute-start.9 = (bf16[400,256]{1,0:T(8,128)(2,1)S(1)}, bf16[400,256]{1,0:T(8,128)(2,1)S(1)}, u32[]{:S(2)}, u32[]{:S(2)}) collective-permute-start(bf16[400,256]{1,0:T(8,128)(2,1)S(1)} %get-tuple-element.75), channel_id=1, source_target_pairs={{0,1},{1,0},{2,3},{3,2},{4,5},{5,4},{6,7},{7,6},{8,9},{9,8},{10,11... | collective-permute-start | bytes 614408 | tf_op jit(solution)/shard_map/ppermute | solution.py:336
  21.4 1.7 %collective-permute-start.8 = (bf16[384,256]{1,0:T(8,128)(2,1)S(1)}, bf16[384,256]{1,0:T(8,128)(2,1)S(1)}, u32[]{:S(2)}, u32[]{:S(2)}) collective-permute-start(bf16[384,256]{1,0:T(8,128)(2,1)S(1)} %get-tuple-element.74), channel_id=1, source_target_pairs={{0,1},{1,0},{2,3},{3,2},{4,5},{5,4},{6,7},{7,6},{8,9},{9,8},{10,11... | collective-permute-start | bytes 589832 | tf_op jit(solution)/shard_map/ppermute | solution.py:336
  23.2 15.1 %collective-permute-start.14 = (bf16[784,256]{1,0:T(8,128)(2,1)S(1)}, bf16[784,256]{1,0:T(8,128)(2,1)S(1)}, u32[]{:S(2)}, u32[]{:S(2)}) collective-permute-start(bf16[784,256]{1,0:T(8,128)(2,1)S(1)} %join_cores.3), channel_id=1, source_target_pairs={{0,4},{1,5},{2,0},{3,1},{4,6},{5,7},{6,2},{7,3},{8,12},{9,13},{10,... | collective-permute-start | bytes 1204232 | tf_op jit(solution)/shard_map/ppermute | solution.py:419
  25.4 7.3 %collective-permute-start.10 = (bf16[32,2048]{1,0:T(8,128)(2,1)S(1)}, bf16[32,2048]{1,0:T(8,128)(2,1)S(1)}, u32[]{:S(2)}, u32[]{:S(2)}) collective-permute-start(bf16[32,2048]{1,0:T(8,128)(2,1)S(1)} %get-tuple-element.78), channel_id=1, source_target_pairs={{0,8},{8,0},{16,24},{24,16},{1,9},{9,1},{17,25},{25,17},{2,10},{10... | collective-permute-start | bytes 393224 | tf_op jit(solution)/shard_map/ppermute | solution.py:336
  27.0 7.9 %collective-permute-start.11 = (bf16[32,2048]{1,0:T(8,128)(2,1)S(1)}, bf16[32,2048]{1,0:T(8,128)(2,1)S(1)}, u32[]{:S(2)}, u32[]{:S(2)}) collective-permute-start(bf16[32,2048]{1,0:T(8,128)(2,1)S(1)} %get-tuple-element.79), channel_id=1, source_target_pairs={{0,16},{8,24},{16,0},{24,8},{1,17},{9,25},{17,1},{25,9},{2,18},{10... | collective-permute-start | bytes 393224 | tf_op jit(solution)/shard_map/ppermute | solution.py:336
  28.5 6.4 %collective-permute-start.12 = (bf16[32,2048]{1,0:T(8,128)(2,1)S(1)}, bf16[32,2048]{1,0:T(8,128)(2,1)S(1)}, u32[]{:S(2)}, u32[]{:S(2)}) collective-permute-start(bf16[32,2048]{1,0:T(8,128)(2,1)S(1)} %get-tuple-element.80), channel_id=1, source_target_pairs={{0,24},{8,16},{16,8},{24,0},{1,25},{9,17},{17,9},{25,1},{2,26},{10... | collective-permute-start | bytes 393224 | tf_op jit(solution)/shard_map/ppermute | solution.py:336
  32.6 4.4 %collective-permute-start.18 = (bf16[240,256]{1,0:T(8,128)(2,1)S(1)}, bf16[240,256]{1,0:T(8,128)(2,1)S(1)}, u32[]{:S(2)}, u32[]{:S(2)}) collective-permute-start(bf16[240,256]{1,0:T(8,128)(2,1)S(1)} %get-tuple-element.90), channel_id=1, source_target_pairs={{0,1},{1,0},{2,3},{3,2},{4,5},{5,4},{6,7},{7,6},{8,9},{9,8},{10,11... | collective-permute-start | bytes 368648 | tf_op jit(solution)/shard_map/ppermute | solution.py:336
  32.7 4.3 %collective-permute-start.15 = (bf16[192,256]{1,0:T(8,128)(2,1)S(1)}, bf16[192,256]{1,0:T(8,128)(2,1)S(1)}, u32[]{:S(2)}, u32[]{:S(2)}) collective-permute-start(bf16[192,256]{1,0:T(8,128)(2,1)S(1)} %get-tuple-element.87), channel_id=1, source_target_pairs={{0,1},{1,0},{2,3},{3,2},{4,5},{5,4},{6,7},{7,6},{8,9},{9,8},{10,11... | collective-permute-start | bytes 294920 | tf_op jit(solution)/shard_map/ppermute | solution.py:336
  34.8 0.7 %copy-start.2 = (s32[64]{0:T(128)S(1)}, s32[64]{0:T(128)}, u32[]{:S(2)}) copy-start(s32[64]{0:T(128)} %assign_ref.1) | copy-start | bytes 772
  34.8 2.2 %collective-permute-start.16 = (bf16[192,256]{1,0:T(8,128)(2,1)S(1)}, bf16[192,256]{1,0:T(8,128)(2,1)S(1)}, u32[]{:S(2)}, u32[]{:S(2)}) collective-permute-start(bf16[192,256]{1,0:T(8,128)(2,1)S(1)} %get-tuple-element.88), channel_id=1, source_target_pairs={{0,1},{1,0},{2,3},{3,2},{4,5},{5,4},{6,7},{7,6},{8,9},{9,8},{10,11... | collective-permute-start | bytes 294920 | tf_op jit(solution)/shard_map/ppermute | solution.py:336
  34.8 2.2 %collective-permute-start.17 = (bf16[192,256]{1,0:T(8,128)(2,1)S(1)}, bf16[192,256]{1,0:T(8,128)(2,1)S(1)}, u32[]{:S(2)}, u32[]{:S(2)}) collective-permute-start(bf16[192,256]{1,0:T(8,128)(2,1)S(1)} %get-tuple-element.89), channel_id=1, source_target_pairs={{0,1},{1,0},{2,3},{3,2},{4,5},{5,4},{6,7},{7,6},{8,9},{9,8},{10,11... | collective-permute-start | bytes 294920 | tf_op jit(solution)/shard_map/ppermute | solution.py:336

commit v6 on v5

--- a/solution.py
+++ b/solution.py
@@ -98,7 +98,7 @@
         forward_rows(x_ref, wd_ref, wu_ref, bias_ref, low_ref, cr_ref)
 
 
-def backward_rows(x_ref, g, low_ref, wu_ref, wo_ref, gg_ref, bg_ref, ht_ref, factor_ref, direct_ref):
+def backward_rows(x_ref, g, low_ref, wu_ref, wo_ref, gg_ref, bg_ref, ht_ref, gc_ref):
     rank = wu_ref.shape[0]
     grad_hidden = jnp.zeros((x_ref.shape[0], rank), F32)
     for c in column_chunks(x_ref.shape[1]):
@@ -109,8 +109,8 @@
         low = grad_gate.astype(BF16)
         gg_ref[:, c] = low
         grad_hidden += mm_nt(low, wu_ref[:, c])
-        if direct_ref is not None:
-            direct_ref[:, c] = grad_crossed * factor_ref[:, c]
+        if gc_ref is not None:
+            gc_ref[:, c] = grad_crossed.astype(BF16)
     grad_hidden = grad_hidden.astype(BF16)
     ht_ref[0:rank, :] = grad_hidden.T
     ht_ref[rank : 2 * rank, :] = low_ref[...].T
@@ -126,25 +126,26 @@
     copies[3].wait()
 
 
-def backward_kernel(n_tower, wu_ref, wo_ref, x_ref, low_ref, factor_ref, *refs):
+def backward_kernel(n_tower, wu_ref, wo_ref, x_ref, low_ref, *refs):
     pieces = refs[:n_tower]
-    g_ref, gh_ref, ht_ref, gg_ref, bg_ref, direct_ref = refs[n_tower:]
+    g_ref, gh_ref, ht_ref, gg_ref, bg_ref, gc_ref = refs[n_tower:]
     me = lax.axis_index("tower")
     rows = pieces[0].shape[0]
     for k, piece in zip(range(len(pieces) - 1, -1, -1), pieces):
         g_ref[pl.ds(pl.multiple_of((me ^ k) * rows, rows), rows), :] = piece[...]
     gh_ref[...] = backward_rows(
-        x_ref, g_ref[...], low_ref, wu_ref, wo_ref, gg_ref, bg_ref, ht_ref, factor_ref, direct_ref
-    )
-
-
-def inputs_kernel(n_tower, wd_ref, gh_ref, direct_ref, *refs):
+        x_ref, g_ref[...], low_ref, wu_ref, wo_ref, gg_ref, bg_ref, ht_ref, gc_ref
+    )
+
+
+def inputs_kernel(n_tower, wd_ref, gh_ref, gc_ref, factor_ref, *refs):
     pieces, gi_ref = refs[:n_tower], refs[n_tower]
     me = lax.axis_index("tower")
     rows = pieces[0].shape[0]
     grad_hidden = gh_ref[...]
     for c in column_chunks(gi_ref.shape[1]):
-        gi_ref[:, c] = (direct_ref[:, c] + mm_nt(grad_hidden, wd_ref[c, :])).astype(BF16)
+        direct = gc_ref[:, c].astype(F32) * factor_ref[:, c]
+        gi_ref[:, c] = (direct + mm_nt(grad_hidden, wd_ref[c, :])).astype(BF16)
     for k, piece in enumerate(pieces):
         piece[...] = gi_ref[pl.ds(pl.multiple_of((me ^ k) * rows, rows), rows), :]
 
@@ -213,11 +214,26 @@
 def first_kernel(x_own, gg_own, cr_own, ht_own, bg_own, keep_ref, *refs):
     send_refs, (lhs_ref, acc_ref) = refs[:-2], refs[-2:]
     outer = is_outer()
-
-    @pl.when(outer)
-    def _():
-        theirs, ours = products(6, 0, [(x_own, gg_own, cr_own, ht_own)], lhs_ref, acc_ref)
-        store_slabs(acc_ref, theirs, ours, [bg_own[...]], send_refs, keep_ref)
+    (send_ref,) = send_refs
+    block, n_slabs = acc_ref.shape[0] // 2, acc_ref.shape[1] // SLAB
+    shard = lax.axis_index("shard")
+    even = lax.rem(shard, 2) == 0
+    last = ht_own.shape[0] - 2 * block
+
+    for here, start, rhs_ref in ((shard < 2, last, cr_own), (outer & (shard >= 2), 0, x_own)):
+
+        @pl.when(here)
+        def _(start=start, rhs_ref=rhs_ref):
+            lhs = ht_own[start : start + 2 * block, :]
+            for j in range(n_slabs):
+                both = mm(lhs, rhs_ref[:, j * SLAB : (j + 1) * SLAB])
+                rows = slice(j * block, (j + 1) * block)
+                low, high = both[:block], both[block:]
+                send_ref[rows, :] = jnp.where(even, high, low).astype(BF16)
+                keep_ref[rows, :] = jnp.where(even, low, high)
+            rows = bias_rows(bg_own[...]).astype(BF16)
+            send_ref[-TILE:, :] = rows
+            keep_ref[-TILE:, :] = rows.astype(F32)
 
     @pl.when(jnp.logical_not(outer))
     def _():
@@ -239,7 +255,7 @@
 
     @pl.when(jnp.logical_not(outer))
     def _():
-        backward_rows(x_ref, g_ref[...], low_ref, wu_ref, wo_ref, gg_ref, bg_ref, ht_ref, None, None)
+        backward_rows(x_ref, g_ref[...], low_ref, wu_ref, wo_ref, gg_ref, bg_ref, ht_ref, None)
         theirs, ours = products(2, 0, [(x_ref, gg_ref, cr_ref, ht_ref)], lhs_ref, acc_ref)
         store_slabs(acc_ref, theirs, ours, [bg_ref[...]], send_refs, keep_ref)
 
@@ -247,7 +263,7 @@
 def near_kernel(wu_ref, wo_ref, x_ref, low_ref, cr_ref, g_ref, *refs):
     own, inner, bg_own, bg_inner, first_ref, keep_ref = refs[:4], refs[4:8], *refs[8:12]
     send_refs, (gg_ref, ht_ref, bg_ref, lhs_ref, acc_ref) = refs[12:-5], refs[-5:]
-    backward_rows(x_ref, g_ref[...], low_ref, wu_ref, wo_ref, gg_ref, bg_ref, ht_ref, None, None)
+    backward_rows(x_ref, g_ref[...], low_ref, wu_ref, wo_ref, gg_ref, bg_ref, ht_ref, None)
     theirs, ours = products(0, 0, [own, (x_ref, gg_ref, cr_ref, ht_ref), inner], lhs_ref, acc_ref)
     store_slabs(acc_ref, theirs, ours, [bg_own[...], bg_ref[...], bg_inner[...]], send_refs, keep_ref)
     sums = slice(0, first_ref.shape[0] - TILE)
@@ -268,32 +284,39 @@
     out_ref[-TILE:, :] = joined_bias(keep_ref[-TILE:, :] + recv_refs[-1][-TILE:, :].astype(F32), n_slabs)
 
 
-def final_kernel(scale, keep_ref, first_ref, second_ref, *refs):
-    near_refs, (out_ref, bg_out, total_ref, bg_ref, sem_ref) = refs[:-5], refs[-5:]
-    each = total_ref.shape[1] // SLAB // len(near_refs)
-    block, width = total_ref.shape
+def before_last_kernel(scale, keep_ref, first_ref, *refs):
+    near_refs, (sum_ref, near_bias_ref, far_bias_ref) = refs[:-3], refs[-3:]
+    block, width = sum_ref.shape
     n_slabs = width // SLAB
-    copies = []
-
-    def write(source, target, i):
-        copies.append(pltpu.make_async_copy(source, target, sem_ref.at[i]))
-        copies[-1].start()
-
+    each = n_slabs // len(near_refs)
     for j in range(n_slabs):
-        c, rows = slice(j * SLAB, (j + 1) * SLAB), slice(j * block, (j + 1) * block)
         at = j % each * block
-        total = keep_ref[rows, :] + near_refs[j // each][at : at + block, :].astype(F32)
-        total = total + second_ref[rows, :].astype(F32)
-        total_ref[:, c] = total * scale
-        write(total_ref.at[:, pl.ds(j * SLAB, SLAB)], out_ref.at[:, pl.ds(j * SLAB, SLAB)], j)
+        total = keep_ref[j * block : (j + 1) * block, :] + near_refs[j // each][at : at + block, :].astype(F32)
+        sum_ref[:, j * SLAB : (j + 1) * SLAB] = total * scale
     here = []
     for i in range(3):
         rows = slice(n_slabs * block + i * TILE, n_slabs * block + (i + 1) * TILE)
         at = each * block + i * TILE
         joined = joined_bias(keep_ref[rows, :] + near_refs[-1][at : at + TILE, :].astype(F32), n_slabs)
         here.append(bias_of(joined.astype(F32), n_slabs))
-    there = [bias_of(ref[-TILE:, :].astype(F32), n_slabs) for ref in (first_ref, second_ref)]
-    bg_ref[...] = (here[0] + here[1]) + ((here[2] + there[0]) + there[1])
+    near_bias_ref[...] = here[0] + here[1]
+    far_bias_ref[...] = here[2] + bias_of(first_ref[-TILE:, :].astype(F32), n_slabs)
+
+
+def final_kernel(scale, sum_ref, near_bias_ref, far_bias_ref, second_ref, out_ref, bg_out, total_ref, bg_ref, sem_ref):
+    block, width = total_ref.shape
+    n_slabs = width // SLAB
+    copies = []
+
+    def write(source, target, i):
+        copies.append(pltpu.make_async_copy(source, target, sem_ref.at[i]))
+        copies[-1].start()
+
+    for j in range(n_slabs):
+        c, rows = slice(j * SLAB, (j + 1) * SLAB), slice(j * block, (j + 1) * block)
+        total_ref[:, c] = sum_ref[:, c] + second_ref[rows, :].astype(F32) * scale
+        write(total_ref.at[:, pl.ds(j * SLAB, SLAB)], out_ref.at[:, pl.ds(j * SLAB, SLAB)], j)
+    bg_ref[...] = near_bias_ref[...] + (far_bias_ref[...] + bias_of(second_ref[-TILE:, :].astype(F32), n_slabs))
     write(bg_ref, bg_out, n_slabs)
     for copy in copies:
         copy.wait()
@@ -384,12 +407,12 @@
         VM * MIB,
         1,
     )
-    g_own, gh_own, ht_own, gg_own, bg_own, direct = call(
+    g_own, gh_own, ht_own, gg_own, bg_own, gc_own = call(
         functools.partial(backward_kernel, n_tower),
-        [sds((n, out), BF16), low, tall, wide, row, sds((n, width), F32)],
+        [sds((n, out), BF16), low, tall, wide, row, wide],
         [],
-        [VMEM] * (5 + n_tower),
-        [wu, wo, x_own, low_own, factor, *pieces[::-1]],
+        [VMEM] * (4 + n_tower),
+        [wu, wo, x_own, low_own, *pieces[::-1]],
         "backward_own",
         cost=1,
     )
@@ -421,8 +444,8 @@
         functools.partial(inputs_kernel, n_tower),
         [sds((top_rows, width), BF16)] * n_tower,
         [pltpu.VMEM((n, width), BF16)],
-        [VMEM] * 3,
-        [wd, gh_own, after(direct, second_sum)],
+        [VMEM] * 4,
+        [wd, gh_own, after(gc_own, second_sum), factor],
         "grad_inputs",
         cost=C4,
     )
@@ -449,16 +472,26 @@
         "place_features",
         cost=1,
     )
+    scale = 1.0 / math.sqrt(n * n_shard)
+    before_last = call(
+        functools.partial(before_last_kernel, scale),
+        [sds((block, width), F32), row, row],
+        [],
+        [VMEM] * (2 + len(near_others)),
+        [near_keep, from_first, *near_others],
+        "before_last",
+        cost=1,
+    )
     weight_grad, bias_grad = call(
-        functools.partial(final_kernel, 1.0 / math.sqrt(n * n_shard)),
+        functools.partial(final_kernel, scale),
         [sds((block, width), F32), row],
         [
             pltpu.VMEM((block, width), F32),
             pltpu.VMEM((1, width), F32),
             pltpu.SemaphoreType.DMA((width // SLAB + 1,)),
         ],
-        [VMEM] * (3 + len(near_others)),
-        [near_keep, from_first, from_second, *near_others],
+        [VMEM] * 4,
+        [*before_last, from_second],
         "add_up",
         out_space=HBM,
     )

time: 39.5 us -> 39.3 us (level)
  waiting for transfers between devices: 8.96 us -> 8.35 us
  starting transfers between devices: 17.7 us -> 18.2 us
    pallas_call x13 -> x14, Pallas kernels: 10.8 us -> 10.8 us  [call(): pl.pallas_call(kernel, out_shape=outs, in_specs=[pl.BlockSpec(memory_spac...]
where the time goes in v6:
time: 39.3 us; the launch traced here: 39.1 us
  starting transfers between devices  18.2 us (46%)
  Pallas kernels  10.8 us (27%)
  waiting for transfers between devices  8.35 us (21%)
  local copies, waits for them, and re-layouts  0.99 us (3%)
  between operations  0.81 us (2%)
    ppermute x15, starting transfers between devices, across(): return lax.ppermute(value, axis, xor_pairs(lax.axis_size(axis), k))  13.9 us
    pallas_call x14, Pallas kernels, call(): pl.pallas_call(kernel, out_shape=outs, in_specs=[pl.BlockSpec(memory_spac...  10.8 us
    ppermute x15, waiting for transfers between devices, across(): return lax.ppermute(value, axis, xor_pairs(lax.axis_size(axis), k))  5.89 us
    ppermute x1, starting transfers between devices, paired_body(): from_second = lax.ppermute(second_sum, 'shard', second)  1.87 us
    ppermute x1, waiting for transfers between devices, paired_body(): from_first = lax.ppermute(first, 'shard', outer)  1.46 us
    ppermute x1, starting transfers between devices, paired_body(): from_first = lax.ppermute(first, 'shard', outer)  1.42 us
    ppermute x1, waiting for transfers between devices, paired_body(): from_second = lax.ppermute(second_sum, 'shard', second)  1 us
    unnamed x8, local copies, waits for them, and re-layouts  0.99 us
  transfers between devices with their start and end apart: 19, of which 8 were waited for; matrix products, arithmetic and copies ran while one was open for 0% of the time, Pallas kernels for 25%

profile of v6, /device:TPU:0, one launch (start us, length us, event | category | flops | bytes accessed | tf_op | source)
XLA Modules:
  0.0 39.1 jit_solution(9616253289164770493)
XLA Ops:
  0.6 0.5 %collective-permute-start.3 = (bf16[128,2048]{1,0:T(8,128)(2,1)}, bf16[128,2048]{1,0:T(8,128)(2,1)S(1)}, u32[]{:S(2)}, u32[]{:S(2)}) collective-permute-start(bf16[128,2048]{1,0:T(8,128)(2,1)} %bitcast.5), channel_id=1, source_target_pairs={{0,1},{1,0},{2,4},{3,5},{4,2},{5,3},{6,7},{7,6},{8,9},{9,8},{10,12... | collective-permute-start | bytes 1572872 | tf_op jit(solution)/shard_map/ppermute | solution.py:387
  1.2 4.1 %collective-permute-start.5 = (bf16[128,2048]{1,0:T(8,128)(2,1)}, bf16[128,2048]{1,0:T(8,128)(2,1)S(1)}, u32[]{:S(2)}, u32[]{:S(2)}) collective-permute-start(bf16[128,2048]{1,0:T(8,128)(2,1)} %bitcast.6), channel_id=1, source_target_pairs={{0,2},{1,3},{2,0},{3,1},{4,6},{5,7},{6,4},{7,5},{8,10},{9,11},{10,... | collective-permute-start | bytes 1572872 | tf_op jit(solution)/shard_map/ppermute | solution.py:359
  5.3 0.8 %copy-done.3 = bf16[32,1024]{1,0:T(8,128)(2,1)S(1)} copy-done((bf16[32,1024]{1,0:T(8,128)(2,1)S(1)}, bf16[32,1024]{1,0:T(8,128)(2,1)}, u32[]{:S(2)}) %copy-start.3) | copy-done | bytes 65560
  6.2 2.5 %collective-permute-start = (bf16[32,256]{1,0:T(8,128)(2,1)S(1)}, bf16[32,256]{1,0:T(8,128)(2,1)S(1)}, u32[]{:S(2)}, u32[]{:S(2)}) collective-permute-start(bf16[32,256]{1,0:T(8,128)(2,1)S(1)} %get-tuple-element.56), channel_id=1, source_target_pairs={{0,24},{8,16},{16,8},{24,0},{1,25},{9,17},{17,9},{25,1},{2,26},{10... | collective-permute-start | bytes 49160 | tf_op jit(solution)/shard_map/ppermute | solution.py:359
  8.7 0.5 %collective-permute-start.1 = (bf16[32,256]{1,0:T(8,128)(2,1)S(1)}, bf16[32,256]{1,0:T(8,128)(2,1)S(1)}, u32[]{:S(2)}, u32[]{:S(2)}) collective-permute-start(bf16[32,256]{1,0:T(8,128)(2,1)S(1)} %get-tuple-element.57), channel_id=1, source_target_pairs={{0,16},{8,24},{16,0},{24,8},{1,17},{9,25},{17,1},{25,9},{2,18},{10... | collective-permute-start | bytes 49160 | tf_op jit(solution)/shard_map/ppermute | solution.py:359
  9.2 0.5 %collective-permute-start.2 = (bf16[32,256]{1,0:T(8,128)(2,1)S(1)}, bf16[32,256]{1,0:T(8,128)(2,1)S(1)}, u32[]{:S(2)}, u32[]{:S(2)}) collective-permute-start(bf16[32,256]{1,0:T(8,128)(2,1)S(1)} %get-tuple-element.58), channel_id=1, source_target_pairs={{0,8},{8,0},{16,24},{24,16},{1,9},{9,1},{17,25},{25,17},{2,10},{10... | collective-permute-start | bytes 49160 | tf_op jit(solution)/shard_map/ppermute | solution.py:359
  9.8 2.1 %forward_own.1 = (bf16[2048,256]{1,0:T(8,128)(2,1)S(1)}, bf16[256,2048]{1,0:T(8,128)(2,1)S(1)}, bf16[2048,256]{1,0:T(8,128)(2,1)S(1)}, bf16[128,2048]{1,0:T(8,12...) custom-call(bf16[2048,256]{1,0:T(8,128)(2,1)} %bitcast.8, ...), custom_call_target="tpu_custom_call" | custom-call | flops 1 | bytes 1 | tf_op jit(solution)/shard_map/forward_own/pallas_call | solution.py:39
  11.9 0.5 %collective-permute-done.1.refs_1_ = bf16[32,256]{1,0:T(8,128)(2,1)S(1)} collective-permute-done((bf16[32,256]{1,0:T(8,128)(2,1)S(1)}, bf16[32,256]{1,0:T(8,128)(2,1)S(1)}, u32[]{:S(2)}, u32[]{:S(2)}) %collective-permute-start.1) | collective-permute-done | bytes 16416 | tf_op jit(solution)/shard_map/ppermute | solution.py:359
  12.5 0.5 %collective-permute-done.2.refs_2_ = bf16[32,256]{1,0:T(8,128)(2,1)S(1)} collective-permute-done((bf16[32,256]{1,0:T(8,128)(2,1)S(1)}, bf16[32,256]{1,0:T(8,128)(2,1)S(1)}, u32[]{:S(2)}, u32[]{:S(2)}) %collective-permute-start.2) | collective-permute-done | bytes 16416 | tf_op jit(solution)/shard_map/ppermute | solution.py:359
  13.0 1.1 %backward_own.1 = (bf16[128,256]{1,0:T(8,128)(2,1)S(1)}, bf16[128,256]{1,0:T(8,128)(2,1)S(1)}, bf16[768,128]{1,0:T(8,128)(2,1)S(1)}, bf16[128,2048]{1,0:T(8,128)...) custom-call(bf16[256,2048]{1,0:T(8,128)(2,1)S(1)} %get-tuple-element.52.wu_ref, ...), custom_call_target="tpu_custom_call" | custom-call | flops 1 | bytes 1 | tf_op jit(solution)/shard_map/backward_own/pallas_call | solution.py:39
  14.1 0.4 first_sums.1
  14.5 0.5 %collective-permute-start.7 = (bf16[128,256]{1,0:T(8,128)(2,1)S(1)}, bf16[128,256]{1,0:T(8,128)(2,1)S(1)}, u32[]{:S(2)}, u32[]{:S(2)}) collective-permute-start(bf16[128,256]{1,0:T(8,128)(2,1)S(1)} %get-tuple-element.70), channel_id=1, source_target_pairs={{0,1},{1,0},{2,4},{3,5},{4,2},{5,3},{6,7},{7,6},{8,9},{9,8},{10,12... | collective-permute-start | bytes 196616 | tf_op jit(solution)/shard_map/ppermute | solution.py:420
  15.0 0.9 %collective-permute-start.6 = (bf16[128,256]{1,0:T(8,128)(2,1)S(1)}, bf16[128,256]{1,0:T(8,128)(2,1)S(1)}, u32[]{:S(2)}, u32[]{:S(2)}) collective-permute-start(bf16[128,256]{1,0:T(8,128)(2,1)S(1)} %get-tuple-element.70), channel_id=1, source_target_pairs={{0,2},{1,3},{2,0},{3,1},{4,6},{5,7},{6,4},{7,5},{8,10},{9,11},{10,... | collective-permute-start | bytes 196616 | tf_op jit(solution)/shard_map/ppermute | solution.py:359
  16.4 1.4 %collective-permute-start.13 = (bf16[784,256]{1,0:T(8,128)(2,1)S(1)}, bf16[784,256]{1,0:T(8,128)(2,1)S(1)}, u32[]{:S(2)}, u32[]{:S(2)}) collective-permute-start(bf16[784,256]{1,0:T(8,128)(2,1)S(1)} %join_cores.2), channel_id=1, source_target_pairs={{0,6},{1,7},{2,3},{3,2},{4,5},{5,4},{6,0},{7,1},{8,14},{9,15},{10,... | collective-permute-start | bytes 1204232 | tf_op jit(solution)/shard_map/ppermute | solution.py:425
  17.8 1.5 %collective-permute-done.6.g_ref = bf16[128,256]{1,0:T(8,128)(2,1)S(1)} collective-permute-done((bf16[128,256]{1,0:T(8,128)(2,1)S(1)}, bf16[128,256]{1,0:T(8,128)(2,1)S(1)}, u32[]{:S(2)}, u32[]{:S(2)}) %collective-permute-start.6) | collective-permute-done | bytes 65568 | tf_op jit(solution)/shard_map/ppermute | solution.py:359
  19.3 0.8 %forward_other.1 = (bf16[128,256]{1,0:T(8,128)(2,1)S(1)}, bf16[128,2048]{1,0:T(8,128)(2,1)S(1)}) custom-call(bf16[128,2048]{1,0:T(8,128)(2,1)S(1)} %collective-permute-done.5.x_ref, bf16[2048,256]{1,0:T(8,128)(2,1)S(1)} %get-tuple-element.51.wd_ref, bf16[256,2048]{1,0:T(8,128)(2,1)S(1)} %get-tuple-element.52.wu_ref, f32[1,2048]{1,0:T(1,128)S(1)} %copy-done.1), custom_call_target="tpu_custom_call" | custom-call | flops 1000000000 | bytes 1 | tf_op jit(solution)/shard_map/forward_other/pallas_call | solution.py:39
  20.1 1.0 %second_sums.1 = (bf16[128,2048]{1,0:T(8,128)(2,1)S(1)}, bf16[768,128]{1,0:T(8,128)(2,1)S(1)}, f32[1,2048]{1,0:T(1,128)S(1)}, f32[784,256]{1,0:T(8,128)S(1)}, bf...) custom-call(bf16[256,2048]{1,0:T(8,128)(2,1)S(1)} %get-tuple-element.52.wu_ref, ...), custom_call_target="tpu_custom_call" | custom-call | flops 1000000000 | bytes 1 | tf_op jit(solution)/shard_map/second_sums/pallas_call | solution.py:39
  21.2 0.5 %collective-permute-start.8 = (bf16[384,256]{1,0:T(8,128)(2,1)S(1)}, bf16[384,256]{1,0:T(8,128)(2,1)S(1)}, u32[]{:S(2)}, u32[]{:S(2)}) collective-permute-start(bf16[384,256]{1,0:T(8,128)(2,1)S(1)} %get-tuple-element.76), channel_id=1, source_target_pairs={{0,1},{1,0},{2,3},{3,2},{4,5},{5,4},{6,7},{7,6},{8,9},{9,8},{10,11... | collective-permute-start | bytes 589832 | tf_op jit(solution)/shard_map/ppermute | solution.py:359
  21.7 1.2 %collective-permute-done.8.refs_0_ = bf16[384,256]{1,0:T(8,128)(2,1)S(1)} collective-permute-done((bf16[384,256]{1,0:T(8,128)(2,1)S(1)}, bf16[384,256]{1,0:T(8,128)(2,1)S(1)}, u32[]{:S(2)}, u32[]{:S(2)}) %collective-permute-start.8) | collective-permute-done | bytes 196640 | tf_op jit(solution)/shard_map/ppermute | solution.py:359
  23.0 1.9 %collective-permute-start.18 = (bf16[784,256]{1,0:T(8,128)(2,1)S(1)}, bf16[784,256]{1,0:T(8,128)(2,1)S(1)}, u32[]{:S(2)}, u32[]{:S(2)}) collective-permute-start(bf16[784,256]{1,0:T(8,128)(2,1)S(1)} %join_cores.3), channel_id=1, source_target_pairs={{0,4},{1,5},{2,0},{3,1},{4,6},{5,7},{6,2},{7,3},{8,12},{9,13},{10,... | collective-permute-start | bytes 1204232 | tf_op jit(solution)/shard_map/ppermute | solution.py:442
  24.9 0.5 %grad_inputs.1 = (bf16[32,2048]{1,0:T(8,128)(2,1)S(1)}, bf16[32,2048]{1,0:T(8,128)(2,1)S(1)}, bf16[32,2048]{1,0:T(8,128)(2,1)S(1)}, bf16[32,2048]{1,0:T(8,128)(2,1)S(1)}) custom-call(bf16[2048,256]{1,0:T(8,128)(2,1)S(1)} %get-tuple-element.51.wd_ref, bf16[128,256]{1,0:T(8,128)(2,1)S(1)} %get-tuple-element.60.gh_ref, ...), custom_call_target="tpu_custom_call" | custom-call | flops 1 | bytes 1 | tf_op jit(solution)/shard_map/grad_inputs/pallas_call | solution.py:39
  25.4 1.5 %collective-permute-start.10 = (bf16[32,2048]{1,0:T(8,128)(2,1)S(1)}, bf16[32,2048]{1,0:T(8,128)(2,1)S(1)}, u32[]{:S(2)}, u32[]{:S(2)}) collective-permute-start(bf16[32,2048]{1,0:T(8,128)(2,1)S(1)} %get-tuple-element.81), channel_id=1, source_target_pairs={{0,8},{8,0},{16,24},{24,16},{1,9},{9,1},{17,25},{25,17},{2,10},{10... | collective-permute-start | bytes 393224 | tf_op jit(solution)/shard_map/ppermute | solution.py:359
  26.9 1.5 %collective-permute-start.11 = (bf16[32,2048]{1,0:T(8,128)(2,1)S(1)}, bf16[32,2048]{1,0:T(8,128)(2,1)S(1)}, u32[]{:S(2)}, u32[]{:S(2)}) collective-permute-start(bf16[32,2048]{1,0:T(8,128)(2,1)S(1)} %get-tuple-element.82), channel_id=1, source_target_pairs={{0,16},{8,24},{16,0},{24,8},{1,17},{9,25},{17,1},{25,9},{2,18},{10... | collective-permute-start | bytes 393224 | tf_op jit(solution)/shard_map/ppermute | solution.py:359
  28.5 0.5 %collective-permute-start.12 = (bf16[32,2048]{1,0:T(8,128)(2,1)S(1)}, bf16[32,2048]{1,0:T(8,128)(2,1)S(1)}, u32[]{:S(2)}, u32[]{:S(2)}) collective-permute-start(bf16[32,2048]{1,0:T(8,128)(2,1)S(1)} %get-tuple-element.83), channel_id=1, source_target_pairs={{0,24},{8,16},{16,8},{24,0},{1,25},{9,17},{17,9},{25,1},{2,26},{10... | collective-permute-start | bytes 393224 | tf_op jit(solution)/shard_map/ppermute | solution.py:359
  28.9 1.5 %collective-permute-done.13.refs_10_.first_ref = bf16[784,256]{1,0:T(8,128)(2,1)S(1)} collective-permute-done((bf16[784,256]{1,0:T(8,128)(2,1)S(1)}, bf16[784,256]{1,0:T(8,128)(2,1)S(1)}, u32[]{:S(2)}, u32[]{:S(2)}) %collective-permute-start.13) | collective-permute-done | bytes 401440 | tf_op jit(solution)/shard_map/ppermute | solution.py:425
  30.4 1.9 %near_sums.1 = (f32[816,256]{1,0:T(8,128)S(1)}, bf16[192,256]{1,0:T(8,128)(2,1)S(1)}, bf16[192,256]{1,0:T(8,128)(2,1)S(1)}, bf16[192,256]{1,0:T(8,128)(2,1)S(1)}, bf16[240,256]{1,0:T(8,128)(2,1)S(1)}) custom-call(bf16[256,2048]{1,0:T(8,128)(2,1)S(1)} %get-tuple-element.52.wu_ref, bf16[2048,256]{1,0:T(8,128)(2,1)S(1)} %get-tuple-element.53.wo_ref, ...), custom_call_target="tpu_custom_call" | custom-call | flops 1000000000 | bytes 1 | tf_op jit(solution)/shard_map/near_sums/pallas_call | solution.py:39
  32.4 0.5 %collective-permute-start.14 = (bf16[192,256]{1,0:T(8,128)(2,1)S(1)}, bf16[192,256]{1,0:T(8,128)(2,1)S(1)}, u32[]{:S(2)}, u32[]{:S(2)}) collective-permute-start(bf16[192,256]{1,0:T(8,128)(2,1)S(1)} %get-tuple-element.90), channel_id=1, source_target_pairs={{0,1},{1,0},{2,3},{3,2},{4,5},{5,4},{6,7},{7,6},{8,9},{9,8},{10,11... | collective-permute-start | bytes 294920 | tf_op jit(solution)/shard_map/ppermute | solution.py:359
  32.9 1.9 %collective-permute-done.11.refs_2_ = bf16[32,2048]{1,0:T(8,128)(2,1)S(1)} collective-permute-done((bf16[32,2048]{1,0:T(8,128)(2,1)S(1)}, bf16[32,2048]{1,0:T(8,128)(2,1)S(1)}, u32[]{:S(2)}, u32[]{:S(2)}) %collective-permute-start.11) | collective-permute-done | bytes 131104 | tf_op jit(solution)/shard_map/ppermute | solution.py:359
  34.8 0.5 %collective-permute-start.16 = (bf16[192,256]{1,0:T(8,128)(2,1)S(1)}, bf16[192,256]{1,0:T(8,128)(2,1)S(1)}, u32[]{:S(2)}, u32[]{:S(2)}) collective-permute-start(bf16[192,256]{1,0:T(8,128)(2,1)S(1)} %get-tuple-element.92), channel_id=1, source_target_pairs={{0,1},{1,0},{2,3},{3,2},{4,5},{5,4},{6,7},{7,6},{8,9},{9,8},{10,11... | collective-permute-start | bytes 294920 | tf_op jit(solution)/shard_map/ppermute | solution.py:359
  35.5 1.5 %place_features.1 = bf16[32,8192]{1,0:T(8,128)(2,1)} custom-call(s32[64]{0:T(128)S(1)} %copy-done.2, bf16[32,2048]{1,0:T(8,128)(2,1)S(1)} %get-tuple-element.80.refs_0_, bf16[32,2048]{1,0:T(8,128)(2,1)S(1)} %collective-permute-done.10.refs_1_, bf16[32,2048]{1,0:T(8,128)(2,1)S(1)} %collective-permute-done.11.refs_2_, ...), custom_call_target="tpu_custom_call" | custom-call | flops 1 | bytes 1 | tf_op jit(solution)/shard_map/place_features/pallas_call | solution.py:39
  37.2 1.0 %collective-permute-done.18.second_ref = bf16[784,256]{1,0:T(8,128)(2,1)S(1)} collective-permute-done((bf16[784,256]{1,0:T(8,128)(2,1)S(1)}, bf16[784,256]{1,0:T(8,128)(2,1)S(1)}, u32[]{:S(2)}, u32[]{:S(2)}) %collective-permute-start.18) | collective-permute-done | bytes 401440 | tf_op jit(solution)/shard_map/ppermute | solution.py:442
  38.2 1.0 %add_up.1 = (f32[96,2048]{1,0:T(8,128)}, f32[1,2048]{1,0:T(1,128)}) custom-call(f32[96,2048]{1,0:T(8,128)S(1)} %get-tuple-element.94.sum_ref, f32[1,2048]{1,0:T(1,128)S(1)} %get-tuple-element.95.near_bias_ref, f32[1,2048]{1,0:T(1,128)S(1)} %get-tuple-element.96.far_bias_ref, bf16[784,256]{1,0:T(8,128)(2,1)S(1)} %collective-permute-done.18.second_ref), custom_call_target="tpu_custom_call" | custom-call | flops 10000000000 | bytes 1 | tf_op jit(solution)/shard_map/add_up/pallas_call | solution.py:39
  (28 shorter events, 1.1 us)
Async XLA Ops:
  0.6 9.1 %copy-start = (bf16[1,128,2048]{2,1,0:T(8,128)(2,1)S(1)}, bf16[1,128,2048]{2,1,0:T(8,128)(2,1)}, u32[]{:S(2)}) copy-start(bf16[1,128,2048]{2,1,0:T(8,128)(2,1)} %param.8) | copy-start | bytes 1572868
  0.6 17.1 %collective-permute-start.3 = (bf16[128,2048]{1,0:T(8,128)(2,1)}, bf16[128,2048]{1,0:T(8,128)(2,1)S(1)}, u32[]{:S(2)}, u32[]{:S(2)}) collective-permute-start(bf16[128,2048]{1,0:T(8,128)(2,1)} %bitcast.5), channel_id=1, source_target_pairs={{0,1},{1,0},{2,4},{3,5},{4,2},{5,3},{6,7},{7,6},{8,9},{9,8},{10,12... | collective-permute-start | bytes 1572872 | tf_op jit(solution)/shard_map/ppermute | solution.py:387
  1.2 18.1 %collective-permute-start.5 = (bf16[128,2048]{1,0:T(8,128)(2,1)}, bf16[128,2048]{1,0:T(8,128)(2,1)S(1)}, u32[]{:S(2)}, u32[]{:S(2)}) collective-permute-start(bf16[128,2048]{1,0:T(8,128)(2,1)} %bitcast.6), channel_id=1, source_target_pairs={{0,2},{1,3},{2,0},{3,1},{4,6},{5,7},{6,4},{7,5},{8,10},{9,11},{10,... | collective-permute-start | bytes 1572872 | tf_op jit(solution)/shard_map/ppermute | solution.py:359
  5.3 0.8 %copy-start.3 = (bf16[32,1024]{1,0:T(8,128)(2,1)S(1)}, bf16[32,1024]{1,0:T(8,128)(2,1)}, u32[]{:S(2)}) copy-start(bf16[32,1024]{1,0:T(8,128)(2,1)} %grad_ref.1) | copy-start | bytes 196612
  6.2 3.6 %copy-start.1 = (f32[1,2048]{1,0:T(1,128)S(1)}, f32[1,2048]{1,0:T(1,128)}, u32[]{:S(2)}) copy-start(f32[1,2048]{1,0:T(1,128)} %bias_ref.5) | copy-start | bytes 24580
  6.2 5.7 %collective-permute-start = (bf16[32,256]{1,0:T(8,128)(2,1)S(1)}, bf16[32,256]{1,0:T(8,128)(2,1)S(1)}, u32[]{:S(2)}, u32[]{:S(2)}) collective-permute-start(bf16[32,256]{1,0:T(8,128)(2,1)S(1)} %get-tuple-element.56), channel_id=1, source_target_pairs={{0,24},{8,16},{16,8},{24,0},{1,25},{9,17},{17,9},{25,1},{2,26},{10... | collective-permute-start | bytes 49160 | tf_op jit(solution)/shard_map/ppermute | solution.py:359
  8.7 3.7 %collective-permute-start.1 = (bf16[32,256]{1,0:T(8,128)(2,1)S(1)}, bf16[32,256]{1,0:T(8,128)(2,1)S(1)}, u32[]{:S(2)}, u32[]{:S(2)}) collective-permute-start(bf16[32,256]{1,0:T(8,128)(2,1)S(1)} %get-tuple-element.57), channel_id=1, source_target_pairs={{0,16},{8,24},{16,0},{24,8},{1,17},{9,25},{17,1},{25,9},{2,18},{10... | collective-permute-start | bytes 49160 | tf_op jit(solution)/shard_map/ppermute | solution.py:359
  9.2 3.7 %collective-permute-start.2 = (bf16[32,256]{1,0:T(8,128)(2,1)S(1)}, bf16[32,256]{1,0:T(8,128)(2,1)S(1)}, u32[]{:S(2)}, u32[]{:S(2)}) collective-permute-start(bf16[32,256]{1,0:T(8,128)(2,1)S(1)} %get-tuple-element.58), channel_id=1, source_target_pairs={{0,8},{8,0},{16,24},{24,16},{1,9},{9,1},{17,25},{25,17},{2,10},{10... | collective-permute-start | bytes 49160 | tf_op jit(solution)/shard_map/ppermute | solution.py:359
  14.4 1.8 %collective-permute-start.4 = (bf16[784,256]{1,0:T(8,128)(2,1)S(1)}, bf16[784,256]{1,0:T(8,128)(2,1)S(1)}, u32[]{:S(2)}, u32[]{:S(2)}) collective-permute-start(bf16[784,256]{1,0:T(8,128)(2,1)S(1)} %get-tuple-element.67), channel_id=1, source_target_pairs={{0,1},{1,0},{2,3},{3,2},{4,5},{5,4},{6,7},{7,6},{8,9},{9,8},{10,11... | collective-permute-start | bytes 1204232 | tf_op jit(solution)/shard_map/ppermute | solution.py:359
  14.5 5.6 %collective-permute-start.7 = (bf16[128,256]{1,0:T(8,128)(2,1)S(1)}, bf16[128,256]{1,0:T(8,128)(2,1)S(1)}, u32[]{:S(2)}, u32[]{:S(2)}) collective-permute-start(bf16[128,256]{1,0:T(8,128)(2,1)S(1)} %get-tuple-element.70), channel_id=1, source_target_pairs={{0,1},{1,0},{2,4},{3,5},{4,2},{5,3},{6,7},{7,6},{8,9},{9,8},{10,12... | collective-permute-start | bytes 196616 | tf_op jit(solution)/shard_map/ppermute | solution.py:420
  15.0 4.3 %collective-permute-start.6 = (bf16[128,256]{1,0:T(8,128)(2,1)S(1)}, bf16[128,256]{1,0:T(8,128)(2,1)S(1)}, u32[]{:S(2)}, u32[]{:S(2)}) collective-permute-start(bf16[128,256]{1,0:T(8,128)(2,1)S(1)} %get-tuple-element.70), channel_id=1, source_target_pairs={{0,2},{1,3},{2,0},{3,1},{4,6},{5,7},{6,4},{7,5},{8,10},{9,11},{10,... | collective-permute-start | bytes 196616 | tf_op jit(solution)/shard_map/ppermute | solution.py:359
  16.4 14.0 %collective-permute-start.13 = (bf16[784,256]{1,0:T(8,128)(2,1)S(1)}, bf16[784,256]{1,0:T(8,128)(2,1)S(1)}, u32[]{:S(2)}, u32[]{:S(2)}) collective-permute-start(bf16[784,256]{1,0:T(8,128)(2,1)S(1)} %join_cores.2), channel_id=1, source_target_pairs={{0,6},{1,7},{2,3},{3,2},{4,5},{5,4},{6,0},{7,1},{8,14},{9,15},{10,... | collective-permute-start | bytes 1204232 | tf_op jit(solution)/shard_map/ppermute | solution.py:425
  21.1 1.8 %collective-permute-start.9 = (bf16[400,256]{1,0:T(8,128)(2,1)S(1)}, bf16[400,256]{1,0:T(8,128)(2,1)S(1)}, u32[]{:S(2)}, u32[]{:S(2)}) collective-permute-start(bf16[400,256]{1,0:T(8,128)(2,1)S(1)} %get-tuple-element.77), channel_id=1, source_target_pairs={{0,1},{1,0},{2,3},{3,2},{4,5},{5,4},{6,7},{7,6},{8,9},{9,8},{10,11... | collective-permute-start | bytes 614408 | tf_op jit(solution)/shard_map/ppermute | solution.py:359
  21.2 1.7 %collective-permute-start.8 = (bf16[384,256]{1,0:T(8,128)(2,1)S(1)}, bf16[384,256]{1,0:T(8,128)(2,1)S(1)}, u32[]{:S(2)}, u32[]{:S(2)}) collective-permute-start(bf16[384,256]{1,0:T(8,128)(2,1)S(1)} %get-tuple-element.76), channel_id=1, source_target_pairs={{0,1},{1,0},{2,3},{3,2},{4,5},{5,4},{6,7},{7,6},{8,9},{9,8},{10,11... | collective-permute-start | bytes 589832 | tf_op jit(solution)/shard_map/ppermute | solution.py:359
  23.0 15.2 %collective-permute-start.18 = (bf16[784,256]{1,0:T(8,128)(2,1)S(1)}, bf16[784,256]{1,0:T(8,128)(2,1)S(1)}, u32[]{:S(2)}, u32[]{:S(2)}) collective-permute-start(bf16[784,256]{1,0:T(8,128)(2,1)S(1)} %join_cores.3), channel_id=1, source_target_pairs={{0,4},{1,5},{2,0},{3,1},{4,6},{5,7},{6,2},{7,3},{8,12},{9,13},{10,... | collective-permute-start | bytes 1204232 | tf_op jit(solution)/shard_map/ppermute | solution.py:442
  25.4 7.0 %collective-permute-start.10 = (bf16[32,2048]{1,0:T(8,128)(2,1)S(1)}, bf16[32,2048]{1,0:T(8,128)(2,1)S(1)}, u32[]{:S(2)}, u32[]{:S(2)}) collective-permute-start(bf16[32,2048]{1,0:T(8,128)(2,1)S(1)} %get-tuple-element.81), channel_id=1, source_target_pairs={{0,8},{8,0},{16,24},{24,16},{1,9},{9,1},{17,25},{25,17},{2,10},{10... | collective-permute-start | bytes 393224 | tf_op jit(solution)/shard_map/ppermute | solution.py:359
  26.9 7.9 %collective-permute-start.11 = (bf16[32,2048]{1,0:T(8,128)(2,1)S(1)}, bf16[32,2048]{1,0:T(8,128)(2,1)S(1)}, u32[]{:S(2)}, u32[]{:S(2)}) collective-permute-start(bf16[32,2048]{1,0:T(8,128)(2,1)S(1)} %get-tuple-element.82), channel_id=1, source_target_pairs={{0,16},{8,24},{16,0},{24,8},{1,17},{9,25},{17,1},{25,9},{2,18},{10... | collective-permute-start | bytes 393224 | tf_op jit(solution)/shard_map/ppermute | solution.py:359
  28.5 6.3 %collective-permute-start.12 = (bf16[32,2048]{1,0:T(8,128)(2,1)S(1)}, bf16[32,2048]{1,0:T(8,128)(2,1)S(1)}, u32[]{:S(2)}, u32[]{:S(2)}) collective-permute-start(bf16[32,2048]{1,0:T(8,128)(2,1)S(1)} %get-tuple-element.83), channel_id=1, source_target_pairs={{0,24},{8,16},{16,8},{24,0},{1,25},{9,17},{17,9},{25,1},{2,26},{10... | collective-permute-start | bytes 393224 | tf_op jit(solution)/shard_map/ppermute | solution.py:359
  32.3 4.6 %collective-permute-start.17 = (bf16[240,256]{1,0:T(8,128)(2,1)S(1)}, bf16[240,256]{1,0:T(8,128)(2,1)S(1)}, u32[]{:S(2)}, u32[]{:S(2)}) collective-permute-start(bf16[240,256]{1,0:T(8,128)(2,1)S(1)} %get-tuple-element.93), channel_id=1, source_target_pairs={{0,1},{1,0},{2,3},{3,2},{4,5},{5,4},{6,7},{7,6},{8,9},{9,8},{10,11... | collective-permute-start | bytes 368648 | tf_op jit(solution)/shard_map/ppermute | solution.py:359
  32.4 4.5 %collective-permute-start.14 = (bf16[192,256]{1,0:T(8,128)(2,1)S(1)}, bf16[192,256]{1,0:T(8,128)(2,1)S(1)}, u32[]{:S(2)}, u32[]{:S(2)}) collective-permute-start(bf16[192,256]{1,0:T(8,128)(2,1)S(1)} %get-tuple-element.90), channel_id=1, source_target_pairs={{0,1},{1,0},{2,3},{3,2},{4,5},{5,4},{6,7},{7,6},{8,9},{9,8},{10,11... | collective-permute-start | bytes 294920 | tf_op jit(solution)/shard_map/ppermute | solution.py:359
  34.8 0.7 %copy-start.2 = (s32[64]{0:T(128)S(1)}, s32[64]{0:T(128)}, u32[]{:S(2)}) copy-start(s32[64]{0:T(128)} %assign_ref.1) | copy-start | bytes 772
  34.8 2.2 %collective-permute-start.15 = (bf16[192,256]{1,0:T(8,128)(2,1)S(1)}, bf16[192,256]{1,0:T(8,128)(2,1)S(1)}, u32[]{:S(2)}, u32[]{:S(2)}) collective-permute-start(bf16[192,256]{1,0:T(8,128)(2,1)S(1)} %get-tuple-element.91), channel_id=1, source_target_pairs={{0,1},{1,0},{2,3},{3,2},{4,5},{5,4},{6,7},{7,6},{8,9},{9,8},{10,11... | collective-permute-start | bytes 294920 | tf_op jit(solution)/shard_map/ppermute | solution.py:359
  34.8 2.2 %collective-permute-start.16 = (bf16[192,256]{1,0:T(8,128)(2,1)S(1)}, bf16[192,256]{1,0:T(8,128)(2,1)S(1)}, u32[]{:S(2)}, u32[]{:S(2)}) collective-permute-start(bf16[192,256]{1,0:T(8,128)(2,1)S(1)} %get-tuple-element.92), channel_id=1, source_target_pairs={{0,1},{1,0},{2,3},{3,2},{4,5},{5,4},{6,7},{7,6},{8,9},{9,8},{10,11... | collective-permute-start | bytes 294920 | tf_op jit(solution)/shard_map/ppermute | solution.py:359

commit v7 on v6

--- a/solution.py
+++ b/solution.py
@@ -50,7 +50,7 @@
 
 
 def column_chunks(width):
-    step = 512 if width % 512 == 0 else width
+    step = 256 if width % 256 == 0 else width
     return [slice(c, c + step) for c in range(0, width, step)]
 
 

time: 39.3 us -> 39.2 us (level)
  no operation moved by 1% of the time
where the time goes in v7:
time: 39.2 us; the launch traced here: 39 us
  starting transfers between devices  18.2 us (46%)
  Pallas kernels  10.6 us (27%)
  waiting for transfers between devices  8.43 us (22%)
  local copies, waits for them, and re-layouts  0.99 us (3%)
  between operations  0.81 us (2%)
    ppermute x15, starting transfers between devices, across(): return lax.ppermute(value, axis, xor_pairs(lax.axis_size(axis), k))  13.9 us
    pallas_call x14, Pallas kernels, call(): pl.pallas_call(kernel, out_shape=outs, in_specs=[pl.BlockSpec(memory_spac...  10.6 us
    ppermute x15, waiting for transfers between devices, across(): return lax.ppermute(value, axis, xor_pairs(lax.axis_size(axis), k))  5.94 us
    ppermute x1, starting transfers between devices, paired_body(): from_second = lax.ppermute(second_sum, 'shard', second)  1.85 us
    ppermute x1, waiting for transfers between devices, paired_body(): from_first = lax.ppermute(first, 'shard', outer)  1.48 us
    ppermute x1, starting transfers between devices, paired_body(): from_first = lax.ppermute(first, 'shard', outer)  1.42 us
    ppermute x1, waiting for transfers between devices, paired_body(): from_second = lax.ppermute(second_sum, 'shard', second)  1.01 us
    unnamed x8, local copies, waits for them, and re-layouts  0.99 us
  transfers between devices with their start and end apart: 19, of which 8 were waited for; matrix products, arithmetic and copies ran while one was open for 0% of the time, Pallas kernels for 25%

profile of v7, /device:TPU:0, one launch (start us, length us, event | category | flops | bytes accessed | tf_op | source)
XLA Modules:
  0.0 39.0 jit_solution(15134101177656242398)
XLA Ops:
  0.6 0.5 %collective-permute-start.3 = (bf16[128,2048]{1,0:T(8,128)(2,1)}, bf16[128,2048]{1,0:T(8,128)(2,1)S(1)}, u32[]{:S(2)}, u32[]{:S(2)}) collective-permute-start(bf16[128,2048]{1,0:T(8,128)(2,1)} %bitcast.5), channel_id=1, source_target_pairs={{0,1},{1,0},{2,4},{3,5},{4,2},{5,3},{6,7},{7,6},{8,9},{9,8},{10,12... | collective-permute-start | bytes 1572872 | tf_op jit(solution)/shard_map/ppermute | solution.py:387
  1.2 4.1 %collective-permute-start.5 = (bf16[128,2048]{1,0:T(8,128)(2,1)}, bf16[128,2048]{1,0:T(8,128)(2,1)S(1)}, u32[]{:S(2)}, u32[]{:S(2)}) collective-permute-start(bf16[128,2048]{1,0:T(8,128)(2,1)} %bitcast.6), channel_id=1, source_target_pairs={{0,2},{1,3},{2,0},{3,1},{4,6},{5,7},{6,4},{7,5},{8,10},{9,11},{10,... | collective-permute-start | bytes 1572872 | tf_op jit(solution)/shard_map/ppermute | solution.py:359
  5.3 0.8 %copy-done.3 = bf16[32,1024]{1,0:T(8,128)(2,1)S(1)} copy-done((bf16[32,1024]{1,0:T(8,128)(2,1)S(1)}, bf16[32,1024]{1,0:T(8,128)(2,1)}, u32[]{:S(2)}) %copy-start.3) | copy-done | bytes 65560
  6.2 2.5 %collective-permute-start = (bf16[32,256]{1,0:T(8,128)(2,1)S(1)}, bf16[32,256]{1,0:T(8,128)(2,1)S(1)}, u32[]{:S(2)}, u32[]{:S(2)}) collective-permute-start(bf16[32,256]{1,0:T(8,128)(2,1)S(1)} %get-tuple-element.56), channel_id=1, source_target_pairs={{0,24},{8,16},{16,8},{24,0},{1,25},{9,17},{17,9},{25,1},{2,26},{10... | collective-permute-start | bytes 49160 | tf_op jit(solution)/shard_map/ppermute | solution.py:359
  8.7 0.5 %collective-permute-start.1 = (bf16[32,256]{1,0:T(8,128)(2,1)S(1)}, bf16[32,256]{1,0:T(8,128)(2,1)S(1)}, u32[]{:S(2)}, u32[]{:S(2)}) collective-permute-start(bf16[32,256]{1,0:T(8,128)(2,1)S(1)} %get-tuple-element.57), channel_id=1, source_target_pairs={{0,16},{8,24},{16,0},{24,8},{1,17},{9,25},{17,1},{25,9},{2,18},{10... | collective-permute-start | bytes 49160 | tf_op jit(solution)/shard_map/ppermute | solution.py:359
  9.2 0.5 %collective-permute-start.2 = (bf16[32,256]{1,0:T(8,128)(2,1)S(1)}, bf16[32,256]{1,0:T(8,128)(2,1)S(1)}, u32[]{:S(2)}, u32[]{:S(2)}) collective-permute-start(bf16[32,256]{1,0:T(8,128)(2,1)S(1)} %get-tuple-element.58), channel_id=1, source_target_pairs={{0,8},{8,0},{16,24},{24,16},{1,9},{9,1},{17,25},{25,17},{2,10},{10... | collective-permute-start | bytes 49160 | tf_op jit(solution)/shard_map/ppermute | solution.py:359
  9.8 2.1 %forward_own.1 = (bf16[2048,256]{1,0:T(8,128)(2,1)S(1)}, bf16[256,2048]{1,0:T(8,128)(2,1)S(1)}, bf16[2048,256]{1,0:T(8,128)(2,1)S(1)}, bf16[128,2048]{1,0:T(8,12...) custom-call(bf16[2048,256]{1,0:T(8,128)(2,1)} %bitcast.8, ...), custom_call_target="tpu_custom_call" | custom-call | flops 1 | bytes 1 | tf_op jit(solution)/shard_map/forward_own/pallas_call | solution.py:39
  11.9 0.5 %collective-permute-done.1.refs_1_ = bf16[32,256]{1,0:T(8,128)(2,1)S(1)} collective-permute-done((bf16[32,256]{1,0:T(8,128)(2,1)S(1)}, bf16[32,256]{1,0:T(8,128)(2,1)S(1)}, u32[]{:S(2)}, u32[]{:S(2)}) %collective-permute-start.1) | collective-permute-done | bytes 16416 | tf_op jit(solution)/shard_map/ppermute | solution.py:359
  12.5 0.5 %collective-permute-done.2.refs_2_ = bf16[32,256]{1,0:T(8,128)(2,1)S(1)} collective-permute-done((bf16[32,256]{1,0:T(8,128)(2,1)S(1)}, bf16[32,256]{1,0:T(8,128)(2,1)S(1)}, u32[]{:S(2)}, u32[]{:S(2)}) %collective-permute-start.2) | collective-permute-done | bytes 16416 | tf_op jit(solution)/shard_map/ppermute | solution.py:359
  13.0 1.0 %backward_own.1 = (bf16[128,256]{1,0:T(8,128)(2,1)S(1)}, bf16[128,256]{1,0:T(8,128)(2,1)S(1)}, bf16[768,128]{1,0:T(8,128)(2,1)S(1)}, bf16[128,2048]{1,0:T(8,128)...) custom-call(bf16[256,2048]{1,0:T(8,128)(2,1)S(1)} %get-tuple-element.52.wu_ref, ...), custom_call_target="tpu_custom_call" | custom-call | flops 1 | bytes 1 | tf_op jit(solution)/shard_map/backward_own/pallas_call | solution.py:39
  14.0 0.4 first_sums.1
  14.5 0.5 %collective-permute-start.7 = (bf16[128,256]{1,0:T(8,128)(2,1)S(1)}, bf16[128,256]{1,0:T(8,128)(2,1)S(1)}, u32[]{:S(2)}, u32[]{:S(2)}) collective-permute-start(bf16[128,256]{1,0:T(8,128)(2,1)S(1)} %get-tuple-element.70), channel_id=1, source_target_pairs={{0,1},{1,0},{2,4},{3,5},{4,2},{5,3},{6,7},{7,6},{8,9},{9,8},{10,12... | collective-permute-start | bytes 196616 | tf_op jit(solution)/shard_map/ppermute | solution.py:420
  15.0 1.0 %collective-permute-start.6 = (bf16[128,256]{1,0:T(8,128)(2,1)S(1)}, bf16[128,256]{1,0:T(8,128)(2,1)S(1)}, u32[]{:S(2)}, u32[]{:S(2)}) collective-permute-start(bf16[128,256]{1,0:T(8,128)(2,1)S(1)} %get-tuple-element.70), channel_id=1, source_target_pairs={{0,2},{1,3},{2,0},{3,1},{4,6},{5,7},{6,4},{7,5},{8,10},{9,11},{10,... | collective-permute-start | bytes 196616 | tf_op jit(solution)/shard_map/ppermute | solution.py:359
  16.3 1.4 %collective-permute-start.13 = (bf16[784,256]{1,0:T(8,128)(2,1)S(1)}, bf16[784,256]{1,0:T(8,128)(2,1)S(1)}, u32[]{:S(2)}, u32[]{:S(2)}) collective-permute-start(bf16[784,256]{1,0:T(8,128)(2,1)S(1)} %join_cores.2), channel_id=1, source_target_pairs={{0,6},{1,7},{2,3},{3,2},{4,5},{5,4},{6,0},{7,1},{8,14},{9,15},{10,... | collective-permute-start | bytes 1204232 | tf_op jit(solution)/shard_map/ppermute | solution.py:425
  17.8 1.5 %collective-permute-done.6.g_ref = bf16[128,256]{1,0:T(8,128)(2,1)S(1)} collective-permute-done((bf16[128,256]{1,0:T(8,128)(2,1)S(1)}, bf16[128,256]{1,0:T(8,128)(2,1)S(1)}, u32[]{:S(2)}, u32[]{:S(2)}) %collective-permute-start.6) | collective-permute-done | bytes 65568 | tf_op jit(solution)/shard_map/ppermute | solution.py:359
  19.2 0.8 %forward_other.1 = (bf16[128,256]{1,0:T(8,128)(2,1)S(1)}, bf16[128,2048]{1,0:T(8,128)(2,1)S(1)}) custom-call(bf16[128,2048]{1,0:T(8,128)(2,1)S(1)} %collective-permute-done.5.x_ref, bf16[2048,256]{1,0:T(8,128)(2,1)S(1)} %get-tuple-element.51.wd_ref, bf16[256,2048]{1,0:T(8,128)(2,1)S(1)} %get-tuple-element.52.wu_ref, f32[1,2048]{1,0:T(1,128)S(1)} %copy-done.1), custom_call_target="tpu_custom_call" | custom-call | flops 1000000000 | bytes 1 | tf_op jit(solution)/shard_map/forward_other/pallas_call | solution.py:39
  20.0 1.0 %second_sums.1 = (bf16[128,2048]{1,0:T(8,128)(2,1)S(1)}, bf16[768,128]{1,0:T(8,128)(2,1)S(1)}, f32[1,2048]{1,0:T(1,128)S(1)}, f32[784,256]{1,0:T(8,128)S(1)}, bf...) custom-call(bf16[256,2048]{1,0:T(8,128)(2,1)S(1)} %get-tuple-element.52.wu_ref, ...), custom_call_target="tpu_custom_call" | custom-call | flops 1000000000 | bytes 1 | tf_op jit(solution)/shard_map/second_sums/pallas_call | solution.py:39
  21.1 0.5 %collective-permute-start.8 = (bf16[384,256]{1,0:T(8,128)(2,1)S(1)}, bf16[384,256]{1,0:T(8,128)(2,1)S(1)}, u32[]{:S(2)}, u32[]{:S(2)}) collective-permute-start(bf16[384,256]{1,0:T(8,128)(2,1)S(1)} %get-tuple-element.76), channel_id=1, source_target_pairs={{0,1},{1,0},{2,3},{3,2},{4,5},{5,4},{6,7},{7,6},{8,9},{9,8},{10,11... | collective-permute-start | bytes 589832 | tf_op jit(solution)/shard_map/ppermute | solution.py:359
  21.6 1.2 %collective-permute-done.8.refs_0_ = bf16[384,256]{1,0:T(8,128)(2,1)S(1)} collective-permute-done((bf16[384,256]{1,0:T(8,128)(2,1)S(1)}, bf16[384,256]{1,0:T(8,128)(2,1)S(1)}, u32[]{:S(2)}, u32[]{:S(2)}) %collective-permute-start.8) | collective-permute-done | bytes 196640 | tf_op jit(solution)/shard_map/ppermute | solution.py:359
  22.9 1.9 %collective-permute-start.18 = (bf16[784,256]{1,0:T(8,128)(2,1)S(1)}, bf16[784,256]{1,0:T(8,128)(2,1)S(1)}, u32[]{:S(2)}, u32[]{:S(2)}) collective-permute-start(bf16[784,256]{1,0:T(8,128)(2,1)S(1)} %join_cores.3), channel_id=1, source_target_pairs={{0,4},{1,5},{2,0},{3,1},{4,6},{5,7},{6,2},{7,3},{8,12},{9,13},{10,... | collective-permute-start | bytes 1204232 | tf_op jit(solution)/shard_map/ppermute | solution.py:442
  24.8 0.5 %grad_inputs.1 = (bf16[32,2048]{1,0:T(8,128)(2,1)S(1)}, bf16[32,2048]{1,0:T(8,128)(2,1)S(1)}, bf16[32,2048]{1,0:T(8,128)(2,1)S(1)}, bf16[32,2048]{1,0:T(8,128)(2,1)S(1)}) custom-call(bf16[2048,256]{1,0:T(8,128)(2,1)S(1)} %get-tuple-element.51.wd_ref, bf16[128,256]{1,0:T(8,128)(2,1)S(1)} %get-tuple-element.60.gh_ref, ...), custom_call_target="tpu_custom_call" | custom-call | flops 1 | bytes 1 | tf_op jit(solution)/shard_map/grad_inputs/pallas_call | solution.py:39
  25.3 1.6 %collective-permute-start.10 = (bf16[32,2048]{1,0:T(8,128)(2,1)S(1)}, bf16[32,2048]{1,0:T(8,128)(2,1)S(1)}, u32[]{:S(2)}, u32[]{:S(2)}) collective-permute-start(bf16[32,2048]{1,0:T(8,128)(2,1)S(1)} %get-tuple-element.81), channel_id=1, source_target_pairs={{0,8},{8,0},{16,24},{24,16},{1,9},{9,1},{17,25},{25,17},{2,10},{10... | collective-permute-start | bytes 393224 | tf_op jit(solution)/shard_map/ppermute | solution.py:359
  26.9 1.5 %collective-permute-start.11 = (bf16[32,2048]{1,0:T(8,128)(2,1)S(1)}, bf16[32,2048]{1,0:T(8,128)(2,1)S(1)}, u32[]{:S(2)}, u32[]{:S(2)}) collective-permute-start(bf16[32,2048]{1,0:T(8,128)(2,1)S(1)} %get-tuple-element.82), channel_id=1, source_target_pairs={{0,16},{8,24},{16,0},{24,8},{1,17},{9,25},{17,1},{25,9},{2,18},{10... | collective-permute-start | bytes 393224 | tf_op jit(solution)/shard_map/ppermute | solution.py:359
  28.4 0.5 %collective-permute-start.12 = (bf16[32,2048]{1,0:T(8,128)(2,1)S(1)}, bf16[32,2048]{1,0:T(8,128)(2,1)S(1)}, u32[]{:S(2)}, u32[]{:S(2)}) collective-permute-start(bf16[32,2048]{1,0:T(8,128)(2,1)S(1)} %get-tuple-element.83), channel_id=1, source_target_pairs={{0,24},{8,16},{16,8},{24,0},{1,25},{9,17},{17,9},{25,1},{2,26},{10... | collective-permute-start | bytes 393224 | tf_op jit(solution)/shard_map/ppermute | solution.py:359
  28.9 1.5 %collective-permute-done.13.refs_10_.first_ref = bf16[784,256]{1,0:T(8,128)(2,1)S(1)} collective-permute-done((bf16[784,256]{1,0:T(8,128)(2,1)S(1)}, bf16[784,256]{1,0:T(8,128)(2,1)S(1)}, u32[]{:S(2)}, u32[]{:S(2)}) %collective-permute-start.13) | collective-permute-done | bytes 401440 | tf_op jit(solution)/shard_map/ppermute | solution.py:425
  30.3 1.9 %near_sums.1 = (f32[816,256]{1,0:T(8,128)S(1)}, bf16[192,256]{1,0:T(8,128)(2,1)S(1)}, bf16[192,256]{1,0:T(8,128)(2,1)S(1)}, bf16[192,256]{1,0:T(8,128)(2,1)S(1)}, bf16[240,256]{1,0:T(8,128)(2,1)S(1)}) custom-call(bf16[256,2048]{1,0:T(8,128)(2,1)S(1)} %get-tuple-element.52.wu_ref, bf16[2048,256]{1,0:T(8,128)(2,1)S(1)} %get-tuple-element.53.wo_ref, ...), custom_call_target="tpu_custom_call" | custom-call | flops 1000000000 | bytes 1 | tf_op jit(solution)/shard_map/near_sums/pallas_call | solution.py:39
  32.3 0.5 %collective-permute-start.14 = (bf16[192,256]{1,0:T(8,128)(2,1)S(1)}, bf16[192,256]{1,0:T(8,128)(2,1)S(1)}, u32[]{:S(2)}, u32[]{:S(2)}) collective-permute-start(bf16[192,256]{1,0:T(8,128)(2,1)S(1)} %get-tuple-element.90), channel_id=1, source_target_pairs={{0,1},{1,0},{2,3},{3,2},{4,5},{5,4},{6,7},{7,6},{8,9},{9,8},{10,11... | collective-permute-start | bytes 294920 | tf_op jit(solution)/shard_map/ppermute | solution.py:359
  32.8 1.9 %collective-permute-done.11.refs_2_ = bf16[32,2048]{1,0:T(8,128)(2,1)S(1)} collective-permute-done((bf16[32,2048]{1,0:T(8,128)(2,1)S(1)}, bf16[32,2048]{1,0:T(8,128)(2,1)S(1)}, u32[]{:S(2)}, u32[]{:S(2)}) %collective-permute-start.11) | collective-permute-done | bytes 131104 | tf_op jit(solution)/shard_map/ppermute | solution.py:359
  34.7 0.5 %collective-permute-start.16 = (bf16[192,256]{1,0:T(8,128)(2,1)S(1)}, bf16[192,256]{1,0:T(8,128)(2,1)S(1)}, u32[]{:S(2)}, u32[]{:S(2)}) collective-permute-start(bf16[192,256]{1,0:T(8,128)(2,1)S(1)} %get-tuple-element.92), channel_id=1, source_target_pairs={{0,1},{1,0},{2,3},{3,2},{4,5},{5,4},{6,7},{7,6},{8,9},{9,8},{10,11... | collective-permute-start | bytes 294920 | tf_op jit(solution)/shard_map/ppermute | solution.py:359
  35.4 1.5 %place_features.1 = bf16[32,8192]{1,0:T(8,128)(2,1)} custom-call(s32[64]{0:T(128)S(1)} %copy-done.2, bf16[32,2048]{1,0:T(8,128)(2,1)S(1)} %get-tuple-element.80.refs_0_, bf16[32,2048]{1,0:T(8,128)(2,1)S(1)} %collective-permute-done.10.refs_1_, bf16[32,2048]{1,0:T(8,128)(2,1)S(1)} %collective-permute-done.11.refs_2_, ...), custom_call_target="tpu_custom_call" | custom-call | flops 1 | bytes 1 | tf_op jit(solution)/shard_map/place_features/pallas_call | solution.py:39
  37.1 1.0 %collective-permute-done.18.second_ref = bf16[784,256]{1,0:T(8,128)(2,1)S(1)} collective-permute-done((bf16[784,256]{1,0:T(8,128)(2,1)S(1)}, bf16[784,256]{1,0:T(8,128)(2,1)S(1)}, u32[]{:S(2)}, u32[]{:S(2)}) %collective-permute-start.18) | collective-permute-done | bytes 401440 | tf_op jit(solution)/shard_map/ppermute | solution.py:442
  38.1 1.0 %add_up.1 = (f32[96,2048]{1,0:T(8,128)}, f32[1,2048]{1,0:T(1,128)}) custom-call(f32[96,2048]{1,0:T(8,128)S(1)} %get-tuple-element.94.sum_ref, f32[1,2048]{1,0:T(1,128)S(1)} %get-tuple-element.95.near_bias_ref, f32[1,2048]{1,0:T(1,128)S(1)} %get-tuple-element.96.far_bias_ref, bf16[784,256]{1,0:T(8,128)(2,1)S(1)} %collective-permute-done.18.second_ref), custom_call_target="tpu_custom_call" | custom-call | flops 10000000000 | bytes 1 | tf_op jit(solution)/shard_map/add_up/pallas_call | solution.py:39
  (28 shorter events, 1.1 us)
Async XLA Ops:
  0.6 9.1 %copy-start = (bf16[1,128,2048]{2,1,0:T(8,128)(2,1)S(1)}, bf16[1,128,2048]{2,1,0:T(8,128)(2,1)}, u32[]{:S(2)}) copy-start(bf16[1,128,2048]{2,1,0:T(8,128)(2,1)} %param.8) | copy-start | bytes 1572868
  0.6 17.1 %collective-permute-start.3 = (bf16[128,2048]{1,0:T(8,128)(2,1)}, bf16[128,2048]{1,0:T(8,128)(2,1)S(1)}, u32[]{:S(2)}, u32[]{:S(2)}) collective-permute-start(bf16[128,2048]{1,0:T(8,128)(2,1)} %bitcast.5), channel_id=1, source_target_pairs={{0,1},{1,0},{2,4},{3,5},{4,2},{5,3},{6,7},{7,6},{8,9},{9,8},{10,12... | collective-permute-start | bytes 1572872 | tf_op jit(solution)/shard_map/ppermute | solution.py:387
  1.2 18.1 %collective-permute-start.5 = (bf16[128,2048]{1,0:T(8,128)(2,1)}, bf16[128,2048]{1,0:T(8,128)(2,1)S(1)}, u32[]{:S(2)}, u32[]{:S(2)}) collective-permute-start(bf16[128,2048]{1,0:T(8,128)(2,1)} %bitcast.6), channel_id=1, source_target_pairs={{0,2},{1,3},{2,0},{3,1},{4,6},{5,7},{6,4},{7,5},{8,10},{9,11},{10,... | collective-permute-start | bytes 1572872 | tf_op jit(solution)/shard_map/ppermute | solution.py:359
  5.3 0.8 %copy-start.3 = (bf16[32,1024]{1,0:T(8,128)(2,1)S(1)}, bf16[32,1024]{1,0:T(8,128)(2,1)}, u32[]{:S(2)}) copy-start(bf16[32,1024]{1,0:T(8,128)(2,1)} %grad_ref.1) | copy-start | bytes 196612
  6.2 3.6 %copy-start.1 = (f32[1,2048]{1,0:T(1,128)S(1)}, f32[1,2048]{1,0:T(1,128)}, u32[]{:S(2)}) copy-start(f32[1,2048]{1,0:T(1,128)} %bias_ref.5) | copy-start | bytes 24580
  6.2 5.7 %collective-permute-start = (bf16[32,256]{1,0:T(8,128)(2,1)S(1)}, bf16[32,256]{1,0:T(8,128)(2,1)S(1)}, u32[]{:S(2)}, u32[]{:S(2)}) collective-permute-start(bf16[32,256]{1,0:T(8,128)(2,1)S(1)} %get-tuple-element.56), channel_id=1, source_target_pairs={{0,24},{8,16},{16,8},{24,0},{1,25},{9,17},{17,9},{25,1},{2,26},{10... | collective-permute-start | bytes 49160 | tf_op jit(solution)/shard_map/ppermute | solution.py:359
  8.7 3.7 %collective-permute-start.1 = (bf16[32,256]{1,0:T(8,128)(2,1)S(1)}, bf16[32,256]{1,0:T(8,128)(2,1)S(1)}, u32[]{:S(2)}, u32[]{:S(2)}) collective-permute-start(bf16[32,256]{1,0:T(8,128)(2,1)S(1)} %get-tuple-element.57), channel_id=1, source_target_pairs={{0,16},{8,24},{16,0},{24,8},{1,17},{9,25},{17,1},{25,9},{2,18},{10... | collective-permute-start | bytes 49160 | tf_op jit(solution)/shard_map/ppermute | solution.py:359
  9.2 3.7 %collective-permute-start.2 = (bf16[32,256]{1,0:T(8,128)(2,1)S(1)}, bf16[32,256]{1,0:T(8,128)(2,1)S(1)}, u32[]{:S(2)}, u32[]{:S(2)}) collective-permute-start(bf16[32,256]{1,0:T(8,128)(2,1)S(1)} %get-tuple-element.58), channel_id=1, source_target_pairs={{0,8},{8,0},{16,24},{24,16},{1,9},{9,1},{17,25},{25,17},{2,10},{10... | collective-permute-start | bytes 49160 | tf_op jit(solution)/shard_map/ppermute | solution.py:359
  14.4 1.8 %collective-permute-start.4 = (bf16[784,256]{1,0:T(8,128)(2,1)S(1)}, bf16[784,256]{1,0:T(8,128)(2,1)S(1)}, u32[]{:S(2)}, u32[]{:S(2)}) collective-permute-start(bf16[784,256]{1,0:T(8,128)(2,1)S(1)} %get-tuple-element.67), channel_id=1, source_target_pairs={{0,1},{1,0},{2,3},{3,2},{4,5},{5,4},{6,7},{7,6},{8,9},{9,8},{10,11... | collective-permute-start | bytes 1204232 | tf_op jit(solution)/shard_map/ppermute | solution.py:359
  14.5 5.6 %collective-permute-start.7 = (bf16[128,256]{1,0:T(8,128)(2,1)S(1)}, bf16[128,256]{1,0:T(8,128)(2,1)S(1)}, u32[]{:S(2)}, u32[]{:S(2)}) collective-permute-start(bf16[128,256]{1,0:T(8,128)(2,1)S(1)} %get-tuple-element.70), channel_id=1, source_target_pairs={{0,1},{1,0},{2,4},{3,5},{4,2},{5,3},{6,7},{7,6},{8,9},{9,8},{10,12... | collective-permute-start | bytes 196616 | tf_op jit(solution)/shard_map/ppermute | solution.py:420
  15.0 4.3 %collective-permute-start.6 = (bf16[128,256]{1,0:T(8,128)(2,1)S(1)}, bf16[128,256]{1,0:T(8,128)(2,1)S(1)}, u32[]{:S(2)}, u32[]{:S(2)}) collective-permute-start(bf16[128,256]{1,0:T(8,128)(2,1)S(1)} %get-tuple-element.70), channel_id=1, source_target_pairs={{0,2},{1,3},{2,0},{3,1},{4,6},{5,7},{6,4},{7,5},{8,10},{9,11},{10,... | collective-permute-start | bytes 196616 | tf_op jit(solution)/shard_map/ppermute | solution.py:359
  16.3 14.0 %collective-permute-start.13 = (bf16[784,256]{1,0:T(8,128)(2,1)S(1)}, bf16[784,256]{1,0:T(8,128)(2,1)S(1)}, u32[]{:S(2)}, u32[]{:S(2)}) collective-permute-start(bf16[784,256]{1,0:T(8,128)(2,1)S(1)} %join_cores.2), channel_id=1, source_target_pairs={{0,6},{1,7},{2,3},{3,2},{4,5},{5,4},{6,0},{7,1},{8,14},{9,15},{10,... | collective-permute-start | bytes 1204232 | tf_op jit(solution)/shard_map/ppermute | solution.py:425
  21.0 1.8 %collective-permute-start.9 = (bf16[400,256]{1,0:T(8,128)(2,1)S(1)}, bf16[400,256]{1,0:T(8,128)(2,1)S(1)}, u32[]{:S(2)}, u32[]{:S(2)}) collective-permute-start(bf16[400,256]{1,0:T(8,128)(2,1)S(1)} %get-tuple-element.77), channel_id=1, source_target_pairs={{0,1},{1,0},{2,3},{3,2},{4,5},{5,4},{6,7},{7,6},{8,9},{9,8},{10,11... | collective-permute-start | bytes 614408 | tf_op jit(solution)/shard_map/ppermute | solution.py:359
  21.1 1.7 %collective-permute-start.8 = (bf16[384,256]{1,0:T(8,128)(2,1)S(1)}, bf16[384,256]{1,0:T(8,128)(2,1)S(1)}, u32[]{:S(2)}, u32[]{:S(2)}) collective-permute-start(bf16[384,256]{1,0:T(8,128)(2,1)S(1)} %get-tuple-element.76), channel_id=1, source_target_pairs={{0,1},{1,0},{2,3},{3,2},{4,5},{5,4},{6,7},{7,6},{8,9},{9,8},{10,11... | collective-permute-start | bytes 589832 | tf_op jit(solution)/shard_map/ppermute | solution.py:359
  22.9 15.2 %collective-permute-start.18 = (bf16[784,256]{1,0:T(8,128)(2,1)S(1)}, bf16[784,256]{1,0:T(8,128)(2,1)S(1)}, u32[]{:S(2)}, u32[]{:S(2)}) collective-permute-start(bf16[784,256]{1,0:T(8,128)(2,1)S(1)} %join_cores.3), channel_id=1, source_target_pairs={{0,4},{1,5},{2,0},{3,1},{4,6},{5,7},{6,2},{7,3},{8,12},{9,13},{10,... | collective-permute-start | bytes 1204232 | tf_op jit(solution)/shard_map/ppermute | solution.py:442
  25.3 7.0 %collective-permute-start.10 = (bf16[32,2048]{1,0:T(8,128)(2,1)S(1)}, bf16[32,2048]{1,0:T(8,128)(2,1)S(1)}, u32[]{:S(2)}, u32[]{:S(2)}) collective-permute-start(bf16[32,2048]{1,0:T(8,128)(2,1)S(1)} %get-tuple-element.81), channel_id=1, source_target_pairs={{0,8},{8,0},{16,24},{24,16},{1,9},{9,1},{17,25},{25,17},{2,10},{10... | collective-permute-start | bytes 393224 | tf_op jit(solution)/shard_map/ppermute | solution.py:359
  26.9 7.9 %collective-permute-start.11 = (bf16[32,2048]{1,0:T(8,128)(2,1)S(1)}, bf16[32,2048]{1,0:T(8,128)(2,1)S(1)}, u32[]{:S(2)}, u32[]{:S(2)}) collective-permute-start(bf16[32,2048]{1,0:T(8,128)(2,1)S(1)} %get-tuple-element.82), channel_id=1, source_target_pairs={{0,16},{8,24},{16,0},{24,8},{1,17},{9,25},{17,1},{25,9},{2,18},{10... | collective-permute-start | bytes 393224 | tf_op jit(solution)/shard_map/ppermute | solution.py:359
  28.4 6.3 %collective-permute-start.12 = (bf16[32,2048]{1,0:T(8,128)(2,1)S(1)}, bf16[32,2048]{1,0:T(8,128)(2,1)S(1)}, u32[]{:S(2)}, u32[]{:S(2)}) collective-permute-start(bf16[32,2048]{1,0:T(8,128)(2,1)S(1)} %get-tuple-element.83), channel_id=1, source_target_pairs={{0,24},{8,16},{16,8},{24,0},{1,25},{9,17},{17,9},{25,1},{2,26},{10... | collective-permute-start | bytes 393224 | tf_op jit(solution)/shard_map/ppermute | solution.py:359
  32.2 4.7 %collective-permute-start.17 = (bf16[240,256]{1,0:T(8,128)(2,1)S(1)}, bf16[240,256]{1,0:T(8,128)(2,1)S(1)}, u32[]{:S(2)}, u32[]{:S(2)}) collective-permute-start(bf16[240,256]{1,0:T(8,128)(2,1)S(1)} %get-tuple-element.93), channel_id=1, source_target_pairs={{0,1},{1,0},{2,3},{3,2},{4,5},{5,4},{6,7},{7,6},{8,9},{9,8},{10,11... | collective-permute-start | bytes 368648 | tf_op jit(solution)/shard_map/ppermute | solution.py:359
  32.3 4.6 %collective-permute-start.14 = (bf16[192,256]{1,0:T(8,128)(2,1)S(1)}, bf16[192,256]{1,0:T(8,128)(2,1)S(1)}, u32[]{:S(2)}, u32[]{:S(2)}) collective-permute-start(bf16[192,256]{1,0:T(8,128)(2,1)S(1)} %get-tuple-element.90), channel_id=1, source_target_pairs={{0,1},{1,0},{2,3},{3,2},{4,5},{5,4},{6,7},{7,6},{8,9},{9,8},{10,11... | collective-permute-start | bytes 294920 | tf_op jit(solution)/shard_map/ppermute | solution.py:359
  34.7 0.7 %copy-start.2 = (s32[64]{0:T(128)S(1)}, s32[64]{0:T(128)}, u32[]{:S(2)}) copy-start(s32[64]{0:T(128)} %assign_ref.1) | copy-start | bytes 772
  34.7 2.2 %collective-permute-start.15 = (bf16[192,256]{1,0:T(8,128)(2,1)S(1)}, bf16[192,256]{1,0:T(8,128)(2,1)S(1)}, u32[]{:S(2)}, u32[]{:S(2)}) collective-permute-start(bf16[192,256]{1,0:T(8,128)(2,1)S(1)} %get-tuple-element.91), channel_id=1, source_target_pairs={{0,1},{1,0},{2,3},{3,2},{4,5},{5,4},{6,7},{7,6},{8,9},{9,8},{10,11... | collective-permute-start | bytes 294920 | tf_op jit(solution)/shard_map/ppermute | solution.py:359
  34.7 2.2 %collective-permute-start.16 = (bf16[192,256]{1,0:T(8,128)(2,1)S(1)}, bf16[192,256]{1,0:T(8,128)(2,1)S(1)}, u32[]{:S(2)}, u32[]{:S(2)}) collective-permute-start(bf16[192,256]{1,0:T(8,128)(2,1)S(1)} %get-tuple-element.92), channel_id=1, source_target_pairs={{0,1},{1,0},{2,3},{3,2},{4,5},{5,4},{6,7},{7,6},{8,9},{9,8},{10,11... | collective-permute-start | bytes 294920 | tf_op jit(solution)/shard_map/ppermute | solution.py:359

commit v8 on v6

--- a/solution.py
+++ b/solution.py
@@ -312,12 +312,12 @@
         copies.append(pltpu.make_async_copy(source, target, sem_ref.at[i]))
         copies[-1].start()
 
+    bg_ref[...] = near_bias_ref[...] + (far_bias_ref[...] + bias_of(second_ref[-TILE:, :].astype(F32), n_slabs))
+    write(bg_ref, bg_out, n_slabs)
     for j in range(n_slabs):
         c, rows = slice(j * SLAB, (j + 1) * SLAB), slice(j * block, (j + 1) * block)
         total_ref[:, c] = sum_ref[:, c] + second_ref[rows, :].astype(F32) * scale
         write(total_ref.at[:, pl.ds(j * SLAB, SLAB)], out_ref.at[:, pl.ds(j * SLAB, SLAB)], j)
-    bg_ref[...] = near_bias_ref[...] + (far_bias_ref[...] + bias_of(second_ref[-TILE:, :].astype(F32), n_slabs))
-    write(bg_ref, bg_out, n_slabs)
     for copy in copies:
         copy.wait()
 

time: 39.3 us -> 39.3 us (level)
  no operation moved by 1% of the time
where the time goes in v8:
time: 39.3 us; the launch traced here: 39.1 us
  starting transfers between devices  18.2 us (46%)
  Pallas kernels  10.8 us (27%)
  waiting for transfers between devices  8.36 us (21%)
  local copies, waits for them, and re-layouts  0.99 us (3%)
  between operations  0.81 us (2%)
    ppermute x15, starting transfers between devices, across(): return lax.ppermute(value, axis, xor_pairs(lax.axis_size(axis), k))  13.9 us
    pallas_call x14, Pallas kernels, call(): pl.pallas_call(kernel, out_shape=outs, in_specs=[pl.BlockSpec(memory_spac...  10.8 us
    ppermute x15, waiting for transfers between devices, across(): return lax.ppermute(value, axis, xor_pairs(lax.axis_size(axis), k))  5.89 us
    ppermute x1, starting transfers between devices, paired_body(): from_second = lax.ppermute(second_sum, 'shard', second)  1.87 us
    ppermute x1, waiting for transfers between devices, paired_body(): from_first = lax.ppermute(first, 'shard', outer)  1.46 us
    ppermute x1, starting transfers between devices, paired_body(): from_first = lax.ppermute(first, 'shard', outer)  1.42 us
    ppermute x1, waiting for transfers between devices, paired_body(): from_second = lax.ppermute(second_sum, 'shard', second)  1 us
    unnamed x8, local copies, waits for them, and re-layouts  0.99 us
  transfers between devices with their start and end apart: 19, of which 8 were waited for; matrix products, arithmetic and copies ran while one was open for 0% of the time, Pallas kernels for 25%

profile of v8, /device:TPU:0, one launch (start us, length us, event | category | flops | bytes accessed | tf_op | source)
XLA Modules:
  0.0 39.1 jit_solution(14645938906385328322)
XLA Ops:
  0.6 0.5 %collective-permute-start.3 = (bf16[128,2048]{1,0:T(8,128)(2,1)}, bf16[128,2048]{1,0:T(8,128)(2,1)S(1)}, u32[]{:S(2)}, u32[]{:S(2)}) collective-permute-start(bf16[128,2048]{1,0:T(8,128)(2,1)} %bitcast.5), channel_id=1, source_target_pairs={{0,1},{1,0},{2,4},{3,5},{4,2},{5,3},{6,7},{7,6},{8,9},{9,8},{10,12... | collective-permute-start | bytes 1572872 | tf_op jit(solution)/shard_map/ppermute | solution.py:387
  1.2 4.1 %collective-permute-start.5 = (bf16[128,2048]{1,0:T(8,128)(2,1)}, bf16[128,2048]{1,0:T(8,128)(2,1)S(1)}, u32[]{:S(2)}, u32[]{:S(2)}) collective-permute-start(bf16[128,2048]{1,0:T(8,128)(2,1)} %bitcast.6), channel_id=1, source_target_pairs={{0,2},{1,3},{2,0},{3,1},{4,6},{5,7},{6,4},{7,5},{8,10},{9,11},{10,... | collective-permute-start | bytes 1572872 | tf_op jit(solution)/shard_map/ppermute | solution.py:359
  5.3 0.8 %copy-done.3 = bf16[32,1024]{1,0:T(8,128)(2,1)S(1)} copy-done((bf16[32,1024]{1,0:T(8,128)(2,1)S(1)}, bf16[32,1024]{1,0:T(8,128)(2,1)}, u32[]{:S(2)}) %copy-start.3) | copy-done | bytes 65560
  6.2 2.5 %collective-permute-start = (bf16[32,256]{1,0:T(8,128)(2,1)S(1)}, bf16[32,256]{1,0:T(8,128)(2,1)S(1)}, u32[]{:S(2)}, u32[]{:S(2)}) collective-permute-start(bf16[32,256]{1,0:T(8,128)(2,1)S(1)} %get-tuple-element.56), channel_id=1, source_target_pairs={{0,24},{8,16},{16,8},{24,0},{1,25},{9,17},{17,9},{25,1},{2,26},{10... | collective-permute-start | bytes 49160 | tf_op jit(solution)/shard_map/ppermute | solution.py:359
  8.7 0.5 %collective-permute-start.1 = (bf16[32,256]{1,0:T(8,128)(2,1)S(1)}, bf16[32,256]{1,0:T(8,128)(2,1)S(1)}, u32[]{:S(2)}, u32[]{:S(2)}) collective-permute-start(bf16[32,256]{1,0:T(8,128)(2,1)S(1)} %get-tuple-element.57), channel_id=1, source_target_pairs={{0,16},{8,24},{16,0},{24,8},{1,17},{9,25},{17,1},{25,9},{2,18},{10... | collective-permute-start | bytes 49160 | tf_op jit(solution)/shard_map/ppermute | solution.py:359
  9.2 0.5 %collective-permute-start.2 = (bf16[32,256]{1,0:T(8,128)(2,1)S(1)}, bf16[32,256]{1,0:T(8,128)(2,1)S(1)}, u32[]{:S(2)}, u32[]{:S(2)}) collective-permute-start(bf16[32,256]{1,0:T(8,128)(2,1)S(1)} %get-tuple-element.58), channel_id=1, source_target_pairs={{0,8},{8,0},{16,24},{24,16},{1,9},{9,1},{17,25},{25,17},{2,10},{10... | collective-permute-start | bytes 49160 | tf_op jit(solution)/shard_map/ppermute | solution.py:359
  9.8 2.1 %forward_own.1 = (bf16[2048,256]{1,0:T(8,128)(2,1)S(1)}, bf16[256,2048]{1,0:T(8,128)(2,1)S(1)}, bf16[2048,256]{1,0:T(8,128)(2,1)S(1)}, bf16[128,2048]{1,0:T(8,12...) custom-call(bf16[2048,256]{1,0:T(8,128)(2,1)} %bitcast.8, ...), custom_call_target="tpu_custom_call" | custom-call | flops 1 | bytes 1 | tf_op jit(solution)/shard_map/forward_own/pallas_call | solution.py:39
  11.9 0.5 %collective-permute-done.1.refs_1_ = bf16[32,256]{1,0:T(8,128)(2,1)S(1)} collective-permute-done((bf16[32,256]{1,0:T(8,128)(2,1)S(1)}, bf16[32,256]{1,0:T(8,128)(2,1)S(1)}, u32[]{:S(2)}, u32[]{:S(2)}) %collective-permute-start.1) | collective-permute-done | bytes 16416 | tf_op jit(solution)/shard_map/ppermute | solution.py:359
  12.5 0.5 %collective-permute-done.2.refs_2_ = bf16[32,256]{1,0:T(8,128)(2,1)S(1)} collective-permute-done((bf16[32,256]{1,0:T(8,128)(2,1)S(1)}, bf16[32,256]{1,0:T(8,128)(2,1)S(1)}, u32[]{:S(2)}, u32[]{:S(2)}) %collective-permute-start.2) | collective-permute-done | bytes 16416 | tf_op jit(solution)/shard_map/ppermute | solution.py:359
  13.0 1.1 %backward_own.1 = (bf16[128,256]{1,0:T(8,128)(2,1)S(1)}, bf16[128,256]{1,0:T(8,128)(2,1)S(1)}, bf16[768,128]{1,0:T(8,128)(2,1)S(1)}, bf16[128,2048]{1,0:T(8,128)...) custom-call(bf16[256,2048]{1,0:T(8,128)(2,1)S(1)} %get-tuple-element.52.wu_ref, ...), custom_call_target="tpu_custom_call" | custom-call | flops 1 | bytes 1 | tf_op jit(solution)/shard_map/backward_own/pallas_call | solution.py:39
  14.1 0.4 first_sums.1
  14.5 0.5 %collective-permute-start.7 = (bf16[128,256]{1,0:T(8,128)(2,1)S(1)}, bf16[128,256]{1,0:T(8,128)(2,1)S(1)}, u32[]{:S(2)}, u32[]{:S(2)}) collective-permute-start(bf16[128,256]{1,0:T(8,128)(2,1)S(1)} %get-tuple-element.70), channel_id=1, source_target_pairs={{0,1},{1,0},{2,4},{3,5},{4,2},{5,3},{6,7},{7,6},{8,9},{9,8},{10,12... | collective-permute-start | bytes 196616 | tf_op jit(solution)/shard_map/ppermute | solution.py:420
  15.0 0.9 %collective-permute-start.6 = (bf16[128,256]{1,0:T(8,128)(2,1)S(1)}, bf16[128,256]{1,0:T(8,128)(2,1)S(1)}, u32[]{:S(2)}, u32[]{:S(2)}) collective-permute-start(bf16[128,256]{1,0:T(8,128)(2,1)S(1)} %get-tuple-element.70), channel_id=1, source_target_pairs={{0,2},{1,3},{2,0},{3,1},{4,6},{5,7},{6,4},{7,5},{8,10},{9,11},{10,... | collective-permute-start | bytes 196616 | tf_op jit(solution)/shard_map/ppermute | solution.py:359
  16.4 1.4 %collective-permute-start.13 = (bf16[784,256]{1,0:T(8,128)(2,1)S(1)}, bf16[784,256]{1,0:T(8,128)(2,1)S(1)}, u32[]{:S(2)}, u32[]{:S(2)}) collective-permute-start(bf16[784,256]{1,0:T(8,128)(2,1)S(1)} %join_cores.2), channel_id=1, source_target_pairs={{0,6},{1,7},{2,3},{3,2},{4,5},{5,4},{6,0},{7,1},{8,14},{9,15},{10,... | collective-permute-start | bytes 1204232 | tf_op jit(solution)/shard_map/ppermute | solution.py:425
  17.8 1.5 %collective-permute-done.6.g_ref = bf16[128,256]{1,0:T(8,128)(2,1)S(1)} collective-permute-done((bf16[128,256]{1,0:T(8,128)(2,1)S(1)}, bf16[128,256]{1,0:T(8,128)(2,1)S(1)}, u32[]{:S(2)}, u32[]{:S(2)}) %collective-permute-start.6) | collective-permute-done | bytes 65568 | tf_op jit(solution)/shard_map/ppermute | solution.py:359
  19.3 0.8 %forward_other.1 = (bf16[128,256]{1,0:T(8,128)(2,1)S(1)}, bf16[128,2048]{1,0:T(8,128)(2,1)S(1)}) custom-call(bf16[128,2048]{1,0:T(8,128)(2,1)S(1)} %collective-permute-done.5.x_ref, bf16[2048,256]{1,0:T(8,128)(2,1)S(1)} %get-tuple-element.51.wd_ref, bf16[256,2048]{1,0:T(8,128)(2,1)S(1)} %get-tuple-element.52.wu_ref, f32[1,2048]{1,0:T(1,128)S(1)} %copy-done.1), custom_call_target="tpu_custom_call" | custom-call | flops 1000000000 | bytes 1 | tf_op jit(solution)/shard_map/forward_other/pallas_call | solution.py:39
  20.1 1.0 %second_sums.1 = (bf16[128,2048]{1,0:T(8,128)(2,1)S(1)}, bf16[768,128]{1,0:T(8,128)(2,1)S(1)}, f32[1,2048]{1,0:T(1,128)S(1)}, f32[784,256]{1,0:T(8,128)S(1)}, bf...) custom-call(bf16[256,2048]{1,0:T(8,128)(2,1)S(1)} %get-tuple-element.52.wu_ref, ...), custom_call_target="tpu_custom_call" | custom-call | flops 1000000000 | bytes 1 | tf_op jit(solution)/shard_map/second_sums/pallas_call | solution.py:39
  21.2 0.5 %collective-permute-start.8 = (bf16[384,256]{1,0:T(8,128)(2,1)S(1)}, bf16[384,256]{1,0:T(8,128)(2,1)S(1)}, u32[]{:S(2)}, u32[]{:S(2)}) collective-permute-start(bf16[384,256]{1,0:T(8,128)(2,1)S(1)} %get-tuple-element.76), channel_id=1, source_target_pairs={{0,1},{1,0},{2,3},{3,2},{4,5},{5,4},{6,7},{7,6},{8,9},{9,8},{10,11... | collective-permute-start | bytes 589832 | tf_op jit(solution)/shard_map/ppermute | solution.py:359
  21.7 1.2 %collective-permute-done.8.refs_0_ = bf16[384,256]{1,0:T(8,128)(2,1)S(1)} collective-permute-done((bf16[384,256]{1,0:T(8,128)(2,1)S(1)}, bf16[384,256]{1,0:T(8,128)(2,1)S(1)}, u32[]{:S(2)}, u32[]{:S(2)}) %collective-permute-start.8) | collective-permute-done | bytes 196640 | tf_op jit(solution)/shard_map/ppermute | solution.py:359
  23.0 1.9 %collective-permute-start.18 = (bf16[784,256]{1,0:T(8,128)(2,1)S(1)}, bf16[784,256]{1,0:T(8,128)(2,1)S(1)}, u32[]{:S(2)}, u32[]{:S(2)}) collective-permute-start(bf16[784,256]{1,0:T(8,128)(2,1)S(1)} %join_cores.3), channel_id=1, source_target_pairs={{0,4},{1,5},{2,0},{3,1},{4,6},{5,7},{6,2},{7,3},{8,12},{9,13},{10,... | collective-permute-start | bytes 1204232 | tf_op jit(solution)/shard_map/ppermute | solution.py:442
  24.9 0.5 %grad_inputs.1 = (bf16[32,2048]{1,0:T(8,128)(2,1)S(1)}, bf16[32,2048]{1,0:T(8,128)(2,1)S(1)}, bf16[32,2048]{1,0:T(8,128)(2,1)S(1)}, bf16[32,2048]{1,0:T(8,128)(2,1)S(1)}) custom-call(bf16[2048,256]{1,0:T(8,128)(2,1)S(1)} %get-tuple-element.51.wd_ref, bf16[128,256]{1,0:T(8,128)(2,1)S(1)} %get-tuple-element.60.gh_ref, ...), custom_call_target="tpu_custom_call" | custom-call | flops 1 | bytes 1 | tf_op jit(solution)/shard_map/grad_inputs/pallas_call | solution.py:39
  25.4 1.5 %collective-permute-start.10 = (bf16[32,2048]{1,0:T(8,128)(2,1)S(1)}, bf16[32,2048]{1,0:T(8,128)(2,1)S(1)}, u32[]{:S(2)}, u32[]{:S(2)}) collective-permute-start(bf16[32,2048]{1,0:T(8,128)(2,1)S(1)} %get-tuple-element.81), channel_id=1, source_target_pairs={{0,8},{8,0},{16,24},{24,16},{1,9},{9,1},{17,25},{25,17},{2,10},{10... | collective-permute-start | bytes 393224 | tf_op jit(solution)/shard_map/ppermute | solution.py:359
  26.9 1.5 %collective-permute-start.11 = (bf16[32,2048]{1,0:T(8,128)(2,1)S(1)}, bf16[32,2048]{1,0:T(8,128)(2,1)S(1)}, u32[]{:S(2)}, u32[]{:S(2)}) collective-permute-start(bf16[32,2048]{1,0:T(8,128)(2,1)S(1)} %get-tuple-element.82), channel_id=1, source_target_pairs={{0,16},{8,24},{16,0},{24,8},{1,17},{9,25},{17,1},{25,9},{2,18},{10... | collective-permute-start | bytes 393224 | tf_op jit(solution)/shard_map/ppermute | solution.py:359
  28.5 0.5 %collective-permute-start.12 = (bf16[32,2048]{1,0:T(8,128)(2,1)S(1)}, bf16[32,2048]{1,0:T(8,128)(2,1)S(1)}, u32[]{:S(2)}, u32[]{:S(2)}) collective-permute-start(bf16[32,2048]{1,0:T(8,128)(2,1)S(1)} %get-tuple-element.83), channel_id=1, source_target_pairs={{0,24},{8,16},{16,8},{24,0},{1,25},{9,17},{17,9},{25,1},{2,26},{10... | collective-permute-start | bytes 393224 | tf_op jit(solution)/shard_map/ppermute | solution.py:359
  28.9 1.5 %collective-permute-done.13.refs_10_.first_ref = bf16[784,256]{1,0:T(8,128)(2,1)S(1)} collective-permute-done((bf16[784,256]{1,0:T(8,128)(2,1)S(1)}, bf16[784,256]{1,0:T(8,128)(2,1)S(1)}, u32[]{:S(2)}, u32[]{:S(2)}) %collective-permute-start.13) | collective-permute-done | bytes 401440 | tf_op jit(solution)/shard_map/ppermute | solution.py:425
  30.4 1.9 %near_sums.1 = (f32[816,256]{1,0:T(8,128)S(1)}, bf16[192,256]{1,0:T(8,128)(2,1)S(1)}, bf16[192,256]{1,0:T(8,128)(2,1)S(1)}, bf16[192,256]{1,0:T(8,128)(2,1)S(1)}, bf16[240,256]{1,0:T(8,128)(2,1)S(1)}) custom-call(bf16[256,2048]{1,0:T(8,128)(2,1)S(1)} %get-tuple-element.52.wu_ref, bf16[2048,256]{1,0:T(8,128)(2,1)S(1)} %get-tuple-element.53.wo_ref, ...), custom_call_target="tpu_custom_call" | custom-call | flops 1000000000 | bytes 1 | tf_op jit(solution)/shard_map/near_sums/pallas_call | solution.py:39
  32.4 0.5 %collective-permute-start.14 = (bf16[192,256]{1,0:T(8,128)(2,1)S(1)}, bf16[192,256]{1,0:T(8,128)(2,1)S(1)}, u32[]{:S(2)}, u32[]{:S(2)}) collective-permute-start(bf16[192,256]{1,0:T(8,128)(2,1)S(1)} %get-tuple-element.90), channel_id=1, source_target_pairs={{0,1},{1,0},{2,3},{3,2},{4,5},{5,4},{6,7},{7,6},{8,9},{9,8},{10,11... | collective-permute-start | bytes 294920 | tf_op jit(solution)/shard_map/ppermute | solution.py:359
  32.9 1.9 %collective-permute-done.11.refs_2_ = bf16[32,2048]{1,0:T(8,128)(2,1)S(1)} collective-permute-done((bf16[32,2048]{1,0:T(8,128)(2,1)S(1)}, bf16[32,2048]{1,0:T(8,128)(2,1)S(1)}, u32[]{:S(2)}, u32[]{:S(2)}) %collective-permute-start.11) | collective-permute-done | bytes 131104 | tf_op jit(solution)/shard_map/ppermute | solution.py:359
  34.8 0.5 %collective-permute-start.16 = (bf16[192,256]{1,0:T(8,128)(2,1)S(1)}, bf16[192,256]{1,0:T(8,128)(2,1)S(1)}, u32[]{:S(2)}, u32[]{:S(2)}) collective-permute-start(bf16[192,256]{1,0:T(8,128)(2,1)S(1)} %get-tuple-element.92), channel_id=1, source_target_pairs={{0,1},{1,0},{2,3},{3,2},{4,5},{5,4},{6,7},{7,6},{8,9},{9,8},{10,11... | collective-permute-start | bytes 294920 | tf_op jit(solution)/shard_map/ppermute | solution.py:359
  35.5 1.5 %place_features.1 = bf16[32,8192]{1,0:T(8,128)(2,1)} custom-call(s32[64]{0:T(128)S(1)} %copy-done.2, bf16[32,2048]{1,0:T(8,128)(2,1)S(1)} %get-tuple-element.80.refs_0_, bf16[32,2048]{1,0:T(8,128)(2,1)S(1)} %collective-permute-done.10.refs_1_, bf16[32,2048]{1,0:T(8,128)(2,1)S(1)} %collective-permute-done.11.refs_2_, ...), custom_call_target="tpu_custom_call" | custom-call | flops 1 | bytes 1 | tf_op jit(solution)/shard_map/place_features/pallas_call | solution.py:39
  37.2 1.0 %collective-permute-done.18.second_ref = bf16[784,256]{1,0:T(8,128)(2,1)S(1)} collective-permute-done((bf16[784,256]{1,0:T(8,128)(2,1)S(1)}, bf16[784,256]{1,0:T(8,128)(2,1)S(1)}, u32[]{:S(2)}, u32[]{:S(2)}) %collective-permute-start.18) | collective-permute-done | bytes 401440 | tf_op jit(solution)/shard_map/ppermute | solution.py:442
  38.2 1.0 %add_up.1 = (f32[96,2048]{1,0:T(8,128)}, f32[1,2048]{1,0:T(1,128)}) custom-call(f32[96,2048]{1,0:T(8,128)S(1)} %get-tuple-element.94.sum_ref, f32[1,2048]{1,0:T(1,128)S(1)} %get-tuple-element.95.near_bias_ref, f32[1,2048]{1,0:T(1,128)S(1)} %get-tuple-element.96.far_bias_ref, bf16[784,256]{1,0:T(8,128)(2,1)S(1)} %collective-permute-done.18.second_ref), custom_call_target="tpu_custom_call" | custom-call | flops 10000000000 | bytes 1 | tf_op jit(solution)/shard_map/add_up/pallas_call | solution.py:39
  (28 shorter events, 1.1 us)
Async XLA Ops:
  0.6 9.1 %copy-start = (bf16[1,128,2048]{2,1,0:T(8,128)(2,1)S(1)}, bf16[1,128,2048]{2,1,0:T(8,128)(2,1)}, u32[]{:S(2)}) copy-start(bf16[1,128,2048]{2,1,0:T(8,128)(2,1)} %param.8) | copy-start | bytes 1572868
  0.6 17.1 %collective-permute-start.3 = (bf16[128,2048]{1,0:T(8,128)(2,1)}, bf16[128,2048]{1,0:T(8,128)(2,1)S(1)}, u32[]{:S(2)}, u32[]{:S(2)}) collective-permute-start(bf16[128,2048]{1,0:T(8,128)(2,1)} %bitcast.5), channel_id=1, source_target_pairs={{0,1},{1,0},{2,4},{3,5},{4,2},{5,3},{6,7},{7,6},{8,9},{9,8},{10,12... | collective-permute-start | bytes 1572872 | tf_op jit(solution)/shard_map/ppermute | solution.py:387
  1.2 18.1 %collective-permute-start.5 = (bf16[128,2048]{1,0:T(8,128)(2,1)}, bf16[128,2048]{1,0:T(8,128)(2,1)S(1)}, u32[]{:S(2)}, u32[]{:S(2)}) collective-permute-start(bf16[128,2048]{1,0:T(8,128)(2,1)} %bitcast.6), channel_id=1, source_target_pairs={{0,2},{1,3},{2,0},{3,1},{4,6},{5,7},{6,4},{7,5},{8,10},{9,11},{10,... | collective-permute-start | bytes 1572872 | tf_op jit(solution)/shard_map/ppermute | solution.py:359
  5.3 0.8 %copy-start.3 = (bf16[32,1024]{1,0:T(8,128)(2,1)S(1)}, bf16[32,1024]{1,0:T(8,128)(2,1)}, u32[]{:S(2)}) copy-start(bf16[32,1024]{1,0:T(8,128)(2,1)} %grad_ref.1) | copy-start | bytes 196612
  6.2 3.6 %copy-start.1 = (f32[1,2048]{1,0:T(1,128)S(1)}, f32[1,2048]{1,0:T(1,128)}, u32[]{:S(2)}) copy-start(f32[1,2048]{1,0:T(1,128)} %bias_ref.5) | copy-start | bytes 24580
  6.2 5.7 %collective-permute-start = (bf16[32,256]{1,0:T(8,128)(2,1)S(1)}, bf16[32,256]{1,0:T(8,128)(2,1)S(1)}, u32[]{:S(2)}, u32[]{:S(2)}) collective-permute-start(bf16[32,256]{1,0:T(8,128)(2,1)S(1)} %get-tuple-element.56), channel_id=1, source_target_pairs={{0,24},{8,16},{16,8},{24,0},{1,25},{9,17},{17,9},{25,1},{2,26},{10... | collective-permute-start | bytes 49160 | tf_op jit(solution)/shard_map/ppermute | solution.py:359
  8.7 3.7 %collective-permute-start.1 = (bf16[32,256]{1,0:T(8,128)(2,1)S(1)}, bf16[32,256]{1,0:T(8,128)(2,1)S(1)}, u32[]{:S(2)}, u32[]{:S(2)}) collective-permute-start(bf16[32,256]{1,0:T(8,128)(2,1)S(1)} %get-tuple-element.57), channel_id=1, source_target_pairs={{0,16},{8,24},{16,0},{24,8},{1,17},{9,25},{17,1},{25,9},{2,18},{10... | collective-permute-start | bytes 49160 | tf_op jit(solution)/shard_map/ppermute | solution.py:359
  9.2 3.7 %collective-permute-start.2 = (bf16[32,256]{1,0:T(8,128)(2,1)S(1)}, bf16[32,256]{1,0:T(8,128)(2,1)S(1)}, u32[]{:S(2)}, u32[]{:S(2)}) collective-permute-start(bf16[32,256]{1,0:T(8,128)(2,1)S(1)} %get-tuple-element.58), channel_id=1, source_target_pairs={{0,8},{8,0},{16,24},{24,16},{1,9},{9,1},{17,25},{25,17},{2,10},{10... | collective-permute-start | bytes 49160 | tf_op jit(solution)/shard_map/ppermute | solution.py:359
  14.4 1.8 %collective-permute-start.4 = (bf16[784,256]{1,0:T(8,128)(2,1)S(1)}, bf16[784,256]{1,0:T(8,128)(2,1)S(1)}, u32[]{:S(2)}, u32[]{:S(2)}) collective-permute-start(bf16[784,256]{1,0:T(8,128)(2,1)S(1)} %get-tuple-element.67), channel_id=1, source_target_pairs={{0,1},{1,0},{2,3},{3,2},{4,5},{5,4},{6,7},{7,6},{8,9},{9,8},{10,11... | collective-permute-start | bytes 1204232 | tf_op jit(solution)/shard_map/ppermute | solution.py:359
  14.5 5.6 %collective-permute-start.7 = (bf16[128,256]{1,0:T(8,128)(2,1)S(1)}, bf16[128,256]{1,0:T(8,128)(2,1)S(1)}, u32[]{:S(2)}, u32[]{:S(2)}) collective-permute-start(bf16[128,256]{1,0:T(8,128)(2,1)S(1)} %get-tuple-element.70), channel_id=1, source_target_pairs={{0,1},{1,0},{2,4},{3,5},{4,2},{5,3},{6,7},{7,6},{8,9},{9,8},{10,12... | collective-permute-start | bytes 196616 | tf_op jit(solution)/shard_map/ppermute | solution.py:420
  15.0 4.3 %collective-permute-start.6 = (bf16[128,256]{1,0:T(8,128)(2,1)S(1)}, bf16[128,256]{1,0:T(8,128)(2,1)S(1)}, u32[]{:S(2)}, u32[]{:S(2)}) collective-permute-start(bf16[128,256]{1,0:T(8,128)(2,1)S(1)} %get-tuple-element.70), channel_id=1, source_target_pairs={{0,2},{1,3},{2,0},{3,1},{4,6},{5,7},{6,4},{7,5},{8,10},{9,11},{10,... | collective-permute-start | bytes 196616 | tf_op jit(solution)/shard_map/ppermute | solution.py:359
  16.4 14.0 %collective-permute-start.13 = (bf16[784,256]{1,0:T(8,128)(2,1)S(1)}, bf16[784,256]{1,0:T(8,128)(2,1)S(1)}, u32[]{:S(2)}, u32[]{:S(2)}) collective-permute-start(bf16[784,256]{1,0:T(8,128)(2,1)S(1)} %join_cores.2), channel_id=1, source_target_pairs={{0,6},{1,7},{2,3},{3,2},{4,5},{5,4},{6,0},{7,1},{8,14},{9,15},{10,... | collective-permute-start | bytes 1204232 | tf_op jit(solution)/shard_map/ppermute | solution.py:425
  21.1 1.8 %collective-permute-start.9 = (bf16[400,256]{1,0:T(8,128)(2,1)S(1)}, bf16[400,256]{1,0:T(8,128)(2,1)S(1)}, u32[]{:S(2)}, u32[]{:S(2)}) collective-permute-start(bf16[400,256]{1,0:T(8,128)(2,1)S(1)} %get-tuple-element.77), channel_id=1, source_target_pairs={{0,1},{1,0},{2,3},{3,2},{4,5},{5,4},{6,7},{7,6},{8,9},{9,8},{10,11... | collective-permute-start | bytes 614408 | tf_op jit(solution)/shard_map/ppermute | solution.py:359
  21.2 1.7 %collective-permute-start.8 = (bf16[384,256]{1,0:T(8,128)(2,1)S(1)}, bf16[384,256]{1,0:T(8,128)(2,1)S(1)}, u32[]{:S(2)}, u32[]{:S(2)}) collective-permute-start(bf16[384,256]{1,0:T(8,128)(2,1)S(1)} %get-tuple-element.76), channel_id=1, source_target_pairs={{0,1},{1,0},{2,3},{3,2},{4,5},{5,4},{6,7},{7,6},{8,9},{9,8},{10,11... | collective-permute-start | bytes 589832 | tf_op jit(solution)/shard_map/ppermute | solution.py:359
  23.0 15.2 %collective-permute-start.18 = (bf16[784,256]{1,0:T(8,128)(2,1)S(1)}, bf16[784,256]{1,0:T(8,128)(2,1)S(1)}, u32[]{:S(2)}, u32[]{:S(2)}) collective-permute-start(bf16[784,256]{1,0:T(8,128)(2,1)S(1)} %join_cores.3), channel_id=1, source_target_pairs={{0,4},{1,5},{2,0},{3,1},{4,6},{5,7},{6,2},{7,3},{8,12},{9,13},{10,... | collective-permute-start | bytes 1204232 | tf_op jit(solution)/shard_map/ppermute | solution.py:442
  25.4 7.0 %collective-permute-start.10 = (bf16[32,2048]{1,0:T(8,128)(2,1)S(1)}, bf16[32,2048]{1,0:T(8,128)(2,1)S(1)}, u32[]{:S(2)}, u32[]{:S(2)}) collective-permute-start(bf16[32,2048]{1,0:T(8,128)(2,1)S(1)} %get-tuple-element.81), channel_id=1, source_target_pairs={{0,8},{8,0},{16,24},{24,16},{1,9},{9,1},{17,25},{25,17},{2,10},{10... | collective-permute-start | bytes 393224 | tf_op jit(solution)/shard_map/ppermute | solution.py:359
  26.9 7.9 %collective-permute-start.11 = (bf16[32,2048]{1,0:T(8,128)(2,1)S(1)}, bf16[32,2048]{1,0:T(8,128)(2,1)S(1)}, u32[]{:S(2)}, u32[]{:S(2)}) collective-permute-start(bf16[32,2048]{1,0:T(8,128)(2,1)S(1)} %get-tuple-element.82), channel_id=1, source_target_pairs={{0,16},{8,24},{16,0},{24,8},{1,17},{9,25},{17,1},{25,9},{2,18},{10... | collective-permute-start | bytes 393224 | tf_op jit(solution)/shard_map/ppermute | solution.py:359
  28.5 6.3 %collective-permute-start.12 = (bf16[32,2048]{1,0:T(8,128)(2,1)S(1)}, bf16[32,2048]{1,0:T(8,128)(2,1)S(1)}, u32[]{:S(2)}, u32[]{:S(2)}) collective-permute-start(bf16[32,2048]{1,0:T(8,128)(2,1)S(1)} %get-tuple-element.83), channel_id=1, source_target_pairs={{0,24},{8,16},{16,8},{24,0},{1,25},{9,17},{17,9},{25,1},{2,26},{10... | collective-permute-start | bytes 393224 | tf_op jit(solution)/shard_map/ppermute | solution.py:359
  32.3 4.6 %collective-permute-start.17 = (bf16[240,256]{1,0:T(8,128)(2,1)S(1)}, bf16[240,256]{1,0:T(8,128)(2,1)S(1)}, u32[]{:S(2)}, u32[]{:S(2)}) collective-permute-start(bf16[240,256]{1,0:T(8,128)(2,1)S(1)} %get-tuple-element.93), channel_id=1, source_target_pairs={{0,1},{1,0},{2,3},{3,2},{4,5},{5,4},{6,7},{7,6},{8,9},{9,8},{10,11... | collective-permute-start | bytes 368648 | tf_op jit(solution)/shard_map/ppermute | solution.py:359
  32.4 4.5 %collective-permute-start.14 = (bf16[192,256]{1,0:T(8,128)(2,1)S(1)}, bf16[192,256]{1,0:T(8,128)(2,1)S(1)}, u32[]{:S(2)}, u32[]{:S(2)}) collective-permute-start(bf16[192,256]{1,0:T(8,128)(2,1)S(1)} %get-tuple-element.90), channel_id=1, source_target_pairs={{0,1},{1,0},{2,3},{3,2},{4,5},{5,4},{6,7},{7,6},{8,9},{9,8},{10,11... | collective-permute-start | bytes 294920 | tf_op jit(solution)/shard_map/ppermute | solution.py:359
  34.8 0.7 %copy-start.2 = (s32[64]{0:T(128)S(1)}, s32[64]{0:T(128)}, u32[]{:S(2)}) copy-start(s32[64]{0:T(128)} %assign_ref.1) | copy-start | bytes 772
  34.8 2.2 %collective-permute-start.15 = (bf16[192,256]{1,0:T(8,128)(2,1)S(1)}, bf16[192,256]{1,0:T(8,128)(2,1)S(1)}, u32[]{:S(2)}, u32[]{:S(2)}) collective-permute-start(bf16[192,256]{1,0:T(8,128)(2,1)S(1)} %get-tuple-element.91), channel_id=1, source_target_pairs={{0,1},{1,0},{2,3},{3,2},{4,5},{5,4},{6,7},{7,6},{8,9},{9,8},{10,11... | collective-permute-start | bytes 294920 | tf_op jit(solution)/shard_map/ppermute | solution.py:359
  34.8 2.2 %collective-permute-start.16 = (bf16[192,256]{1,0:T(8,128)(2,1)S(1)}, bf16[192,256]{1,0:T(8,128)(2,1)S(1)}, u32[]{:S(2)}, u32[]{:S(2)}) collective-permute-start(bf16[192,256]{1,0:T(8,128)(2,1)S(1)} %get-tuple-element.92), channel_id=1, source_target_pairs={{0,1},{1,0},{2,3},{3,2},{4,5},{5,4},{6,7},{7,6},{8,9},{9,8},{10,11... | collective-permute-start | bytes 294920 | tf_op jit(solution)/shard_map/ppermute | solution.py:359

commit v9 on v6

--- a/solution.py
+++ b/solution.py
@@ -126,12 +126,16 @@
     copies[3].wait()
 
 
+def piece_order(n_tower):
+    return [n_tower - 1, *range(1, n_tower - 1), 0]
+
+
 def backward_kernel(n_tower, wu_ref, wo_ref, x_ref, low_ref, *refs):
     pieces = refs[:n_tower]
     g_ref, gh_ref, ht_ref, gg_ref, bg_ref, gc_ref = refs[n_tower:]
     me = lax.axis_index("tower")
     rows = pieces[0].shape[0]
-    for k, piece in zip(range(len(pieces) - 1, -1, -1), pieces):
+    for k, piece in zip(piece_order(len(pieces)), pieces):
         g_ref[pl.ds(pl.multiple_of((me ^ k) * rows, rows), rows), :] = piece[...]
     gh_ref[...] = backward_rows(
         x_ref, g_ref[...], low_ref, wu_ref, wo_ref, gg_ref, bg_ref, ht_ref, gc_ref
@@ -412,7 +416,7 @@
         [sds((n, out), BF16), low, tall, wide, row, wide],
         [],
         [VMEM] * (4 + n_tower),
-        [wu, wo, x_own, low_own, *pieces[::-1]],
+        [wu, wo, x_own, low_own, *[pieces[k] for k in piece_order(n_tower)]],
         "backward_own",
         cost=1,
     )

time: 39.3 us -> 39.3 us (level)
  no operation moved by 1% of the time
where the time goes in v9:
time: 39.3 us; the launch traced here: 39.2 us
  starting transfers between devices  18.2 us (46%)
  Pallas kernels  10.8 us (27%)
  waiting for transfers between devices  8.44 us (21%)
  local copies, waits for them, and re-layouts  0.99 us (3%)
  between operations  0.81 us (2%)
    ppermute x15, starting transfers between devices, across(): return lax.ppermute(value, axis, xor_pairs(lax.axis_size(axis), k))  13.9 us
    pallas_call x14, Pallas kernels, call(): pl.pallas_call(kernel, out_shape=outs, in_specs=[pl.BlockSpec(memory_spac...  10.8 us
    ppermute x15, waiting for transfers between devices, across(): return lax.ppermute(value, axis, xor_pairs(lax.axis_size(axis), k))  5.9 us
    ppermute x1, starting transfers between devices, paired_body(): from_second = lax.ppermute(second_sum, 'shard', second)  1.84 us
    ppermute x1, waiting for transfers between devices, paired_body(): from_first = lax.ppermute(first, 'shard', outer)  1.5 us
    ppermute x1, starting transfers between devices, paired_body(): from_first = lax.ppermute(first, 'shard', outer)  1.41 us
    ppermute x1, waiting for transfers between devices, paired_body(): from_second = lax.ppermute(second_sum, 'shard', second)  1.03 us
    unnamed x8, local copies, waits for them, and re-layouts  0.99 us
  transfers between devices with their start and end apart: 19, of which 8 were waited for; matrix products, arithmetic and copies ran while one was open for 0% of the time, Pallas kernels for 25%

profile of v9, /device:TPU:0, one launch (start us, length us, event | category | flops | bytes accessed | tf_op | source)
XLA Modules:
  0.0 39.2 jit_solution(9893511343291409298)
XLA Ops:
  0.6 0.5 %collective-permute-start.3 = (bf16[128,2048]{1,0:T(8,128)(2,1)}, bf16[128,2048]{1,0:T(8,128)(2,1)S(1)}, u32[]{:S(2)}, u32[]{:S(2)}) collective-permute-start(bf16[128,2048]{1,0:T(8,128)(2,1)} %bitcast.5), channel_id=1, source_target_pairs={{0,1},{1,0},{2,4},{3,5},{4,2},{5,3},{6,7},{7,6},{8,9},{9,8},{10,12... | collective-permute-start | bytes 1572872 | tf_op jit(solution)/shard_map/ppermute | solution.py:391
  1.2 4.1 %collective-permute-start.5 = (bf16[128,2048]{1,0:T(8,128)(2,1)}, bf16[128,2048]{1,0:T(8,128)(2,1)S(1)}, u32[]{:S(2)}, u32[]{:S(2)}) collective-permute-start(bf16[128,2048]{1,0:T(8,128)(2,1)} %bitcast.6), channel_id=1, source_target_pairs={{0,2},{1,3},{2,0},{3,1},{4,6},{5,7},{6,4},{7,5},{8,10},{9,11},{10,... | collective-permute-start | bytes 1572872 | tf_op jit(solution)/shard_map/ppermute | solution.py:363
  5.3 0.8 %copy-done.3 = bf16[32,1024]{1,0:T(8,128)(2,1)S(1)} copy-done((bf16[32,1024]{1,0:T(8,128)(2,1)S(1)}, bf16[32,1024]{1,0:T(8,128)(2,1)}, u32[]{:S(2)}) %copy-start.3) | copy-done | bytes 65560
  6.2 2.5 %collective-permute-start = (bf16[32,256]{1,0:T(8,128)(2,1)S(1)}, bf16[32,256]{1,0:T(8,128)(2,1)S(1)}, u32[]{:S(2)}, u32[]{:S(2)}) collective-permute-start(bf16[32,256]{1,0:T(8,128)(2,1)S(1)} %get-tuple-element.56), channel_id=1, source_target_pairs={{0,24},{8,16},{16,8},{24,0},{1,25},{9,17},{17,9},{25,1},{2,26},{10... | collective-permute-start | bytes 49160 | tf_op jit(solution)/shard_map/ppermute | solution.py:363
  8.7 0.5 %collective-permute-start.1 = (bf16[32,256]{1,0:T(8,128)(2,1)S(1)}, bf16[32,256]{1,0:T(8,128)(2,1)S(1)}, u32[]{:S(2)}, u32[]{:S(2)}) collective-permute-start(bf16[32,256]{1,0:T(8,128)(2,1)S(1)} %get-tuple-element.57), channel_id=1, source_target_pairs={{0,8},{8,0},{16,24},{24,16},{1,9},{9,1},{17,25},{25,17},{2,10},{10... | collective-permute-start | bytes 49160 | tf_op jit(solution)/shard_map/ppermute | solution.py:363
  9.3 0.5 %collective-permute-start.2 = (bf16[32,256]{1,0:T(8,128)(2,1)S(1)}, bf16[32,256]{1,0:T(8,128)(2,1)S(1)}, u32[]{:S(2)}, u32[]{:S(2)}) collective-permute-start(bf16[32,256]{1,0:T(8,128)(2,1)S(1)} %get-tuple-element.58), channel_id=1, source_target_pairs={{0,16},{8,24},{16,0},{24,8},{1,17},{9,25},{17,1},{25,9},{2,18},{10... | collective-permute-start | bytes 49160 | tf_op jit(solution)/shard_map/ppermute | solution.py:363
  9.8 2.1 %forward_own.1 = (bf16[2048,256]{1,0:T(8,128)(2,1)S(1)}, bf16[256,2048]{1,0:T(8,128)(2,1)S(1)}, bf16[2048,256]{1,0:T(8,128)(2,1)S(1)}, bf16[128,2048]{1,0:T(8,12...) custom-call(bf16[2048,256]{1,0:T(8,128)(2,1)} %bitcast.8, ...), custom_call_target="tpu_custom_call" | custom-call | flops 1 | bytes 1 | tf_op jit(solution)/shard_map/forward_own/pallas_call | solution.py:39
  11.9 0.5 %collective-permute-done.1.refs_1_ = bf16[32,256]{1,0:T(8,128)(2,1)S(1)} collective-permute-done((bf16[32,256]{1,0:T(8,128)(2,1)S(1)}, bf16[32,256]{1,0:T(8,128)(2,1)S(1)}, u32[]{:S(2)}, u32[]{:S(2)}) %collective-permute-start.1) | collective-permute-done | bytes 16416 | tf_op jit(solution)/shard_map/ppermute | solution.py:363
  12.5 0.5 %collective-permute-done.2.refs_2_ = bf16[32,256]{1,0:T(8,128)(2,1)S(1)} collective-permute-done((bf16[32,256]{1,0:T(8,128)(2,1)S(1)}, bf16[32,256]{1,0:T(8,128)(2,1)S(1)}, u32[]{:S(2)}, u32[]{:S(2)}) %collective-permute-start.2) | collective-permute-done | bytes 16416 | tf_op jit(solution)/shard_map/ppermute | solution.py:363
  13.0 1.1 %backward_own.1 = (bf16[128,256]{1,0:T(8,128)(2,1)S(1)}, bf16[128,256]{1,0:T(8,128)(2,1)S(1)}, bf16[768,128]{1,0:T(8,128)(2,1)S(1)}, bf16[128,2048]{1,0:T(8,128)...) custom-call(bf16[256,2048]{1,0:T(8,128)(2,1)S(1)} %get-tuple-element.52.wu_ref, ...), custom_call_target="tpu_custom_call" | custom-call | flops 1 | bytes 1 | tf_op jit(solution)/shard_map/backward_own/pallas_call | solution.py:39
  14.1 0.4 first_sums.1
  14.6 0.5 %collective-permute-start.7 = (bf16[128,256]{1,0:T(8,128)(2,1)S(1)}, bf16[128,256]{1,0:T(8,128)(2,1)S(1)}, u32[]{:S(2)}, u32[]{:S(2)}) collective-permute-start(bf16[128,256]{1,0:T(8,128)(2,1)S(1)} %get-tuple-element.70), channel_id=1, source_target_pairs={{0,1},{1,0},{2,4},{3,5},{4,2},{5,3},{6,7},{7,6},{8,9},{9,8},{10,12... | collective-permute-start | bytes 196616 | tf_op jit(solution)/shard_map/ppermute | solution.py:424
  15.1 0.9 %collective-permute-start.6 = (bf16[128,256]{1,0:T(8,128)(2,1)S(1)}, bf16[128,256]{1,0:T(8,128)(2,1)S(1)}, u32[]{:S(2)}, u32[]{:S(2)}) collective-permute-start(bf16[128,256]{1,0:T(8,128)(2,1)S(1)} %get-tuple-element.70), channel_id=1, source_target_pairs={{0,2},{1,3},{2,0},{3,1},{4,6},{5,7},{6,4},{7,5},{8,10},{9,11},{10,... | collective-permute-start | bytes 196616 | tf_op jit(solution)/shard_map/ppermute | solution.py:363
  16.4 1.4 %collective-permute-start.13 = (bf16[784,256]{1,0:T(8,128)(2,1)S(1)}, bf16[784,256]{1,0:T(8,128)(2,1)S(1)}, u32[]{:S(2)}, u32[]{:S(2)}) collective-permute-start(bf16[784,256]{1,0:T(8,128)(2,1)S(1)} %join_cores.2), channel_id=1, source_target_pairs={{0,6},{1,7},{2,3},{3,2},{4,5},{5,4},{6,0},{7,1},{8,14},{9,15},{10,... | collective-permute-start | bytes 1204232 | tf_op jit(solution)/shard_map/ppermute | solution.py:429
  17.8 1.5 %collective-permute-done.6.g_ref = bf16[128,256]{1,0:T(8,128)(2,1)S(1)} collective-permute-done((bf16[128,256]{1,0:T(8,128)(2,1)S(1)}, bf16[128,256]{1,0:T(8,128)(2,1)S(1)}, u32[]{:S(2)}, u32[]{:S(2)}) %collective-permute-start.6) | collective-permute-done | bytes 65568 | tf_op jit(solution)/shard_map/ppermute | solution.py:363
  19.3 0.8 %forward_other.1 = (bf16[128,256]{1,0:T(8,128)(2,1)S(1)}, bf16[128,2048]{1,0:T(8,128)(2,1)S(1)}) custom-call(bf16[128,2048]{1,0:T(8,128)(2,1)S(1)} %collective-permute-done.5.x_ref, bf16[2048,256]{1,0:T(8,128)(2,1)S(1)} %get-tuple-element.51.wd_ref, bf16[256,2048]{1,0:T(8,128)(2,1)S(1)} %get-tuple-element.52.wu_ref, f32[1,2048]{1,0:T(1,128)S(1)} %copy-done.1), custom_call_target="tpu_custom_call" | custom-call | flops 1000000000 | bytes 1 | tf_op jit(solution)/shard_map/forward_other/pallas_call | solution.py:39
  20.1 1.0 %second_sums.1 = (bf16[128,2048]{1,0:T(8,128)(2,1)S(1)}, bf16[768,128]{1,0:T(8,128)(2,1)S(1)}, f32[1,2048]{1,0:T(1,128)S(1)}, f32[784,256]{1,0:T(8,128)S(1)}, bf...) custom-call(bf16[256,2048]{1,0:T(8,128)(2,1)S(1)} %get-tuple-element.52.wu_ref, ...), custom_call_target="tpu_custom_call" | custom-call | flops 1000000000 | bytes 1 | tf_op jit(solution)/shard_map/second_sums/pallas_call | solution.py:39
  21.2 0.5 %collective-permute-start.8 = (bf16[384,256]{1,0:T(8,128)(2,1)S(1)}, bf16[384,256]{1,0:T(8,128)(2,1)S(1)}, u32[]{:S(2)}, u32[]{:S(2)}) collective-permute-start(bf16[384,256]{1,0:T(8,128)(2,1)S(1)} %get-tuple-element.76), channel_id=1, source_target_pairs={{0,1},{1,0},{2,3},{3,2},{4,5},{5,4},{6,7},{7,6},{8,9},{9,8},{10,11... | collective-permute-start | bytes 589832 | tf_op jit(solution)/shard_map/ppermute | solution.py:363
  21.7 1.2 %collective-permute-done.8.refs_0_ = bf16[384,256]{1,0:T(8,128)(2,1)S(1)} collective-permute-done((bf16[384,256]{1,0:T(8,128)(2,1)S(1)}, bf16[384,256]{1,0:T(8,128)(2,1)S(1)}, u32[]{:S(2)}, u32[]{:S(2)}) %collective-permute-start.8) | collective-permute-done | bytes 196640 | tf_op jit(solution)/shard_map/ppermute | solution.py:363
  23.0 1.8 %collective-permute-start.18 = (bf16[784,256]{1,0:T(8,128)(2,1)S(1)}, bf16[784,256]{1,0:T(8,128)(2,1)S(1)}, u32[]{:S(2)}, u32[]{:S(2)}) collective-permute-start(bf16[784,256]{1,0:T(8,128)(2,1)S(1)} %join_cores.3), channel_id=1, source_target_pairs={{0,4},{1,5},{2,0},{3,1},{4,6},{5,7},{6,2},{7,3},{8,12},{9,13},{10,... | collective-permute-start | bytes 1204232 | tf_op jit(solution)/shard_map/ppermute | solution.py:446
  24.9 0.5 %grad_inputs.1 = (bf16[32,2048]{1,0:T(8,128)(2,1)S(1)}, bf16[32,2048]{1,0:T(8,128)(2,1)S(1)}, bf16[32,2048]{1,0:T(8,128)(2,1)S(1)}, bf16[32,2048]{1,0:T(8,128)(2,1)S(1)}) custom-call(bf16[2048,256]{1,0:T(8,128)(2,1)S(1)} %get-tuple-element.51.wd_ref, bf16[128,256]{1,0:T(8,128)(2,1)S(1)} %get-tuple-element.60.gh_ref, ...), custom_call_target="tpu_custom_call" | custom-call | flops 1 | bytes 1 | tf_op jit(solution)/shard_map/grad_inputs/pallas_call | solution.py:39
  25.4 1.5 %collective-permute-start.10 = (bf16[32,2048]{1,0:T(8,128)(2,1)S(1)}, bf16[32,2048]{1,0:T(8,128)(2,1)S(1)}, u32[]{:S(2)}, u32[]{:S(2)}) collective-permute-start(bf16[32,2048]{1,0:T(8,128)(2,1)S(1)} %get-tuple-element.81), channel_id=1, source_target_pairs={{0,8},{8,0},{16,24},{24,16},{1,9},{9,1},{17,25},{25,17},{2,10},{10... | collective-permute-start | bytes 393224 | tf_op jit(solution)/shard_map/ppermute | solution.py:363
  26.9 1.5 %collective-permute-start.11 = (bf16[32,2048]{1,0:T(8,128)(2,1)S(1)}, bf16[32,2048]{1,0:T(8,128)(2,1)S(1)}, u32[]{:S(2)}, u32[]{:S(2)}) collective-permute-start(bf16[32,2048]{1,0:T(8,128)(2,1)S(1)} %get-tuple-element.82), channel_id=1, source_target_pairs={{0,16},{8,24},{16,0},{24,8},{1,17},{9,25},{17,1},{25,9},{2,18},{10... | collective-permute-start | bytes 393224 | tf_op jit(solution)/shard_map/ppermute | solution.py:363
  28.5 0.5 %collective-permute-start.12 = (bf16[32,2048]{1,0:T(8,128)(2,1)S(1)}, bf16[32,2048]{1,0:T(8,128)(2,1)S(1)}, u32[]{:S(2)}, u32[]{:S(2)}) collective-permute-start(bf16[32,2048]{1,0:T(8,128)(2,1)S(1)} %get-tuple-element.83), channel_id=1, source_target_pairs={{0,24},{8,16},{16,8},{24,0},{1,25},{9,17},{17,9},{25,1},{2,26},{10... | collective-permute-start | bytes 393224 | tf_op jit(solution)/shard_map/ppermute | solution.py:363
  28.9 1.5 %collective-permute-done.13.refs_10_.first_ref = bf16[784,256]{1,0:T(8,128)(2,1)S(1)} collective-permute-done((bf16[784,256]{1,0:T(8,128)(2,1)S(1)}, bf16[784,256]{1,0:T(8,128)(2,1)S(1)}, u32[]{:S(2)}, u32[]{:S(2)}) %collective-permute-start.13) | collective-permute-done | bytes 401440 | tf_op jit(solution)/shard_map/ppermute | solution.py:429
  30.4 1.9 %near_sums.1 = (f32[816,256]{1,0:T(8,128)S(1)}, bf16[192,256]{1,0:T(8,128)(2,1)S(1)}, bf16[192,256]{1,0:T(8,128)(2,1)S(1)}, bf16[192,256]{1,0:T(8,128)(2,1)S(1)}, bf16[240,256]{1,0:T(8,128)(2,1)S(1)}) custom-call(bf16[256,2048]{1,0:T(8,128)(2,1)S(1)} %get-tuple-element.52.wu_ref, bf16[2048,256]{1,0:T(8,128)(2,1)S(1)} %get-tuple-element.53.wo_ref, ...), custom_call_target="tpu_custom_call" | custom-call | flops 1000000000 | bytes 1 | tf_op jit(solution)/shard_map/near_sums/pallas_call | solution.py:39
  32.5 0.5 %collective-permute-start.14 = (bf16[192,256]{1,0:T(8,128)(2,1)S(1)}, bf16[192,256]{1,0:T(8,128)(2,1)S(1)}, u32[]{:S(2)}, u32[]{:S(2)}) collective-permute-start(bf16[192,256]{1,0:T(8,128)(2,1)S(1)} %get-tuple-element.90), channel_id=1, source_target_pairs={{0,1},{1,0},{2,3},{3,2},{4,5},{5,4},{6,7},{7,6},{8,9},{9,8},{10,11... | collective-permute-start | bytes 294920 | tf_op jit(solution)/shard_map/ppermute | solution.py:363
  33.0 1.8 %collective-permute-done.11.refs_2_ = bf16[32,2048]{1,0:T(8,128)(2,1)S(1)} collective-permute-done((bf16[32,2048]{1,0:T(8,128)(2,1)S(1)}, bf16[32,2048]{1,0:T(8,128)(2,1)S(1)}, u32[]{:S(2)}, u32[]{:S(2)}) %collective-permute-start.11) | collective-permute-done | bytes 131104 | tf_op jit(solution)/shard_map/ppermute | solution.py:363
  34.8 0.5 %collective-permute-start.16 = (bf16[192,256]{1,0:T(8,128)(2,1)S(1)}, bf16[192,256]{1,0:T(8,128)(2,1)S(1)}, u32[]{:S(2)}, u32[]{:S(2)}) collective-permute-start(bf16[192,256]{1,0:T(8,128)(2,1)S(1)} %get-tuple-element.92), channel_id=1, source_target_pairs={{0,1},{1,0},{2,3},{3,2},{4,5},{5,4},{6,7},{7,6},{8,9},{9,8},{10,11... | collective-permute-start | bytes 294920 | tf_op jit(solution)/shard_map/ppermute | solution.py:363
  35.5 1.5 %place_features.1 = bf16[32,8192]{1,0:T(8,128)(2,1)} custom-call(s32[64]{0:T(128)S(1)} %copy-done.2, bf16[32,2048]{1,0:T(8,128)(2,1)S(1)} %get-tuple-element.80.refs_0_, bf16[32,2048]{1,0:T(8,128)(2,1)S(1)} %collective-permute-done.10.refs_1_, bf16[32,2048]{1,0:T(8,128)(2,1)S(1)} %collective-permute-done.11.refs_2_, ...), custom_call_target="tpu_custom_call" | custom-call | flops 1 | bytes 1 | tf_op jit(solution)/shard_map/place_features/pallas_call | solution.py:39
  37.2 1.0 %collective-permute-done.18.second_ref = bf16[784,256]{1,0:T(8,128)(2,1)S(1)} collective-permute-done((bf16[784,256]{1,0:T(8,128)(2,1)S(1)}, bf16[784,256]{1,0:T(8,128)(2,1)S(1)}, u32[]{:S(2)}, u32[]{:S(2)}) %collective-permute-start.18) | collective-permute-done | bytes 401440 | tf_op jit(solution)/shard_map/ppermute | solution.py:446
  38.2 1.0 %add_up.1 = (f32[96,2048]{1,0:T(8,128)}, f32[1,2048]{1,0:T(1,128)}) custom-call(f32[96,2048]{1,0:T(8,128)S(1)} %get-tuple-element.94.sum_ref, f32[1,2048]{1,0:T(1,128)S(1)} %get-tuple-element.95.near_bias_ref, f32[1,2048]{1,0:T(1,128)S(1)} %get-tuple-element.96.far_bias_ref, bf16[784,256]{1,0:T(8,128)(2,1)S(1)} %collective-permute-done.18.second_ref), custom_call_target="tpu_custom_call" | custom-call | flops 10000000000 | bytes 1 | tf_op jit(solution)/shard_map/add_up/pallas_call | solution.py:39
  (28 shorter events, 1.1 us)
Async XLA Ops:
  0.6 9.1 %copy-start = (bf16[1,128,2048]{2,1,0:T(8,128)(2,1)S(1)}, bf16[1,128,2048]{2,1,0:T(8,128)(2,1)}, u32[]{:S(2)}) copy-start(bf16[1,128,2048]{2,1,0:T(8,128)(2,1)} %param.8) | copy-start | bytes 1572868
  0.6 17.2 %collective-permute-start.3 = (bf16[128,2048]{1,0:T(8,128)(2,1)}, bf16[128,2048]{1,0:T(8,128)(2,1)S(1)}, u32[]{:S(2)}, u32[]{:S(2)}) collective-permute-start(bf16[128,2048]{1,0:T(8,128)(2,1)} %bitcast.5), channel_id=1, source_target_pairs={{0,1},{1,0},{2,4},{3,5},{4,2},{5,3},{6,7},{7,6},{8,9},{9,8},{10,12... | collective-permute-start | bytes 1572872 | tf_op jit(solution)/shard_map/ppermute | solution.py:391
  1.2 18.2 %collective-permute-start.5 = (bf16[128,2048]{1,0:T(8,128)(2,1)}, bf16[128,2048]{1,0:T(8,128)(2,1)S(1)}, u32[]{:S(2)}, u32[]{:S(2)}) collective-permute-start(bf16[128,2048]{1,0:T(8,128)(2,1)} %bitcast.6), channel_id=1, source_target_pairs={{0,2},{1,3},{2,0},{3,1},{4,6},{5,7},{6,4},{7,5},{8,10},{9,11},{10,... | collective-permute-start | bytes 1572872 | tf_op jit(solution)/shard_map/ppermute | solution.py:363
  5.3 0.8 %copy-start.3 = (bf16[32,1024]{1,0:T(8,128)(2,1)S(1)}, bf16[32,1024]{1,0:T(8,128)(2,1)}, u32[]{:S(2)}) copy-start(bf16[32,1024]{1,0:T(8,128)(2,1)} %grad_ref.1) | copy-start | bytes 196612
  6.2 3.6 %copy-start.1 = (f32[1,2048]{1,0:T(1,128)S(1)}, f32[1,2048]{1,0:T(1,128)}, u32[]{:S(2)}) copy-start(f32[1,2048]{1,0:T(1,128)} %bias_ref.5) | copy-start | bytes 24580
  6.2 5.7 %collective-permute-start = (bf16[32,256]{1,0:T(8,128)(2,1)S(1)}, bf16[32,256]{1,0:T(8,128)(2,1)S(1)}, u32[]{:S(2)}, u32[]{:S(2)}) collective-permute-start(bf16[32,256]{1,0:T(8,128)(2,1)S(1)} %get-tuple-element.56), channel_id=1, source_target_pairs={{0,24},{8,16},{16,8},{24,0},{1,25},{9,17},{17,9},{25,1},{2,26},{10... | collective-permute-start | bytes 49160 | tf_op jit(solution)/shard_map/ppermute | solution.py:363
  8.7 3.7 %collective-permute-start.1 = (bf16[32,256]{1,0:T(8,128)(2,1)S(1)}, bf16[32,256]{1,0:T(8,128)(2,1)S(1)}, u32[]{:S(2)}, u32[]{:S(2)}) collective-permute-start(bf16[32,256]{1,0:T(8,128)(2,1)S(1)} %get-tuple-element.57), channel_id=1, source_target_pairs={{0,8},{8,0},{16,24},{24,16},{1,9},{9,1},{17,25},{25,17},{2,10},{10... | collective-permute-start | bytes 49160 | tf_op jit(solution)/shard_map/ppermute | solution.py:363
  9.3 3.7 %collective-permute-start.2 = (bf16[32,256]{1,0:T(8,128)(2,1)S(1)}, bf16[32,256]{1,0:T(8,128)(2,1)S(1)}, u32[]{:S(2)}, u32[]{:S(2)}) collective-permute-start(bf16[32,256]{1,0:T(8,128)(2,1)S(1)} %get-tuple-element.58), channel_id=1, source_target_pairs={{0,16},{8,24},{16,0},{24,8},{1,17},{9,25},{17,1},{25,9},{2,18},{10... | collective-permute-start | bytes 49160 | tf_op jit(solution)/shard_map/ppermute | solution.py:363
  14.5 1.8 %collective-permute-start.4 = (bf16[784,256]{1,0:T(8,128)(2,1)S(1)}, bf16[784,256]{1,0:T(8,128)(2,1)S(1)}, u32[]{:S(2)}, u32[]{:S(2)}) collective-permute-start(bf16[784,256]{1,0:T(8,128)(2,1)S(1)} %get-tuple-element.67), channel_id=1, source_target_pairs={{0,1},{1,0},{2,3},{3,2},{4,5},{5,4},{6,7},{7,6},{8,9},{9,8},{10,11... | collective-permute-start | bytes 1204232 | tf_op jit(solution)/shard_map/ppermute | solution.py:363
  14.6 5.6 %collective-permute-start.7 = (bf16[128,256]{1,0:T(8,128)(2,1)S(1)}, bf16[128,256]{1,0:T(8,128)(2,1)S(1)}, u32[]{:S(2)}, u32[]{:S(2)}) collective-permute-start(bf16[128,256]{1,0:T(8,128)(2,1)S(1)} %get-tuple-element.70), channel_id=1, source_target_pairs={{0,1},{1,0},{2,4},{3,5},{4,2},{5,3},{6,7},{7,6},{8,9},{9,8},{10,12... | collective-permute-start | bytes 196616 | tf_op jit(solution)/shard_map/ppermute | solution.py:424
  15.1 4.3 %collective-permute-start.6 = (bf16[128,256]{1,0:T(8,128)(2,1)S(1)}, bf16[128,256]{1,0:T(8,128)(2,1)S(1)}, u32[]{:S(2)}, u32[]{:S(2)}) collective-permute-start(bf16[128,256]{1,0:T(8,128)(2,1)S(1)} %get-tuple-element.70), channel_id=1, source_target_pairs={{0,2},{1,3},{2,0},{3,1},{4,6},{5,7},{6,4},{7,5},{8,10},{9,11},{10,... | collective-permute-start | bytes 196616 | tf_op jit(solution)/shard_map/ppermute | solution.py:363
  16.4 14.0 %collective-permute-start.13 = (bf16[784,256]{1,0:T(8,128)(2,1)S(1)}, bf16[784,256]{1,0:T(8,128)(2,1)S(1)}, u32[]{:S(2)}, u32[]{:S(2)}) collective-permute-start(bf16[784,256]{1,0:T(8,128)(2,1)S(1)} %join_cores.2), channel_id=1, source_target_pairs={{0,6},{1,7},{2,3},{3,2},{4,5},{5,4},{6,0},{7,1},{8,14},{9,15},{10,... | collective-permute-start | bytes 1204232 | tf_op jit(solution)/shard_map/ppermute | solution.py:429
  21.1 1.8 %collective-permute-start.9 = (bf16[400,256]{1,0:T(8,128)(2,1)S(1)}, bf16[400,256]{1,0:T(8,128)(2,1)S(1)}, u32[]{:S(2)}, u32[]{:S(2)}) collective-permute-start(bf16[400,256]{1,0:T(8,128)(2,1)S(1)} %get-tuple-element.77), channel_id=1, source_target_pairs={{0,1},{1,0},{2,3},{3,2},{4,5},{5,4},{6,7},{7,6},{8,9},{9,8},{10,11... | collective-permute-start | bytes 614408 | tf_op jit(solution)/shard_map/ppermute | solution.py:363
  21.2 1.7 %collective-permute-start.8 = (bf16[384,256]{1,0:T(8,128)(2,1)S(1)}, bf16[384,256]{1,0:T(8,128)(2,1)S(1)}, u32[]{:S(2)}, u32[]{:S(2)}) collective-permute-start(bf16[384,256]{1,0:T(8,128)(2,1)S(1)} %get-tuple-element.76), channel_id=1, source_target_pairs={{0,1},{1,0},{2,3},{3,2},{4,5},{5,4},{6,7},{7,6},{8,9},{9,8},{10,11... | collective-permute-start | bytes 589832 | tf_op jit(solution)/shard_map/ppermute | solution.py:363
  23.0 15.2 %collective-permute-start.18 = (bf16[784,256]{1,0:T(8,128)(2,1)S(1)}, bf16[784,256]{1,0:T(8,128)(2,1)S(1)}, u32[]{:S(2)}, u32[]{:S(2)}) collective-permute-start(bf16[784,256]{1,0:T(8,128)(2,1)S(1)} %join_cores.3), channel_id=1, source_target_pairs={{0,4},{1,5},{2,0},{3,1},{4,6},{5,7},{6,2},{7,3},{8,12},{9,13},{10,... | collective-permute-start | bytes 1204232 | tf_op jit(solution)/shard_map/ppermute | solution.py:446
  25.4 7.1 %collective-permute-start.10 = (bf16[32,2048]{1,0:T(8,128)(2,1)S(1)}, bf16[32,2048]{1,0:T(8,128)(2,1)S(1)}, u32[]{:S(2)}, u32[]{:S(2)}) collective-permute-start(bf16[32,2048]{1,0:T(8,128)(2,1)S(1)} %get-tuple-element.81), channel_id=1, source_target_pairs={{0,8},{8,0},{16,24},{24,16},{1,9},{9,1},{17,25},{25,17},{2,10},{10... | collective-permute-start | bytes 393224 | tf_op jit(solution)/shard_map/ppermute | solution.py:363
  26.9 7.9 %collective-permute-start.11 = (bf16[32,2048]{1,0:T(8,128)(2,1)S(1)}, bf16[32,2048]{1,0:T(8,128)(2,1)S(1)}, u32[]{:S(2)}, u32[]{:S(2)}) collective-permute-start(bf16[32,2048]{1,0:T(8,128)(2,1)S(1)} %get-tuple-element.82), channel_id=1, source_target_pairs={{0,16},{8,24},{16,0},{24,8},{1,17},{9,25},{17,1},{25,9},{2,18},{10... | collective-permute-start | bytes 393224 | tf_op jit(solution)/shard_map/ppermute | solution.py:363
  28.5 6.3 %collective-permute-start.12 = (bf16[32,2048]{1,0:T(8,128)(2,1)S(1)}, bf16[32,2048]{1,0:T(8,128)(2,1)S(1)}, u32[]{:S(2)}, u32[]{:S(2)}) collective-permute-start(bf16[32,2048]{1,0:T(8,128)(2,1)S(1)} %get-tuple-element.83), channel_id=1, source_target_pairs={{0,24},{8,16},{16,8},{24,0},{1,25},{9,17},{17,9},{25,1},{2,26},{10... | collective-permute-start | bytes 393224 | tf_op jit(solution)/shard_map/ppermute | solution.py:363
  32.4 4.6 %collective-permute-start.17 = (bf16[240,256]{1,0:T(8,128)(2,1)S(1)}, bf16[240,256]{1,0:T(8,128)(2,1)S(1)}, u32[]{:S(2)}, u32[]{:S(2)}) collective-permute-start(bf16[240,256]{1,0:T(8,128)(2,1)S(1)} %get-tuple-element.93), channel_id=1, source_target_pairs={{0,1},{1,0},{2,3},{3,2},{4,5},{5,4},{6,7},{7,6},{8,9},{9,8},{10,11... | collective-permute-start | bytes 368648 | tf_op jit(solution)/shard_map/ppermute | solution.py:363
  32.5 4.5 %collective-permute-start.14 = (bf16[192,256]{1,0:T(8,128)(2,1)S(1)}, bf16[192,256]{1,0:T(8,128)(2,1)S(1)}, u32[]{:S(2)}, u32[]{:S(2)}) collective-permute-start(bf16[192,256]{1,0:T(8,128)(2,1)S(1)} %get-tuple-element.90), channel_id=1, source_target_pairs={{0,1},{1,0},{2,3},{3,2},{4,5},{5,4},{6,7},{7,6},{8,9},{9,8},{10,11... | collective-permute-start | bytes 294920 | tf_op jit(solution)/shard_map/ppermute | solution.py:363
  34.8 0.7 %copy-start.2 = (s32[64]{0:T(128)S(1)}, s32[64]{0:T(128)}, u32[]{:S(2)}) copy-start(s32[64]{0:T(128)} %assign_ref.1) | copy-start | bytes 772
  34.8 2.2 %collective-permute-start.15 = (bf16[192,256]{1,0:T(8,128)(2,1)S(1)}, bf16[192,256]{1,0:T(8,128)(2,1)S(1)}, u32[]{:S(2)}, u32[]{:S(2)}) collective-permute-start(bf16[192,256]{1,0:T(8,128)(2,1)S(1)} %get-tuple-element.91), channel_id=1, source_target_pairs={{0,1},{1,0},{2,3},{3,2},{4,5},{5,4},{6,7},{7,6},{8,9},{9,8},{10,11... | collective-permute-start | bytes 294920 | tf_op jit(solution)/shard_map/ppermute | solution.py:363
  34.8 2.2 %collective-permute-start.16 = (bf16[192,256]{1,0:T(8,128)(2,1)S(1)}, bf16[192,256]{1,0:T(8,128)(2,1)S(1)}, u32[]{:S(2)}, u32[]{:S(2)}) collective-permute-start(bf16[192,256]{1,0:T(8,128)(2,1)S(1)} %get-tuple-element.92), channel_id=1, source_target_pairs={{0,1},{1,0},{2,3},{3,2},{4,5},{5,4},{6,7},{7,6},{8,9},{9,8},{10,11... | collective-permute-start | bytes 294920 | tf_op jit(solution)/shard_map/ppermute | solution.py:363
